TPU v7x, 32 devices: a whole 2x2x4 slice. The times are simulated.
32 devices in a mesh: elec: 4 (over x, core), space: 8 (over z, y).
Axes of the slice: x: 2, y: 2, z: 4, core: 2. Of those that a mesh axis runs over, the one named last changes fastest.
Arguments:
- potentials: bfloat16 [2048, 16, 8, 128], P('elec', 'space'), may hold values from -6 to 6
- quadrupoles: int32 [4, 32768], replicated, may hold values from 0 to 2047
- residuals: float32 [32768], replicated, may hold values from -0.03125 to 0.03125
- cell_weight: float32 [16, 8, 128], P('space'), may hold values from 0.5 to 2
Outputs:
- model_gradient: float32 [16, 8, 128], P('space')
All inputs are finite; a program needn't handle non-finite values.
Results may differ from a plain program's by a relative error of at most 0.0054.
Values may be sent and summed in bfloat16 or wider, within the bound.
No kernel may reach another device: no remote copies, remote signals or barrier semaphores. Data moves between devices by JAX's collectives and lax.ppermute only.
A program may use at most 192 MiB of HBM per device.

v0:
```python
import jax
import jax.numpy as jnp
from jax import lax
from jax.sharding import PartitionSpec as P


def extended(block, sides, width):
    for axis, dim in sides:
        count = lax.axis_size(axis)
        forward = [(i, i + 1) for i in range(count - 1)]
        backward = [(target, source) for source, target in forward]
        low = lax.ppermute(
            lax.slice_in_dim(block, block.shape[dim] - width, None, axis=dim), axis, forward
        )
        high = lax.ppermute(lax.slice_in_dim(block, 0, width, axis=dim), axis, backward)
        block = jnp.concatenate([low, block, high], axis=dim)
    return block


def slopes_of(padded):
    field = padded.astype(jnp.float32)
    grad_x = 0.5 * (field[:, 2:] - field[:, :-2])
    inner = field[:, 1:-1]
    pad_z = jnp.pad(inner, ((0, 0), (0, 0), (1, 1), (0, 0)))
    grad_z = 0.5 * (pad_z[:, :, 2:] - pad_z[:, :, :-2])
    pad_y = jnp.pad(inner, ((0, 0), (0, 0), (0, 0), (1, 1)))
    grad_y = 0.5 * (pad_y[:, :, :, 2:] - pad_y[:, :, :, :-2])
    return jnp.stack([grad_x, grad_z, grad_y], axis=0).astype(jnp.bfloat16)


def coupling_rows(quadrupoles, residuals, first, count, width):
    source_a = quadrupoles[0]
    source_b = quadrupoles[1]
    probe_m = quadrupoles[2]
    probe_n = quadrupoles[3]
    rows = jnp.concatenate([source_a, source_a, source_b, source_b]) - first
    cols = jnp.concatenate([probe_m, probe_n, probe_m, probe_n])
    values = jnp.concatenate([residuals, -residuals, -residuals, residuals])
    valid = (rows >= 0) & (rows < count)
    flat = jnp.where(valid, rows * width + cols, count * width)
    summed = jax.ops.segment_sum(values, flat, num_segments=count * width)
    return summed.reshape(count, width).astype(jnp.bfloat16)


def local(potentials, quadrupoles, residuals, cell_weight):
    local_fields, planes_dev, thickness, breadth = potentials.shape
    groups = lax.axis_size("elec")
    width = local_fields * groups
    padded = extended(potentials, (("space", 1),), 1)
    own_slopes = slopes_of(padded)
    coupling = coupling_rows(quadrupoles, residuals, 0, width, width)
    sectioned = own_slopes.reshape(3, local_fields, planes_dev * thickness, breadth)
    moved = lax.all_to_all(sectioned, "elec", split_axis=2, concat_axis=1, tiled=True)
    image = jnp.einsum("ef,kfpy->kepy", coupling, moved, preferred_element_type=jnp.float32)
    share = jnp.sum(moved.astype(jnp.float32) * image, axis=(0, 1))
    summed = lax.all_gather(share, "elec", axis=0, tiled=True).reshape(
        planes_dev, thickness, breadth
    )
    return summed * cell_weight


def solution(mesh):
    placed = (P("elec", "space", None, None), P(), P(), P("space", None, None))
    return jax.shard_map(
        local, mesh=mesh, in_specs=placed, out_specs=P("space", None, None), check_vma=False
    )
```

profile of v0, /device:TPU:0, one launch (start us, length us, event | category | flops | bytes accessed | tf_op | source)
XLA Modules:
  0.0 830.6 jit_solution(2620555808783657711)
XLA Ops:
  0.0 0.0 copy-start
  0.0 0.0 copy-start.1
  0.0 1.8 fusion.15
  1.8 4.9 collective-permute-start
  6.8 1.3 collective-permute-start.1
  8.1 0.0 copy-done.1
  8.1 0.4 slice_bitcast_fusion.3
  8.5 43.1 %collective-permute-done = bf16[512,1,8,128]{3,2,1,0:T(8,128)(2,1)S(1)} collective-permute-done((bf16[512,1,8,128]{3,2,1,0:T(8,128)(2,1)S(1)}, bf16[512,1,8,128]{3,2,1,0:T(8,128)(2,1)S(1)}, u32[]{:S(2)}, u32[]{:S(2)}) %collective-permute-start) | collective-permute-done | bytes 1048608 | tf_op jit(solution)/shard_map/ppermute | solution.py:12
  51.6 0.0 collective-permute-done.1
  51.6 0.0 copy-done
  51.6 1.1 maximum_convert_fusion
  52.7 0.7 fusion.14
  53.4 3.4 fusion.9
  56.8 0.5 copy.10
  57.4 0.5 copy.11
  57.9 0.5 copy.9
  58.5 3.3 pad_maximum_fusion
  61.8 0.0 copy-start.2
  61.8 5.4 all-to-all-start
  67.3 5.3 and_select_fusion
  72.5 0.0 copy-done.2
  72.6 689.1 %scatter_custom_fusion = f32[4194304]{0:T(1024)} fusion(s32[131072]{0:T(1024)S(1)} %bitcast.34, f32[131072]{0:T(1024)S(1)} %pad_maximum_fusion.1, f32[]{:T(128)} %constant.6.clone.1), kind=kCustom, calls=%fused_computation.9 | custom fusion | flops 131072 | bytes 16777220 | tf_op jit(solution)/shard_map/scatter-add | solution.py:41
  761.7 8.9 %convert_element_type.20 = bf16[4194304]{0:T(1024)(128)(2,1)} convert(f32[4194304]{0:T(1024)} %scatter_custom_fusion) | non-fusion elementwise | flops 4194304 | bytes 25165824 | tf_op jit(solution)/shard_map/convert_element_type | solution.py:42
  770.6 13.3 %reshape.253 = bf16[2048,2048,1,1]{1,0,2,3:T(8,128)(2,1)} reshape(bf16[4194304]{0:T(1024)(128)(2,1)} %convert_element_type.20) | data formatting | bytes 16777216 | tf_op jit(solution)/shard_map/convert_element_type | solution.py:42
  784.0 0.0 all-to-all-done
  784.0 11.2 %copy.13 = bf16[3,4,512,4,128]{2,1,4,3,0:T(4,128)(2,1)} copy(bf16[3,4,512,4,128]{4,2,0,3,1:T(8,128)(2,1)} %bitcast.5) | data formatting | bytes 12582912 | tf_op jit(solution)/shard_map/all_to_all | solution.py:53
  795.2 11.1 %all_to_all.16 = bf16[3,2048,4,128]{1,3,2,0:T(8,128)(2,1)} reshape(bf16[3,4,512,4,128]{2,1,4,3,0:T(4,128)(2,1)} %copy.13) | data formatting | bytes 12582912 | tf_op jit(solution)/shard_map/all_to_all | solution.py:53
  806.2 0.0 copy-start.3
  806.2 18.5 %fusion = f32[4,128]{1,0:T(4,128)S(1)} fusion(bf16[3,2048,4,128]{1,3,2,0:T(8,128)(2,1)} %all_to_all.16, bf16[2048,2048,1,1]{1,0,2,3:T(8,128)(2,1)} %reshape.253), kind=kOutput, calls=%fused_computation.2 | convolution fusion | flops 12894339072 | bytes 14682112 | tf_op jit(solution)/shard_map/ef,kfpy->kepy/dot_general | solution.py:54
  824.7 5.2 all-gather
  829.9 0.0 copy-done.3
  830.0 0.6 bitcast_multiply_fusion.1
  (2 shorter events, 0.0 us)
Async XLA Ops:
  0.0 51.6 %copy-start = (bf16[512,2,8,128]{3,2,1,0:T(8,128)(2,1)S(1)}, bf16[512,2,8,128]{3,2,1,0:T(8,128)(2,1)}, u32[]{:S(2)}) copy-start(bf16[512,2,8,128]{3,2,1,0:T(8,128)(2,1)} %param.4) | copy-start | bytes 6291460
  0.0 8.1 copy-start.1
  1.8 49.7 %collective-permute-start = (bf16[512,1,8,128]{3,2,1,0:T(8,128)(2,1)S(1)}, bf16[512,1,8,128]{3,2,1,0:T(8,128)(2,1)S(1)}, u32[]{:S(2)}, u32[]{:S(2)}) collective-permute-start(bf16[512,1,8,128]{3,2,1,0:T(8,128)(2,1)S(1)} %get-tuple-element.9), channel_id=1, source_target_pairs={{0,1},{1,2},{2,3},{3,4},{4,5},{5,6},{6,7},{8,9},{9,10},{10,11},{11... | collective-permute-start | bytes 3145736 | tf_op jit(solution)/shard_map/ppermute | solution.py:12
  6.8 44.8 %collective-permute-start.1 = (bf16[512,1,8,128]{3,2,1,0:T(8,128)(2,1)S(1)}, bf16[512,1,8,128]{3,2,1,0:T(8,128)(2,1)S(1)}, u32[]{:S(2)}, u32[]{:S(2)}) collective-permute-start(bf16[512,1,8,128]{3,2,1,0:T(8,128)(2,1)S(1)} %get-tuple-element.10), channel_id=1, source_target_pairs={{1,0},{2,1},{3,2},{4,3},{5,4},{6,5},{7,6},{9,8},{10,9},{11,10},{12... | collective-permute-start | bytes 3145736 | tf_op jit(solution)/shard_map/ppermute | solution.py:15
  61.8 10.7 %copy-start.2 = (f32[32768]{0:T(1024)S(1)}, f32[32768]{0:T(1024)}, u32[]{:S(2)}) copy-start(f32[32768]{0:T(1024)} %param.6) | copy-start | bytes 393220
  61.8 722.2 %all-to-all-start = ((bf16[3,512,16,128]{3,1,0,2:T(8,128)(2,1)}), bf16[3,512,16,128]{3,1,0,2:T(8,128)(2,1)}, u32[]{:S(2)}, u32[]{:S(2)}) async-start(bf16[3,512,16,128]{3,1,0,2:T(8,128)(2,1)} %pad_maximum_fusion), calls=%async_computation | async-start | bytes 12582912 | tf_op jit(solution)/shard_map/all_to_all | solution.py:53
  806.2 23.7 %copy-start.3 = (f32[2,8,128]{2,1,0:T(8,128)S(1)}, f32[2,8,128]{2,1,0:T(8,128)}, u32[]{:S(2)}) copy-start(f32[2,8,128]{2,1,0:T(8,128)} %param.7) | copy-start | bytes 24580
where the time goes:
time: 833 us; the launch traced here: 831 us
  other arithmetic  712 us (85%)
  waiting for transfers between devices  43.1 us (5%)
  local copies, waits for them, and re-layouts  39.4 us (5%)
  matrix products  18.5 us (2%)
  starting transfers between devices  11.7 us (1%)
    scatter-add x1, other arithmetic, coupling_rows(): summed = jax.ops.segment_sum(values, flat, num_segments=count * width)  689 us
    ppermute x1, waiting for transfers between devices, extended(): lax.ppermute(lax.slice_in_dim(block, block.shape[dim] - width, None, axis...  43.1 us
    all_to_all x2, local copies, waits for them, and re-layouts, local(): lax.all_to_all(sectioned, 'elec', split_axis=2, concat_axis=1, tiled=True)  22.3 us
    dot_general x1, matrix products, local(): jnp.einsum('ef,kfpy->kepy', coupling, moved, preferred_element_type=jnp.f...  18.5 us
  transfers between devices with their start and end apart: 3, of which 1 were waited for; matrix products, arithmetic and copies ran while one was open for 86% of the time, Pallas kernels for 0%

commit v1 on v0

v1 whole, which is shorter than its diff:
```python
import jax
import jax.numpy as jnp
from jax import lax
from jax.experimental import pallas as pl
from jax.experimental.pallas import tpu as pltpu
from jax.sharding import Mesh, PartitionSpec as P

BLOCK = 256
CHUNK = 1024


def onehots(dest, base, rows, plus, minus, up, down):
    zero = jnp.zeros((16, CHUNK), jnp.bfloat16)
    for group in range(rows // 16):
        here = lax.broadcasted_iota(jnp.int16, (16, CHUNK), 0) + jnp.int16(16 * group)
        dest[pl.ds(16 * group, 16), pl.ds(base, CHUNK)] = jnp.where(
            plus == here, up, jnp.where(minus == here, down, zero)
        )


def segment(kind, index, cols, electrodes):
    if kind == "folded":
        return BLOCK + index * cols
    at = index * cols
    return jnp.where(at < BLOCK, at, at - BLOCK + electrodes // 2)


def coupling_kernel(kind, shape, place, quads, res, out, *hot):
    electrodes, rows, pairs, share = shape
    cols = out.shape[0]
    group = (2 * place[0] + place[3]) * pairs + place[2]
    row_base = (place[1] * rows + group // share) * BLOCK
    col_base = row_base + segment(kind, group % share, cols, electrodes)
    steps = quads.shape[1] // CHUNK

    def build(step, rows_hot, cols_hot):
        at = pl.ds(pl.multiple_of(step * CHUNK, CHUNK), CHUNK)
        number = [quads[i : i + 1, at] for i in range(4)]
        empty = (number[0] == number[1]) | (number[2] == number[3])
        value = jnp.where(empty, 0.0, res[0:1, at])
        value = jnp.broadcast_to(value, (16, CHUNK)).astype(jnp.bfloat16)
        one = jnp.ones((16, CHUNK), jnp.bfloat16)

        def wide(row, base):
            local = (row - base) & (electrodes - 1)
            return jnp.broadcast_to(local, (16, CHUNK)).astype(jnp.int16)

        ends = [(0, 1, 2, 3), (2, 3, 0, 1)][: 2 if kind == "folded" else 1]
        for index, (a, b, m, n) in enumerate(ends):
            onehots(rows_hot, index * CHUNK, BLOCK, wide(number[a], row_base), wide(number[b], row_base), one, -one)
            onehots(cols_hot, index * CHUNK, cols, wide(number[m], col_base), wide(number[n], col_base), value, -value)

    def multiply(rows_hot, cols_hot):
        return lax.dot_general(
            cols_hot[...],
            rows_hot[...],
            (((1,), (1,)), ((), ())),
            preferred_element_type=jnp.float32,
        )

    build(0, hot[0], hot[1])

    def pair(index, total):
        build(2 * index + 1, hot[2], hot[3])
        total = total + multiply(hot[0], hot[1])
        build(jnp.minimum(2 * index + 2, steps - 1), hot[0], hot[1])
        return total + multiply(hot[2], hot[3])

    total = lax.fori_loop(0, steps // 2, pair, jnp.zeros((cols, BLOCK), jnp.float32))
    out[...] = total.astype(jnp.bfloat16)


SMEM = pl.BlockSpec(memory_space=pltpu.SMEM)
VMEM = pl.BlockSpec(memory_space=pltpu.VMEM)


def coupling_piece(kind, place, quadrupoles, residuals, shape, cols):
    depth = (2 if kind == "folded" else 1) * CHUNK
    hot = [pltpu.VMEM((rows, depth), jnp.bfloat16) for rows in (BLOCK, cols, BLOCK, cols)]
    return pl.pallas_call(
        lambda *refs: coupling_kernel(kind, shape, *refs),
        out_shape=jax.ShapeDtypeStruct((cols, BLOCK), jnp.bfloat16),
        in_specs=[SMEM, VMEM, VMEM],
        out_specs=VMEM,
        scratch_shapes=hot,
        compiler_params=pltpu.CompilerParams(vmem_limit_bytes=16 << 20),
        cost_estimate=pl.CostEstimate(
            flops=2 * cols * BLOCK * quadrupoles.shape[1] * depth // CHUNK,
            bytes_accessed=1 << 20,
            transcendentals=0,
        ),
        name="coupling_" + kind,
    )(place, quadrupoles, residuals)


def assemble_kernel(rows, far, place, *refs):
    pieces, field = refs[:-1], refs[-1]
    electrodes = field.shape[1]
    tiles, count, _ = pieces[0].shape
    members = len(pieces) // len(far)
    for index, piece in enumerate(pieces):
        slot, k = index // members, index % members
        row = 1 - place[0] if far[slot] else place[0]
        member = (place[1] + members - k) % members
        first = (row * members + member) * count - place[1] * rows * BLOCK
        first = pl.multiple_of((first + electrodes) % electrodes, count)
        for tile in range(tiles):
            field[tiles * (slot // 2) + tile, pl.ds(first, count)] = piece[tile]


def assemble(place, pieces, far, rows, electrodes):
    tiles = pieces[0].shape[0]
    return pl.pallas_call(
        lambda *refs: assemble_kernel(rows, far, *refs),
        out_shape=jax.ShapeDtypeStruct((tiles * (len(far) // 2), electrodes, 128), jnp.bfloat16),
        in_specs=[SMEM] + [VMEM] * len(pieces),
        out_specs=VMEM,
        compiler_params=pltpu.CompilerParams(vmem_limit_bytes=16 << 20),
        cost_estimate=pl.CostEstimate(flops=0, bytes_accessed=4 << 20, transcendentals=0),
        name="assemble_fields",
    )(place, *pieces)


def gradient_kernel(shape, parts, last, place, field, before, *refs):
    electrodes, rows, pairs, share = shape
    arrays = refs[: len(parts)]
    out, joined, turned, image = refs[len(parts) :]
    tiles = field.shape[0] // 3
    window = turned.shape[1]
    for kind in ("folded", "shared"):
        for array, (far_row, far_par, lane, contents) in zip(arrays, parts):
            row = 1 - place[0] if far_row else place[0]
            par = 1 - place[3] if far_par else place[3]
            source = 0
            for held, cols in contents:
                for k in range(pairs):
                    group = (2 * row + par) * pairs + (place[2] + pairs - k) % pairs
                    if held == kind:
                        at = pl.multiple_of(segment(kind, group % share, cols, electrodes), 16)
                        joined[pl.ds(at, cols), pl.ds(lane, array.shape[2])] = array[k, source : source + cols]
                source += cols
    first = pl.multiple_of((group // share) * BLOCK, BLOCK)
    turned[...] = joined[:window].T
    for tile in range(0, 3 * tiles, 2):
        two = [field[tile + i, pl.ds(first, window)] for i in range(2)]
        both = jnp.dot(turned[...], jnp.concatenate(two, axis=1), preferred_element_type=jnp.float32)
        image[tile] = both[:, :128]
        image[tile + 1] = both[:, 128:]
    lane = lax.broadcasted_iota(jnp.int32, (16, 128), 1)

    def fold(product):
        return product[:8] + product[8:]

    def along(value):
        return jnp.where(lane == 0, 0.0, value) - jnp.where(lane == 1, 0.0, pltpu.roll(value, 2, 1))

    nothing = jnp.zeros((1, 128), jnp.float32)
    for plane in range(2):

        def step(index, totals):
            at = pl.multiple_of(index * 16, 16)
            u = [
                field[tiles * plane + j, pl.ds(first + at, 16)].astype(jnp.float32)
                for j in range(2 * tiles)
            ]
            v = [image[tiles * plane + j, pl.ds(at, 16)] for j in range(2 * tiles)]
            new = []
            for j in range(tiles):
                new.append(fold(along(u[j]) * along(v[j])))
            for j in range(tiles - 1):
                new.append(fold((u[j] - u[j + 1]) * (v[j] - v[j + 1])))
            new.append(fold(u[tiles - 1] * v[tiles - 1]))
            for j in range(tiles):
                new.append(fold((u[j] - u[j + tiles]) * (v[j] - v[j + tiles])))
            return tuple(a + b for a, b in zip(totals, new))

        base = 3 * tiles * plane
        totals = lax.fori_loop(0, BLOCK // 16, step, tuple(before[base + j] for j in range(3 * tiles)))
        if not last:
            for j in range(3 * tiles):
                out[base + j] = totals[j]
            continue
        total = [0.25 * jnp.sum(value, axis=0, keepdims=True) for value in totals]
        for j in range(tiles):
            out[2 * plane, 2 * j : 2 * j + 1] = pltpu.roll(total[j], 127, 1)
            out[2 * plane, 2 * j + 1 : 2 * j + 2] = total[tiles + j]
            out[2 * plane + 1, 2 * j : 2 * j + 1] = total[2 * tiles + j]
            out[2 * plane + 1, 2 * j + 1 : 2 * j + 2] = nothing


def gradient_sums(place, field, before, entries, shape, window, last):
    arrays = [entry[0] for entry in entries]
    parts = [entry[1:] for entry in entries]
    tiles = field.shape[0] // 3
    folded = max(cols for part in parts for kind, cols in part[3] if kind == "folded")
    covered = max(window, BLOCK + shape[3] * folded)
    size = (4, 2 * tiles, 128) if last else before.shape
    return pl.pallas_call(
        lambda *refs: gradient_kernel(shape, parts, last, *refs),
        out_shape=jax.ShapeDtypeStruct(size, jnp.float32),
        in_specs=[SMEM, VMEM, VMEM] + [VMEM] * len(arrays),
        out_specs=VMEM,
        scratch_shapes=[
            pltpu.VMEM((covered, BLOCK), jnp.bfloat16),
            pltpu.VMEM((BLOCK, window), jnp.bfloat16),
            pltpu.VMEM((3 * tiles, BLOCK, 128), jnp.float32),
        ],
        compiler_params=pltpu.CompilerParams(vmem_limit_bytes=16 << 20),
        cost_estimate=pl.CostEstimate(
            flops=2 * BLOCK * window * 3 * tiles * 128, bytes_accessed=8 << 20, transcendentals=0
        ),
        name="gradient_sums",
    )(place, field, before, *arrays)


def rotations(value, axis):
    size = lax.axis_size(axis)
    return [
        lax.ppermute(value, axis, [(i, (i + k) % size) for i in range(size)]) for k in range(1, size)
    ]


def local(potentials, quadrupoles, residuals, cell_weight):
    count = potentials.shape[0]
    row, mem = lax.axis_index("row"), lax.axis_index("mem")
    pair, par = lax.axis_index("pair"), lax.axis_index("par")
    members, pairs = lax.axis_size("mem"), lax.axis_size("pair")
    electrodes = 2 * members * count
    rows = electrodes // BLOCK // members
    window = electrodes // 2 + BLOCK
    share = 4 * pairs // rows
    folded = -(-(window - 2 * BLOCK) // (16 * share)) * 16
    shared = 2 * BLOCK // share
    shape = (electrodes, rows, pairs, share)
    place = jnp.stack([row, mem, pair, par]).astype(jnp.int32)

    planes = jnp.transpose(potentials, (1, 2, 0, 3))
    even, odd = planes[:, 0::2], planes[:, ::-1][:, 0::2]
    mine = jnp.where(row == 0, even, odd)
    theirs = jnp.where(row == 0, odd, even)
    native, native_out = (jnp.where(par == 0, a[0], a[1]) for a in (mine, theirs))
    other, other_out = (jnp.where(par == 0, a[1], a[0]) for a in (mine, theirs))
    swap = [(0, 1), (1, 0)]
    ring = [(i, i - 1, 0) for i in range(1, pairs)] + [(i, i + 1, 1) for i in range(pairs - 1)]
    ahead = [(2 * a + p, 2 * b + p) for a, b, p in ring]
    ahead_across = [
        (2 * pairs * r + a, 2 * pairs * (1 - r) + b) for r in range(2) for a, b in ahead
    ]
    relay = lax.ppermute(other_out, "par", swap)
    first = [
        lax.ppermute(native_out, "row", swap),
        lax.ppermute(other, "par", swap),
        lax.ppermute(native_out, ("row", "pair", "par"), ahead_across),
        lax.ppermute(native, ("pair", "par"), ahead),
    ]
    inputs = (place, quadrupoles, residuals.reshape(1, -1), shape)

    piece = coupling_piece("folded", *inputs, folded)
    relay, first, _ = lax.optimization_barrier((relay, first, piece))
    second_across = lax.ppermute(relay, "row", swap)
    turns = rotations(piece, "pair")
    shared_piece = coupling_piece("shared", *inputs, shared)
    shared_turns = rotations(shared_piece, "pair")
    moved = second_across, first, native, turns
    (second_across, first, native, turns), _ = lax.optimization_barrier((moved, shared_piece))
    column = jnp.stack([piece] + turns)
    by_row = lax.ppermute(column, "row", swap)
    by_par = lax.ppermute(column, "par", swap)

    moved = second_across, first, native, shared_turns, by_row, by_par
    second_across, first, native, shared_turns, by_row, by_par = lax.optimization_barrier(moved)
    across, second, halo_across, halo = first
    tiles = native.shape[0]
    pieces = []
    for array in (native, across, second, second_across, halo, halo_across):
        pieces += [array] + rotations(array, "mem")
    field = assemble(place, pieces, (0, 1, 0, 1, 0, 1), rows, electrodes)
    shared_column = jnp.stack([shared_piece] + shared_turns)
    shared_by_row = lax.ppermute(shared_column, "row", swap)
    shared_by_par = lax.ppermute(shared_column, "par", swap)

    def entries(part, shared_part, far_row, far_par):
        return [
            (part, far_row, far_par, 0, (("folded", folded),)),
            (shared_part, far_row, far_par, 0, (("shared", shared),)),
        ]

    sums = jnp.zeros((6 * tiles, 8, 128), jnp.float32)
    near = entries(column, shared_column, 0, 0)
    staged = rows == 4
    arrived = by_row, by_par, shared_by_row, shared_by_par
    if staged:
        sums = gradient_sums(place, field, sums, near, shape, window, False)
        arrived, sums = lax.optimization_barrier((arrived, sums))
    by_row, by_par, shared_by_row, shared_by_par = arrived
    beside = entries(by_row, shared_by_row, 1, 0), entries(by_par, shared_by_par, 0, 1)
    half = BLOCK // 2
    lower = jnp.concatenate([by_row[..., :half], shared_by_row[..., :half]], axis=1)
    upper = jnp.concatenate([by_par[..., half:], shared_by_par[..., half:]], axis=1)
    corner = lax.ppermute(lower, "par", swap), lax.ppermute(upper, "row", swap)
    if staged:
        for part in beside:
            sums = gradient_sums(place, field, sums, part, shape, window, False)
        corner, sums = lax.optimization_barrier((corner, sums))
    contents = (("folded", folded), ("shared", shared))
    far = [(corner[0], 1, 1, 0, contents), (corner[1], 1, 1, half, contents)]
    part = far if staged else near + beside[0] + beside[1] + far
    sums = gradient_sums(place, field, sums, part, shape, window, True)

    sums = jnp.where(par == 0, sums, sums[::-1])
    sums = jnp.where(row == 0, sums, sums[:, ::-1])
    total = jnp.where(par == 0, sums[:2], sums[2:])
    total = total + lax.ppermute(jnp.where(par == 0, sums[2:], sums[:2]), "par", swap)
    total = total + lax.ppermute(total, "row", swap)
    for turn in rotations(total, "mem"):
        total = total + turn
    return total * cell_weight


def solution(mesh):
    elec, space = mesh.devices.shape
    names = ("row", "mem", "pair", "par")
    finer = Mesh(mesh.devices.reshape(2, elec // 2, space // 2, 2), names)
    e, s = names[:2], names[2:]
    placed = (P(e, s, None, None), P(), P(), P(s, None, None))
    return jax.shard_map(local, mesh=finer, in_specs=placed, out_specs=P(s, None, None), check_vma=False)
```

time: 833 us -> 101 us (0.12)
  other arithmetic: 712 us -> 3.2 us
  Pallas kernels: 0 us -> 41.6 us
  local copies, waits for them, and re-layouts: 39.4 us -> 2.36 us
  waiting for transfers between devices: 43.1 us -> 23.7 us
  matrix products: 18.5 us -> 0 us
  starting transfers between devices: 11.7 us -> 29.9 us
    scatter-add x1 -> x0, other arithmetic: 689 us -> none  [coupling_rows(): summed = jax.ops.segment_sum(values, flat, num_segments=count * width)]
    pallas_call x0 -> x7, Pallas kernels: none -> 41.6 us  [the longest x2 22.1 us: coupling_piece(): pl.pallas_call(lambda *refs: coupling_kernel(kind, shape, *refs), out_sha...]
    ppermute x2 -> x27, starting transfers between devices: 6.23 us -> 29.9 us  [the longest x13 9.1 us: rotations(): lax.ppermute(value, axis, [(i, (i + k) % size) for i in range(size)])]
    all_to_all x2 -> x0, local copies, waits for them, and re-layouts: 22.3 us -> none  [local(): lax.all_to_all(sectioned, 'elec', split_axis=2, concat_axis=1, tiled=True)]
    ppermute x2 -> x27, waiting for transfers between devices: 43.1 us -> 23.7 us  [the longest x13 10.1 us: rotations(): lax.ppermute(value, axis, [(i, (i + k) % size) for i in range(size)])]
    dot_general x1 -> x0, matrix products: 18.5 us -> none  [local(): jnp.einsum('ef,kfpy->kepy', coupling, moved, preferred_element_type=jnp.f...]
    convert_element_type x1 -> x0, local copies, waits for them, and re-layouts: 13.3 us -> none  [coupling_rows(): return summed.reshape(count, width).astype(jnp.bfloat16)]
    convert_element_type x2 -> x0, other arithmetic: 10 us -> none  [the longest x1 8.9 us: coupling_rows(): return summed.reshape(count, width).astype(jnp.bfloat16)]
  transfers between devices with their start and end apart: 3 -> 27, of which waited for: 1 -> 15; matrix products, arithmetic and copies ran while one was open for 86% -> 1% of each run, Pallas kernels for 0% -> 36%
where the time goes in v1:
time: 101 us
  Pallas kernels  41.6 us (41%)
  starting transfers between devices  29.9 us (30%)
  waiting for transfers between devices  23.7 us (23%)
  other arithmetic  3.2 us (3%)
  local copies, waits for them, and re-layouts  2.36 us (2%)
    pallas_call x2, Pallas kernels, coupling_piece(): pl.pallas_call(lambda *refs: coupling_kernel(kind, shape, *refs), out_sha...  22.1 us
    pallas_call x4, Pallas kernels, gradient_sums(): pl.pallas_call(lambda *refs: gradient_kernel(shape, parts, last, *refs),...  18.5 us
    ppermute x13, waiting for transfers between devices, rotations(): lax.ppermute(value, axis, [(i, (i + k) % size) for i in range(size)])  10.1 us
    ppermute x13, starting transfers between devices, rotations(): lax.ppermute(value, axis, [(i, (i + k) % size) for i in range(size)])  9.1 us
    ppermute x1, starting transfers between devices, local(): lax.ppermute(other, 'par', swap)  5.97 us
    ppermute x1, waiting for transfers between devices, local(): relay = lax.ppermute(other_out, 'par', swap)  5.44 us
    ppermute x1, starting transfers between devices, local(): lax.ppermute(native_out, 'row', swap)  2.94 us
    ppermute x1, waiting for transfers between devices, local(): lax.ppermute(native, ('pair', 'par'), ahead)  2.81 us
  transfers between devices with their start and end apart: 27, of which 15 were waited for; matrix products, arithmetic and copies ran while one was open for 1% of the time, Pallas kernels for 36%

profile of v1, /device:TPU:0, one launch (start us, length us, event | category | flops | bytes accessed | tf_op | source)
XLA Modules:
  0.0 101.0 jit_solution(14643321708792064259)
XLA Ops:
  0.0 2.1 %copy.7 = bf16[512,2,8,128]{3,0,2,1:T(8,128)(2,1)S(1)} copy(bf16[512,2,8,128]{3,2,1,0:T(8,128)(2,1)} %param.4) | data formatting | bytes 4194304 | tf_op args[0]
  2.1 0.1 slice.45
  2.2 0.4 broadcast_select_fusion
  2.6 0.0 copy-start
  2.6 0.0 copy-start.1
  2.7 1.1 %select_bitcast_fusion.2 = (bf16[4,512,128]{2,1,0:T(8,128)(2,1)}, bf16[4,512,128]{2,1,0:T(8,128)(2,1)}) fusion(pred[]{:T(512)S(6)} %eq.4, bf16[2,4,512,128]{3,2,1,0:T(8,128)(2,1)S(1)} %get-tuple-element.72), kind=kLoop, calls=%fused_computation.5 | loop fusion | flops 524288 | bytes 2097153 | tf_op jit(solution)/shard_map/jit(_where)/select_n | solution.py:241
  3.7 2.9 %collective-permute-start.1 = (bf16[4,512,128]{2,1,0:T(8,128)(2,1)}, bf16[4,512,128]{2,1,0:T(8,128)(2,1)S(1)}, u32[]{:S(2)}, u32[]{:S(2)}) collective-permute-start(bf16[4,512,128]{2,1,0:T(8,128)(2,1)} %get-tuple-element.75), channel_id=1, source_target_pairs={{0,16},{16,0},{1,17},{17,1},{2,18},{18,2},{3,19},{19,3},{4,20},{20... | collective-permute-start | bytes 1572872 | tf_op jit(solution)/shard_map/ppermute | solution.py:251
  6.7 1.3 %collective-permute-start.3 = (bf16[4,512,128]{2,1,0:T(8,128)(2,1)}, bf16[4,512,128]{2,1,0:T(8,128)(2,1)S(1)}, u32[]{:S(2)}, u32[]{:S(2)}) collective-permute-start(bf16[4,512,128]{2,1,0:T(8,128)(2,1)} %get-tuple-element.75), channel_id=1, source_target_pairs={{2,16},{4,18},{6,20},{1,19},{3,21},{5,23},{18,0},{20,2},{22,4},{17... | collective-permute-start | bytes 1572872 | tf_op jit(solution)/shard_map/ppermute | solution.py:253
  8.0 0.9 select_bitcast_fusion
  8.8 1.3 %collective-permute-start.4 = (bf16[4,512,128]{2,1,0:T(8,128)(2,1)S(1)}, bf16[4,512,128]{2,1,0:T(8,128)(2,1)S(1)}, u32[]{:S(2)}, u32[]{:S(2)}) collective-permute-start(bf16[4,512,128]{2,1,0:T(8,128)(2,1)S(1)} %get-tuple-element.52.refs_1_), channel_id=1, source_target_pairs={{2,0},{4,2},{6,4},{1,3},{3,5},{5,7},{10,8},{12,10},{14,12},{9,11},... | collective-permute-start | bytes 1572872 | tf_op jit(solution)/shard_map/ppermute | solution.py:254
  10.1 6.0 %collective-permute-start.2 = (bf16[4,512,128]{2,1,0:T(8,128)(2,1)}, bf16[4,512,128]{2,1,0:T(8,128)(2,1)S(1)}, u32[]{:S(2)}, u32[]{:S(2)}) collective-permute-start(bf16[4,512,128]{2,1,0:T(8,128)(2,1)} %get-tuple-element.74), channel_id=1, source_target_pairs={{0,1},{1,0},{2,3},{3,2},{4,5},{5,4},{6,7},{7,6},{8,9},{9,8},{10,11... | collective-permute-start | bytes 1572872 | tf_op jit(solution)/shard_map/ppermute | solution.py:252
  16.1 0.1 collective-permute-start
  16.2 0.1 pad_add_fusion.refs_0_
  16.2 14.2 %coupling_folded.1 = bf16[192,256]{1,0:T(8,128)(2,1)S(1)} custom-call(s32[4]{0:T(128)S(1)} %pad_add_fusion.refs_0_, s32[4,32768]{1,0:T(4,128)S(1)} %copy-done, f32[1,32768]{1,0:T(1,128)S(1)} %bitcast.26), custom_call_target="tpu_custom_call" | custom-call | flops 6442450944 | bytes 1048576 | tf_op jit(solution)/shard_map/coupling_folded/pallas_call | solution.py:80
  30.5 2.8 %collective-permute-done.4.refs_9_ = bf16[4,512,128]{2,1,0:T(8,128)(2,1)S(1)} collective-permute-done((bf16[4,512,128]{2,1,0:T(8,128)(2,1)S(1)}, bf16[4,512,128]{2,1,0:T(8,128)(2,1)S(1)}, u32[]{:S(2)}, u32[]{:S(2)}) %collective-permute-start.4) | collective-permute-done | bytes 524320 | tf_op jit(solution)/shard_map/ppermute | solution.py:254
  33.3 0.0 collective-permute-done.1.refs_3_
  33.3 0.0 collective-permute-done.3.refs_11_
  33.3 0.0 collective-permute-done.2.refs_5_
  33.3 5.4 %collective-permute-done = bf16[4,512,128]{2,1,0:T(8,128)(2,1)} collective-permute-done((bf16[4,512,128]{2,1,0:T(8,128)(2,1)}, bf16[4,512,128]{2,1,0:T(8,128)(2,1)}, u32[]{:S(2)}, u32[]{:S(2)}) %collective-permute-start) | collective-permute-done | bytes 524320 | tf_op jit(solution)/shard_map/ppermute | solution.py:249
  38.7 1.5 %collective-permute-start.5 = (bf16[4,512,128]{2,1,0:T(8,128)(2,1)}, bf16[4,512,128]{2,1,0:T(8,128)(2,1)S(1)}, u32[]{:S(2)}, u32[]{:S(2)}) collective-permute-start(bf16[4,512,128]{2,1,0:T(8,128)(2,1)} %collective-permute-done), channel_id=1, source_target_pairs={{0,16},{16,0},{1,17},{17,1},{2,18},{18,2},{3,19},{19,3},{4,20},{20... | collective-permute-start | bytes 1572872 | tf_op jit(solution)/shard_map/ppermute | solution.py:260
  40.2 1.5 %collective-permute-start.6 = (bf16[192,256]{1,0:T(8,128)(2,1)S(1)}, bf16[192,256]{1,0:T(8,128)(2,1)S(1)}, u32[]{:S(2)}, u32[]{:S(2)}) collective-permute-start(bf16[192,256]{1,0:T(8,128)(2,1)S(1)} %coupling_folded.1), channel_id=1, source_target_pairs={{0,2},{2,4},{4,6},{6,0},{1,3},{3,5},{5,7},{7,1},{8,10},{10,12},{12... | collective-permute-start | bytes 294920 | tf_op jit(solution)/shard_map/ppermute | solution.py:219
  41.8 0.6 collective-permute-start.7
  42.3 2.1 %collective-permute-start.8 = (bf16[192,256]{1,0:T(8,128)(2,1)S(1)}, bf16[192,256]{1,0:T(8,128)(2,1)S(1)}, u32[]{:S(2)}, u32[]{:S(2)}) collective-permute-start(bf16[192,256]{1,0:T(8,128)(2,1)S(1)} %coupling_folded.1), channel_id=1, source_target_pairs={{0,6},{2,0},{4,2},{6,4},{1,7},{3,1},{5,3},{7,5},{8,14},{10,8},{12,... | collective-permute-start | bytes 294920 | tf_op jit(solution)/shard_map/ppermute | solution.py:219
  44.4 7.9 %coupling_shared.1 = bf16[128,256]{1,0:T(8,128)(2,1)S(1)} custom-call(s32[4]{0:T(128)S(1)} %pad_add_fusion.refs_0_, s32[4,32768]{1,0:T(4,128)S(1)} %copy-done, f32[1,32768]{1,0:T(1,128)S(1)} %bitcast.27), custom_call_target="tpu_custom_call" | custom-call | flops 2147483648 | bytes 1048576 | tf_op jit(solution)/shard_map/coupling_shared/pallas_call | solution.py:80
  52.4 0.0 collective-permute-done.6
  52.4 0.0 collective-permute-done.5.refs_7_
  52.4 0.1 pad_maximum_fusion.refs_3_
  52.5 0.6 collective-permute-start.12
  53.1 1.7 %collective-permute-start.13 = (bf16[4,192,256]{2,1,0:T(8,128)(2,1)S(1)}, bf16[4,192,256]{2,1,0:T(8,128)(2,1)S(1)}, u32[]{:S(2)}, u32[]{:S(2)}) collective-permute-start(bf16[4,192,256]{2,1,0:T(8,128)(2,1)S(1)} %pad_maximum_fusion.refs_3_), channel_id=1, source_target_pairs={{0,1},{1,0},{2,3},{3,2},{4,5},{5,4},{6,7},{7,6},{8,9},{9,8},{10,11... | collective-permute-start | bytes 1179656 | tf_op jit(solution)/shard_map/ppermute | solution.py:268
  54.8 1.6 %collective-permute-start.10 = (bf16[128,256]{1,0:T(8,128)(2,1)S(1)}, bf16[128,256]{1,0:T(8,128)(2,1)S(1)}, u32[]{:S(2)}, u32[]{:S(2)}) collective-permute-start(bf16[128,256]{1,0:T(8,128)(2,1)S(1)} %coupling_shared.1), channel_id=1, source_target_pairs={{0,4},{2,6},{4,0},{6,2},{1,5},{3,7},{5,1},{7,3},{8,12},{10,14},{12... | collective-permute-start | bytes 196616 | tf_op jit(solution)/shard_map/ppermute | solution.py:219
  56.5 1.7 %collective-permute-start.11 = (bf16[128,256]{1,0:T(8,128)(2,1)S(1)}, bf16[128,256]{1,0:T(8,128)(2,1)S(1)}, u32[]{:S(2)}, u32[]{:S(2)}) collective-permute-start(bf16[128,256]{1,0:T(8,128)(2,1)S(1)} %coupling_shared.1), channel_id=1, source_target_pairs={{0,6},{2,0},{4,2},{6,4},{1,7},{3,1},{5,3},{7,5},{8,14},{10,8},{12,... | collective-permute-start | bytes 196616 | tf_op jit(solution)/shard_map/ppermute | solution.py:219
  58.2 0.3 collective-permute-start.9
  58.5 2.3 %collective-permute-done.10 = bf16[128,256]{1,0:T(8,128)(2,1)S(1)} collective-permute-done((bf16[128,256]{1,0:T(8,128)(2,1)S(1)}, bf16[128,256]{1,0:T(8,128)(2,1)S(1)}, u32[]{:S(2)}, u32[]{:S(2)}) %collective-permute-start.10) | collective-permute-done | bytes 65568 | tf_op jit(solution)/shard_map/ppermute | solution.py:219
  60.8 0.1 collective-permute-done.11
  60.9 3.3 %collective-permute-done.9 = bf16[128,256]{1,0:T(8,128)(2,1)S(1)} collective-permute-done((bf16[128,256]{1,0:T(8,128)(2,1)S(1)}, bf16[128,256]{1,0:T(8,128)(2,1)S(1)}, u32[]{:S(2)}, u32[]{:S(2)}) %collective-permute-start.9) | collective-permute-done | bytes 65568 | tf_op jit(solution)/shard_map/ppermute | solution.py:219
  64.2 0.0 collective-permute-done.12.refs_3_
  64.2 0.5 collective-permute-start.15
  64.7 0.1 collective-permute-start.16
  64.8 0.4 collective-permute-start.17
  65.3 0.1 collective-permute-start.18
  65.3 0.8 collective-permute-done.14.refs_2_
  66.1 0.1 collective-permute-start.19
  66.3 0.6 collective-permute-done.15.refs_4_
  66.9 0.7 collective-permute-start.20
  67.6 0.1 collective-permute-done.16.refs_6_
  67.6 0.5 collective-permute-start.21
  68.1 0.3 collective-permute-done.17.refs_8_
  68.4 0.7 collective-permute-done.18.refs_10_
  69.1 0.7 collective-permute-done.19.refs_12_
  69.9 1.0 assemble_fields.1.refs_1_
  70.9 4.6 %gradient_sums.4.refs_2_ = f32[24,8,128]{2,1,0:T(8,128)S(1)} custom-call(s32[4]{0:T(128)S(1)} %pad_add_fusion.refs_0_, bf16[12,2048,128]{2,1,0:T(8,128)(2,1)S(1)} %assemble_fields.1.refs_1_, f32[24,8,128]{2,1,0:T(8,128)S(1)} %broadcast_in_dim.3.refs_2_, bf16[4,192,256]{2,1,0:T(8,128)(2,1)S(1)} %pad_maximum_fusion.refs_3_, ...), custom_call_target="tpu_custom_call" | custom-call | flops 1006632960 | bytes 8388608 | tf_op jit(solution)/shard_map/gradient_sums/pallas_call | solution.py:198
  75.5 0.5 collective-permute-done.21.refs_4_
  76.1 1.1 %collective-permute-start.23 = (bf16[4,320,128]{2,1,0:T(8,128)(2,1)S(1)}, bf16[4,320,128]{2,1,0:T(8,128)(2,1)S(1)}, u32[]{:S(2)}, u32[]{:S(2)}) collective-permute-start(bf16[4,320,128]{2,1,0:T(8,128)(2,1)S(1)} %pad_maximum_fusion.2), channel_id=1, source_target_pairs={{0,16},{16,0},{1,17},{17,1},{2,18},{18,2},{3,19},{19,3},{4,20},{20... | collective-permute-start | bytes 983048 | tf_op jit(solution)/shard_map/ppermute | solution.py:300
  77.3 0.6 collective-permute-start.22
  77.8 4.6 %gradient_sums.5.refs_2_ = f32[24,8,128]{2,1,0:T(8,128)S(1)} custom-call(s32[4]{0:T(128)S(1)} %pad_add_fusion.refs_0_, bf16[12,2048,128]{2,1,0:T(8,128)(2,1)S(1)} %assemble_fields.1.refs_1_, f32[24,8,128]{2,1,0:T(8,128)S(1)} %gradient_sums.4.refs_2_, bf16[4,192,256]{2,1,0:T(8,128)(2,1)S(1)} %collective-permute-done.12.refs_3_, ...), custom_call_target="tpu_custom_call" | custom-call | flops 1006632960 | bytes 8388608 | tf_op jit(solution)/shard_map/gradient_sums/pallas_call | solution.py:198
  82.4 4.6 %gradient_sums.6.refs_2_ = f32[24,8,128]{2,1,0:T(8,128)S(1)} custom-call(s32[4]{0:T(128)S(1)} %pad_add_fusion.refs_0_, bf16[12,2048,128]{2,1,0:T(8,128)(2,1)S(1)} %assemble_fields.1.refs_1_, f32[24,8,128]{2,1,0:T(8,128)S(1)} %gradient_sums.5.refs_2_, bf16[4,192,256]{2,1,0:T(8,128)(2,1)S(1)} %collective-permute-done.13.refs_3_, ...), custom_call_target="tpu_custom_call" | custom-call | flops 1006632960 | bytes 8388608 | tf_op jit(solution)/shard_map/gradient_sums/pallas_call | solution.py:198
  87.0 0.0 copy-start.2
  87.0 4.8 %gradient_sums.7 = f32[4,8,128]{2,1,0:T(8,128)S(1)} custom-call(s32[4]{0:T(128)S(1)} %pad_add_fusion.refs_0_, bf16[12,2048,128]{2,1,0:T(8,128)(2,1)S(1)} %assemble_fields.1.refs_1_, f32[24,8,128]{2,1,0:T(8,128)S(1)} %gradient_sums.6.refs_2_, bf16[4,320,128]{2,1,0:T(8,128)(2,1)S(1)} %collective-permute-done.22.refs_3_, ...), custom_call_target="tpu_custom_call" | custom-call | flops 1006632960 | bytes 8388608 | tf_op jit(solution)/shard_map/gradient_sums/pallas_call | solution.py:198
  91.9 1.6 %collective-permute-start.24 = (f32[2,8,128]{2,1,0:T(8,128)S(1)}, f32[2,8,128]{2,1,0:T(8,128)S(1)}, u32[]{:S(2)}, u32[]{:S(2)}) collective-permute-start(f32[2,8,128]{2,1,0:T(8,128)S(1)} %slice_select_fusion), channel_id=1, source_target_pairs={{0,1},{1,0},{2,3},{3,2},{4,5},{5,4},{6,7},{7,6},{8,9},{9,8},{10,11... | collective-permute-start | bytes 24584 | tf_op jit(solution)/shard_map/ppermute | solution.py:313
  93.5 2.1 %collective-permute-done.24 = f32[2,8,128]{2,1,0:T(8,128)S(1)} collective-permute-done((f32[2,8,128]{2,1,0:T(8,128)S(1)}, f32[2,8,128]{2,1,0:T(8,128)S(1)}, u32[]{:S(2)}, u32[]{:S(2)}) %collective-permute-start.24) | collective-permute-done | bytes 8224 | tf_op jit(solution)/shard_map/ppermute | solution.py:313
  95.6 1.0 %collective-permute-start.25 = (f32[2,8,128]{2,1,0:T(8,128)S(1)}, f32[2,8,128]{2,1,0:T(8,128)S(1)}, u32[]{:S(2)}, u32[]{:S(2)}) collective-permute-start(f32[2,8,128]{2,1,0:T(8,128)S(1)} %select_add_fusion), channel_id=1, source_target_pairs={{0,16},{16,0},{1,17},{17,1},{2,18},{18,2},{3,19},{19,3},{4,20},{20... | collective-permute-start | bytes 24584 | tf_op jit(solution)/shard_map/ppermute | solution.py:314
  96.6 2.6 %collective-permute-done.25 = f32[2,8,128]{2,1,0:T(8,128)S(1)} collective-permute-done((f32[2,8,128]{2,1,0:T(8,128)S(1)}, f32[2,8,128]{2,1,0:T(8,128)S(1)}, u32[]{:S(2)}, u32[]{:S(2)}) %collective-permute-start.25) | collective-permute-done | bytes 8224 | tf_op jit(solution)/shard_map/ppermute | solution.py:314
  99.2 1.2 %collective-permute-done.26 = f32[2,8,128]{2,1,0:T(8,128)S(1)} collective-permute-done((f32[2,8,128]{2,1,0:T(8,128)S(1)}, f32[2,8,128]{2,1,0:T(8,128)S(1)}, u32[]{:S(2)}, u32[]{:S(2)}) %collective-permute-start.26) | collective-permute-done | bytes 8224 | tf_op jit(solution)/shard_map/ppermute | solution.py:219
  100.4 0.6 add_multiply_fusion
  (25 shorter events, 0.3 us)
Async XLA Ops:
  2.6 13.6 %copy-start = (s32[4,32768]{1,0:T(4,128)S(1)}, s32[4,32768]{1,0:T(4,128)}, u32[]{:S(2)}) copy-start(s32[4,32768]{1,0:T(4,128)} %refs_1_.3) | copy-start | bytes 1572868
  2.6 13.6 %copy-start.1 = (f32[32768]{0:T(1024)S(1)}, f32[32768]{0:T(1024)}, u32[]{:S(2)}) copy-start(f32[32768]{0:T(1024)} %param.6) | copy-start | bytes 393220
  3.7 29.5 %collective-permute-start.1 = (bf16[4,512,128]{2,1,0:T(8,128)(2,1)}, bf16[4,512,128]{2,1,0:T(8,128)(2,1)S(1)}, u32[]{:S(2)}, u32[]{:S(2)}) collective-permute-start(bf16[4,512,128]{2,1,0:T(8,128)(2,1)} %get-tuple-element.75), channel_id=1, source_target_pairs={{0,16},{16,0},{1,17},{17,1},{2,18},{18,2},{3,19},{19,3},{4,20},{20... | collective-permute-start | bytes 1572872 | tf_op jit(solution)/shard_map/ppermute | solution.py:251
  6.7 26.6 %collective-permute-start.3 = (bf16[4,512,128]{2,1,0:T(8,128)(2,1)}, bf16[4,512,128]{2,1,0:T(8,128)(2,1)S(1)}, u32[]{:S(2)}, u32[]{:S(2)}) collective-permute-start(bf16[4,512,128]{2,1,0:T(8,128)(2,1)} %get-tuple-element.75), channel_id=1, source_target_pairs={{2,16},{4,18},{6,20},{1,19},{3,21},{5,23},{18,0},{20,2},{22,4},{17... | collective-permute-start | bytes 1572872 | tf_op jit(solution)/shard_map/ppermute | solution.py:253
  8.8 24.4 %collective-permute-start.4 = (bf16[4,512,128]{2,1,0:T(8,128)(2,1)S(1)}, bf16[4,512,128]{2,1,0:T(8,128)(2,1)S(1)}, u32[]{:S(2)}, u32[]{:S(2)}) collective-permute-start(bf16[4,512,128]{2,1,0:T(8,128)(2,1)S(1)} %get-tuple-element.52.refs_1_), channel_id=1, source_target_pairs={{2,0},{4,2},{6,4},{1,3},{3,5},{5,7},{10,8},{12,10},{14,12},{9,11},... | collective-permute-start | bytes 1572872 | tf_op jit(solution)/shard_map/ppermute | solution.py:254
  10.1 23.2 %collective-permute-start.2 = (bf16[4,512,128]{2,1,0:T(8,128)(2,1)}, bf16[4,512,128]{2,1,0:T(8,128)(2,1)S(1)}, u32[]{:S(2)}, u32[]{:S(2)}) collective-permute-start(bf16[4,512,128]{2,1,0:T(8,128)(2,1)} %get-tuple-element.74), channel_id=1, source_target_pairs={{0,1},{1,0},{2,3},{3,2},{4,5},{5,4},{6,7},{7,6},{8,9},{9,8},{10,11... | collective-permute-start | bytes 1572872 | tf_op jit(solution)/shard_map/ppermute | solution.py:252
  16.1 22.6 %collective-permute-start = (bf16[4,512,128]{2,1,0:T(8,128)(2,1)}, bf16[4,512,128]{2,1,0:T(8,128)(2,1)}, u32[]{:S(2)}, u32[]{:S(2)}) collective-permute-start(bf16[4,512,128]{2,1,0:T(8,128)(2,1)} %get-tuple-element.76), channel_id=1, source_target_pairs={{0,1},{1,0},{2,3},{3,2},{4,5},{5,4},{6,7},{7,6},{8,9},{9,8},{10,11... | collective-permute-start | bytes 1572872 | tf_op jit(solution)/shard_map/ppermute | solution.py:249
  38.7 13.7 %collective-permute-start.5 = (bf16[4,512,128]{2,1,0:T(8,128)(2,1)}, bf16[4,512,128]{2,1,0:T(8,128)(2,1)S(1)}, u32[]{:S(2)}, u32[]{:S(2)}) collective-permute-start(bf16[4,512,128]{2,1,0:T(8,128)(2,1)} %collective-permute-done), channel_id=1, source_target_pairs={{0,16},{16,0},{1,17},{17,1},{2,18},{18,2},{3,19},{19,3},{4,20},{20... | collective-permute-start | bytes 1572872 | tf_op jit(solution)/shard_map/ppermute | solution.py:260
  40.2 12.2 %collective-permute-start.6 = (bf16[192,256]{1,0:T(8,128)(2,1)S(1)}, bf16[192,256]{1,0:T(8,128)(2,1)S(1)}, u32[]{:S(2)}, u32[]{:S(2)}) collective-permute-start(bf16[192,256]{1,0:T(8,128)(2,1)S(1)} %coupling_folded.1), channel_id=1, source_target_pairs={{0,2},{2,4},{4,6},{6,0},{1,3},{3,5},{5,7},{7,1},{8,10},{10,12},{12... | collective-permute-start | bytes 294920 | tf_op jit(solution)/shard_map/ppermute | solution.py:219
  41.8 10.6 %collective-permute-start.7 = (bf16[192,256]{1,0:T(8,128)(2,1)S(1)}, bf16[192,256]{1,0:T(8,128)(2,1)S(1)}, u32[]{:S(2)}, u32[]{:S(2)}) collective-permute-start(bf16[192,256]{1,0:T(8,128)(2,1)S(1)} %coupling_folded.1), channel_id=1, source_target_pairs={{0,4},{2,6},{4,0},{6,2},{1,5},{3,7},{5,1},{7,3},{8,12},{10,14},{12... | collective-permute-start | bytes 294920 | tf_op jit(solution)/shard_map/ppermute | solution.py:219
  42.3 10.0 %collective-permute-start.8 = (bf16[192,256]{1,0:T(8,128)(2,1)S(1)}, bf16[192,256]{1,0:T(8,128)(2,1)S(1)}, u32[]{:S(2)}, u32[]{:S(2)}) collective-permute-start(bf16[192,256]{1,0:T(8,128)(2,1)S(1)} %coupling_folded.1), channel_id=1, source_target_pairs={{0,6},{2,0},{4,2},{6,4},{1,7},{3,1},{5,3},{7,5},{8,14},{10,8},{12,... | collective-permute-start | bytes 294920 | tf_op jit(solution)/shard_map/ppermute | solution.py:219
  52.5 11.8 %collective-permute-start.12 = (bf16[4,192,256]{2,1,0:T(8,128)(2,1)S(1)}, bf16[4,192,256]{2,1,0:T(8,128)(2,1)S(1)}, u32[]{:S(2)}, u32[]{:S(2)}) collective-permute-start(bf16[4,192,256]{2,1,0:T(8,128)(2,1)S(1)} %pad_maximum_fusion.refs_3_), channel_id=1, source_target_pairs={{0,16},{16,0},{1,17},{17,1},{2,18},{18,2},{3,19},{19,3},{4,20},{20... | collective-permute-start | bytes 1179656 | tf_op jit(solution)/shard_map/ppermute | solution.py:267
  53.1 11.2 %collective-permute-start.13 = (bf16[4,192,256]{2,1,0:T(8,128)(2,1)S(1)}, bf16[4,192,256]{2,1,0:T(8,128)(2,1)S(1)}, u32[]{:S(2)}, u32[]{:S(2)}) collective-permute-start(bf16[4,192,256]{2,1,0:T(8,128)(2,1)S(1)} %pad_maximum_fusion.refs_3_), channel_id=1, source_target_pairs={{0,1},{1,0},{2,3},{3,2},{4,5},{5,4},{6,7},{7,6},{8,9},{9,8},{10,11... | collective-permute-start | bytes 1179656 | tf_op jit(solution)/shard_map/ppermute | solution.py:268
  54.8 6.0 %collective-permute-start.10 = (bf16[128,256]{1,0:T(8,128)(2,1)S(1)}, bf16[128,256]{1,0:T(8,128)(2,1)S(1)}, u32[]{:S(2)}, u32[]{:S(2)}) collective-permute-start(bf16[128,256]{1,0:T(8,128)(2,1)S(1)} %coupling_shared.1), channel_id=1, source_target_pairs={{0,4},{2,6},{4,0},{6,2},{1,5},{3,7},{5,1},{7,3},{8,12},{10,14},{12... | collective-permute-start | bytes 196616 | tf_op jit(solution)/shard_map/ppermute | solution.py:219
  56.5 4.4 %collective-permute-start.11 = (bf16[128,256]{1,0:T(8,128)(2,1)S(1)}, bf16[128,256]{1,0:T(8,128)(2,1)S(1)}, u32[]{:S(2)}, u32[]{:S(2)}) collective-permute-start(bf16[128,256]{1,0:T(8,128)(2,1)S(1)} %coupling_shared.1), channel_id=1, source_target_pairs={{0,6},{2,0},{4,2},{6,4},{1,7},{3,1},{5,3},{7,5},{8,14},{10,8},{12,... | collective-permute-start | bytes 196616 | tf_op jit(solution)/shard_map/ppermute | solution.py:219
  58.2 6.1 %collective-permute-start.9 = (bf16[128,256]{1,0:T(8,128)(2,1)S(1)}, bf16[128,256]{1,0:T(8,128)(2,1)S(1)}, u32[]{:S(2)}, u32[]{:S(2)}) collective-permute-start(bf16[128,256]{1,0:T(8,128)(2,1)S(1)} %coupling_shared.1), channel_id=1, source_target_pairs={{0,2},{2,4},{4,6},{6,0},{1,3},{3,5},{5,7},{7,1},{8,10},{10,12},{12... | collective-permute-start | bytes 196616 | tf_op jit(solution)/shard_map/ppermute | solution.py:219
  64.2 1.9 %collective-permute-start.14 = (bf16[4,512,128]{2,1,0:T(8,128)(2,1)S(1)}, bf16[4,512,128]{2,1,0:T(8,128)(2,1)S(1)}, u32[]{:S(2)}, u32[]{:S(2)}) collective-permute-start(bf16[4,512,128]{2,1,0:T(8,128)(2,1)S(1)} %get-tuple-element.52.refs_1_), channel_id=1, source_target_pairs={{0,8},{8,0},{1,9},{9,1},{2,10},{10,2},{3,11},{11,3},{4,12},{12,4},... | collective-permute-start | bytes 1572872 | tf_op jit(solution)/shard_map/ppermute | solution.py:219
  64.2 2.7 %collective-permute-start.15 = (bf16[4,512,128]{2,1,0:T(8,128)(2,1)S(1)}, bf16[4,512,128]{2,1,0:T(8,128)(2,1)S(1)}, u32[]{:S(2)}, u32[]{:S(2)}) collective-permute-start(bf16[4,512,128]{2,1,0:T(8,128)(2,1)S(1)} %collective-permute-done.1.refs_3_), channel_id=1, source_target_pairs={{0,8},{8,0},{1,9},{9,1},{2,10},{10,2},{3,11},{11,3},{4,12},{12,4},... | collective-permute-start | bytes 1572872 | tf_op jit(solution)/shard_map/ppermute | solution.py:219
  64.7 2.9 %collective-permute-start.16 = (bf16[4,512,128]{2,1,0:T(8,128)(2,1)S(1)}, bf16[4,512,128]{2,1,0:T(8,128)(2,1)S(1)}, u32[]{:S(2)}, u32[]{:S(2)}) collective-permute-start(bf16[4,512,128]{2,1,0:T(8,128)(2,1)S(1)} %collective-permute-done.2.refs_5_), channel_id=1, source_target_pairs={{0,8},{8,0},{1,9},{9,1},{2,10},{10,2},{3,11},{11,3},{4,12},{12,4},... | collective-permute-start | bytes 1572872 | tf_op jit(solution)/shard_map/ppermute | solution.py:219
  64.8 3.6 %collective-permute-start.17 = (bf16[4,512,128]{2,1,0:T(8,128)(2,1)S(1)}, bf16[4,512,128]{2,1,0:T(8,128)(2,1)S(1)}, u32[]{:S(2)}, u32[]{:S(2)}) collective-permute-start(bf16[4,512,128]{2,1,0:T(8,128)(2,1)S(1)} %collective-permute-done.5.refs_7_), channel_id=1, source_target_pairs={{0,8},{8,0},{1,9},{9,1},{2,10},{10,2},{3,11},{11,3},{4,12},{12,4},... | collective-permute-start | bytes 1572872 | tf_op jit(solution)/shard_map/ppermute | solution.py:219
  65.3 3.9 %collective-permute-start.18 = (bf16[4,512,128]{2,1,0:T(8,128)(2,1)S(1)}, bf16[4,512,128]{2,1,0:T(8,128)(2,1)S(1)}, u32[]{:S(2)}, u32[]{:S(2)}) collective-permute-start(bf16[4,512,128]{2,1,0:T(8,128)(2,1)S(1)} %collective-permute-done.4.refs_9_), channel_id=1, source_target_pairs={{0,8},{8,0},{1,9},{9,1},{2,10},{10,2},{3,11},{11,3},{4,12},{12,4},... | collective-permute-start | bytes 1572872 | tf_op jit(solution)/shard_map/ppermute | solution.py:219
  66.1 3.7 %collective-permute-start.19 = (bf16[4,512,128]{2,1,0:T(8,128)(2,1)S(1)}, bf16[4,512,128]{2,1,0:T(8,128)(2,1)S(1)}, u32[]{:S(2)}, u32[]{:S(2)}) collective-permute-start(bf16[4,512,128]{2,1,0:T(8,128)(2,1)S(1)} %collective-permute-done.3.refs_11_), channel_id=1, source_target_pairs={{0,8},{8,0},{1,9},{9,1},{2,10},{10,2},{3,11},{11,3},{4,12},{12,4},... | collective-permute-start | bytes 1572872 | tf_op jit(solution)/shard_map/ppermute | solution.py:219
  66.9 8.6 %collective-permute-start.20 = (bf16[4,128,256]{2,1,0:T(8,128)(2,1)S(1)}, bf16[4,128,256]{2,1,0:T(8,128)(2,1)S(1)}, u32[]{:S(2)}, u32[]{:S(2)}) collective-permute-start(bf16[4,128,256]{2,1,0:T(8,128)(2,1)S(1)} %pad_maximum_fusion.3.refs_4_), channel_id=1, source_target_pairs={{0,16},{16,0},{1,17},{17,1},{2,18},{18,2},{3,19},{19,3},{4,20},{20... | collective-permute-start | bytes 786440 | tf_op jit(solution)/shard_map/ppermute | solution.py:279
  67.6 8.3 %collective-permute-start.21 = (bf16[4,128,256]{2,1,0:T(8,128)(2,1)S(1)}, bf16[4,128,256]{2,1,0:T(8,128)(2,1)S(1)}, u32[]{:S(2)}, u32[]{:S(2)}) collective-permute-start(bf16[4,128,256]{2,1,0:T(8,128)(2,1)S(1)} %pad_maximum_fusion.3.refs_4_), channel_id=1, source_target_pairs={{0,1},{1,0},{2,3},{3,2},{4,5},{5,4},{6,7},{7,6},{8,9},{9,8},{10,11... | collective-permute-start | bytes 786440 | tf_op jit(solution)/shard_map/ppermute | solution.py:280
  76.1 10.9 %collective-permute-start.23 = (bf16[4,320,128]{2,1,0:T(8,128)(2,1)S(1)}, bf16[4,320,128]{2,1,0:T(8,128)(2,1)S(1)}, u32[]{:S(2)}, u32[]{:S(2)}) collective-permute-start(bf16[4,320,128]{2,1,0:T(8,128)(2,1)S(1)} %pad_maximum_fusion.2), channel_id=1, source_target_pairs={{0,16},{16,0},{1,17},{17,1},{2,18},{18,2},{3,19},{19,3},{4,20},{20... | collective-permute-start | bytes 983048 | tf_op jit(solution)/shard_map/ppermute | solution.py:300
  77.3 9.7 %collective-permute-start.22 = (bf16[4,320,128]{2,1,0:T(8,128)(2,1)S(1)}, bf16[4,320,128]{2,1,0:T(8,128)(2,1)S(1)}, u32[]{:S(2)}, u32[]{:S(2)}) collective-permute-start(bf16[4,320,128]{2,1,0:T(8,128)(2,1)S(1)} %pad_maximum_fusion.1), channel_id=1, source_target_pairs={{0,1},{1,0},{2,3},{3,2},{4,5},{5,4},{6,7},{7,6},{8,9},{9,8},{10,11... | collective-permute-start | bytes 983048 | tf_op jit(solution)/shard_map/ppermute | solution.py:300
  87.0 13.4 %copy-start.2 = (f32[2,8,128]{2,1,0:T(8,128)S(1)}, f32[2,8,128]{2,1,0:T(8,128)}, u32[]{:S(2)}) copy-start(f32[2,8,128]{2,1,0:T(8,128)} %param.7) | copy-start | bytes 24580
  91.9 3.7 %collective-permute-start.24 = (f32[2,8,128]{2,1,0:T(8,128)S(1)}, f32[2,8,128]{2,1,0:T(8,128)S(1)}, u32[]{:S(2)}, u32[]{:S(2)}) collective-permute-start(f32[2,8,128]{2,1,0:T(8,128)S(1)} %slice_select_fusion), channel_id=1, source_target_pairs={{0,1},{1,0},{2,3},{3,2},{4,5},{5,4},{6,7},{7,6},{8,9},{9,8},{10,11... | collective-permute-start | bytes 24584 | tf_op jit(solution)/shard_map/ppermute | solution.py:313
  95.6 3.7 %collective-permute-start.25 = (f32[2,8,128]{2,1,0:T(8,128)S(1)}, f32[2,8,128]{2,1,0:T(8,128)S(1)}, u32[]{:S(2)}, u32[]{:S(2)}) collective-permute-start(f32[2,8,128]{2,1,0:T(8,128)S(1)} %select_add_fusion), channel_id=1, source_target_pairs={{0,16},{16,0},{1,17},{17,1},{2,18},{18,2},{3,19},{19,3},{4,20},{20... | collective-permute-start | bytes 24584 | tf_op jit(solution)/shard_map/ppermute | solution.py:314
  99.2 1.2 %collective-permute-start.26 = (f32[2,8,128]{2,1,0:T(8,128)S(1)}, f32[2,8,128]{2,1,0:T(8,128)S(1)}, u32[]{:S(2)}, u32[]{:S(2)}) collective-permute-start(f32[2,8,128]{2,1,0:T(8,128)S(1)} %add.10), channel_id=1, source_target_pairs={{0,8},{8,0},{1,9},{9,1},{2,10},{10,2},{3,11},{11,3},{4,12},{12,4},... | collective-permute-start | bytes 24584 | tf_op jit(solution)/shard_map/ppermute | solution.py:219

commit v2 on v1

v2 whole, which is shorter than its diff:
```python
import jax
import jax.numpy as jnp
from jax import lax
from jax.experimental import pallas as pl
from jax.experimental.pallas import tpu as pltpu
from jax.sharding import Mesh, PartitionSpec as P

BLOCK = 256
CHUNK = 1024


def onehots(dest, first, rows, plus, minus, up, down):
    zero = jnp.zeros((16, CHUNK), jnp.bfloat16)
    for group in range(rows // 16):
        here = lax.broadcasted_iota(jnp.int16, (16, CHUNK), 0) + jnp.int16(16 * group)
        dest[pl.ds(first + 16 * group, 16)] = jnp.where(
            plus == here, up, jnp.where(minus == here, down, zero)
        )


def segment(kind, index, cols, electrodes):
    if kind == "folded":
        return BLOCK + index * cols
    at = index * cols
    return jnp.where(at < BLOCK, at, at - BLOCK + electrodes // 2)


def coupling_kernel(shape, place, quads, res, out, *hot):
    electrodes, rows, pairs, share, folded, shared = shape
    group = (2 * place[0] + place[3]) * pairs + place[2]
    row_base = (place[1] * rows + group // share) * BLOCK
    folded_base = row_base + segment("folded", group % share, folded, electrodes)
    shared_base = row_base + segment("shared", group % share, shared, electrodes)
    steps = quads.shape[1] // CHUNK

    def build(step, near_hot, far_hot, cols_hot, back_hot):
        at = pl.ds(pl.multiple_of(step * CHUNK, CHUNK), CHUNK)
        number = [quads[i : i + 1, at] for i in range(4)]
        empty = (number[0] == number[1]) | (number[2] == number[3])
        value = jnp.where(empty, 0.0, res[0:1, at])
        value = jnp.broadcast_to(value, (16, CHUNK)).astype(jnp.bfloat16)
        one = jnp.ones((16, CHUNK), jnp.bfloat16)

        def wide(row, base):
            local = (row - base) & (electrodes - 1)
            return jnp.broadcast_to(local, (16, CHUNK)).astype(jnp.int16)

        a, b, m, n = number
        onehots(near_hot, 0, BLOCK, wide(a, row_base), wide(b, row_base), one, -one)
        onehots(far_hot, 0, BLOCK, wide(m, row_base), wide(n, row_base), one, -one)
        onehots(cols_hot, 0, folded, wide(m, folded_base), wide(n, folded_base), value, -value)
        onehots(cols_hot, folded, shared, wide(m, shared_base), wide(n, shared_base), value, -value)
        onehots(back_hot, 0, folded, wide(a, folded_base), wide(b, folded_base), value, -value)

    def multiply(near_hot, far_hot, cols_hot, back_hot):
        dims = (((1,), (1,)), ((), ()))
        ahead = lax.dot_general(cols_hot[...], near_hot[...], dims, preferred_element_type=jnp.float32)
        back = lax.dot_general(back_hot[...], far_hot[...], dims, preferred_element_type=jnp.float32)
        return ahead[:folded] + back, ahead[folded:]

    def add(total, new):
        return total[0] + new[0], total[1] + new[1]

    build(0, *hot[:4])

    def pair(index, total):
        build(2 * index + 1, *hot[4:])
        total = add(total, multiply(*hot[:4]))
        build(jnp.minimum(2 * index + 2, steps - 1), *hot[:4])
        return add(total, multiply(*hot[4:]))

    zeros = jnp.zeros((folded, BLOCK), jnp.float32), jnp.zeros((shared, BLOCK), jnp.float32)
    total = lax.fori_loop(0, steps // 2, pair, zeros)
    out[:folded] = total[0].astype(jnp.bfloat16)
    out[folded:] = total[1].astype(jnp.bfloat16)


SMEM = pl.BlockSpec(memory_space=pltpu.SMEM)
VMEM = pl.BlockSpec(memory_space=pltpu.VMEM)


def coupling_piece(place, quadrupoles, residuals, shape):
    folded, shared = shape[4:]
    hot = [pltpu.VMEM((rows, CHUNK), jnp.bfloat16) for rows in (BLOCK, BLOCK, folded + shared, folded)]
    return pl.pallas_call(
        lambda *refs: coupling_kernel(shape, *refs),
        out_shape=jax.ShapeDtypeStruct((folded + shared, BLOCK), jnp.bfloat16),
        in_specs=[SMEM, VMEM, VMEM],
        out_specs=VMEM,
        scratch_shapes=hot + hot,
        compiler_params=pltpu.CompilerParams(vmem_limit_bytes=16 << 20),
        cost_estimate=pl.CostEstimate(
            flops=2 * (2 * folded + shared) * BLOCK * quadrupoles.shape[1],
            bytes_accessed=1 << 20,
            transcendentals=0,
        ),
        name="coupling_piece",
    )(place, quadrupoles, residuals)


def assemble_kernel(rows, far, place, *refs):
    pieces, field = refs[:-1], refs[-1]
    electrodes = field.shape[1]
    tiles, count, _ = pieces[0].shape
    members = len(pieces) // len(far)
    for index, piece in enumerate(pieces):
        slot, k = index // members, index % members
        row = 1 - place[0] if far[slot] else place[0]
        member = (place[1] + members - k) % members
        first = (row * members + member) * count - place[1] * rows * BLOCK
        first = pl.multiple_of((first + electrodes) % electrodes, count)
        for tile in range(tiles):
            field[tiles * (slot // 2) + tile, pl.ds(first, count)] = piece[tile]


def assemble(place, pieces, far, rows, electrodes):
    tiles = pieces[0].shape[0]
    return pl.pallas_call(
        lambda *refs: assemble_kernel(rows, far, *refs),
        out_shape=jax.ShapeDtypeStruct((tiles * (len(far) // 2), electrodes, 128), jnp.bfloat16),
        in_specs=[SMEM] + [VMEM] * len(pieces),
        out_specs=VMEM,
        compiler_params=pltpu.CompilerParams(vmem_limit_bytes=16 << 20),
        cost_estimate=pl.CostEstimate(flops=0, bytes_accessed=4 << 20, transcendentals=0),
        name="assemble_fields",
    )(place, *pieces)


def gradient_kernel(shape, parts, last, place, field, before, *refs):
    electrodes, rows, pairs, share, folded, shared = shape
    arrays = refs[: len(parts)]
    out, joined, turned, image = refs[len(parts) :]
    tiles = field.shape[0] // 3
    window = turned.shape[1]
    for kind, source, cols in (("folded", 0, folded), ("shared", folded, shared)):
        for array, (far_row, far_par, lane) in zip(arrays, parts):
            row = 1 - place[0] if far_row else place[0]
            par = 1 - place[3] if far_par else place[3]
            for k in range(pairs):
                group = (2 * row + par) * pairs + (place[2] + pairs - k) % pairs
                at = pl.multiple_of(segment(kind, group % share, cols, electrodes), 16)
                joined[pl.ds(at, cols), pl.ds(lane, array.shape[2])] = array[k, source : source + cols]
    first = pl.multiple_of((group // share) * BLOCK, BLOCK)
    turned[...] = joined[:window].T
    for tile in range(0, 3 * tiles, 2):
        two = [field[tile + i, pl.ds(first, window)] for i in range(2)]
        both = jnp.dot(turned[...], jnp.concatenate(two, axis=1), preferred_element_type=jnp.float32)
        image[tile] = both[:, :128]
        image[tile + 1] = both[:, 128:]
    lane = lax.broadcasted_iota(jnp.int32, (16, 128), 1)

    def fold(product):
        return product[:8] + product[8:]

    def along(value):
        return jnp.where(lane == 0, 0.0, value) - jnp.where(lane == 1, 0.0, pltpu.roll(value, 2, 1))

    nothing = jnp.zeros((1, 128), jnp.float32)
    for plane in range(2):

        def step(index, totals):
            at = pl.multiple_of(index * 16, 16)
            u = [
                field[tiles * plane + j, pl.ds(first + at, 16)].astype(jnp.float32)
                for j in range(2 * tiles)
            ]
            v = [image[tiles * plane + j, pl.ds(at, 16)] for j in range(2 * tiles)]
            new = []
            for j in range(tiles):
                new.append(fold(along(u[j]) * along(v[j])))
            for j in range(tiles - 1):
                new.append(fold((u[j] - u[j + 1]) * (v[j] - v[j + 1])))
            new.append(fold(u[tiles - 1] * v[tiles - 1]))
            for j in range(tiles):
                new.append(fold((u[j] - u[j + tiles]) * (v[j] - v[j + tiles])))
            return tuple(a + b for a, b in zip(totals, new))

        base = 3 * tiles * plane
        start = tuple(before[base + j] for j in range(3 * tiles))
        totals = lax.fori_loop(0, BLOCK // 16, step, start, unroll=4)
        if not last:
            for j in range(3 * tiles):
                out[base + j] = totals[j]
            continue
        total = [0.25 * jnp.sum(value, axis=0, keepdims=True) for value in totals]
        for j in range(tiles):
            out[2 * plane, 2 * j : 2 * j + 1] = pltpu.roll(total[j], 127, 1)
            out[2 * plane, 2 * j + 1 : 2 * j + 2] = total[tiles + j]
            out[2 * plane + 1, 2 * j : 2 * j + 1] = total[2 * tiles + j]
            out[2 * plane + 1, 2 * j + 1 : 2 * j + 2] = nothing


def gradient_sums(place, field, before, entries, shape, window, last):
    arrays = [entry[0] for entry in entries]
    parts = [entry[1:] for entry in entries]
    tiles = field.shape[0] // 3
    covered = max(window, BLOCK + shape[3] * shape[4])
    size = (4, 2 * tiles, 128) if last else before.shape
    return pl.pallas_call(
        lambda *refs: gradient_kernel(shape, parts, last, *refs),
        out_shape=jax.ShapeDtypeStruct(size, jnp.float32),
        in_specs=[SMEM, VMEM, VMEM] + [VMEM] * len(arrays),
        out_specs=VMEM,
        scratch_shapes=[
            pltpu.VMEM((covered, BLOCK), jnp.bfloat16),
            pltpu.VMEM((BLOCK, window), jnp.bfloat16),
            pltpu.VMEM((3 * tiles, BLOCK, 128), jnp.float32),
        ],
        compiler_params=pltpu.CompilerParams(vmem_limit_bytes=16 << 20),
        cost_estimate=pl.CostEstimate(
            flops=2 * BLOCK * window * 3 * tiles * 128, bytes_accessed=8 << 20, transcendentals=0
        ),
        name="gradient_sums",
    )(place, field, before, *arrays)


def rotations(value, axis):
    size = lax.axis_size(axis)
    return [
        lax.ppermute(value, axis, [(i, (i + k) % size) for i in range(size)]) for k in range(1, size)
    ]


def local(potentials, quadrupoles, residuals, cell_weight):
    count = potentials.shape[0]
    row, mem = lax.axis_index("row"), lax.axis_index("mem")
    pair, par = lax.axis_index("pair"), lax.axis_index("par")
    members, pairs = lax.axis_size("mem"), lax.axis_size("pair")
    electrodes = 2 * members * count
    rows = electrodes // BLOCK // members
    window = electrodes // 2 + BLOCK
    share = 4 * pairs // rows
    folded = -(-(window - 2 * BLOCK) // (16 * share)) * 16
    shared = 2 * BLOCK // share
    shape = (electrodes, rows, pairs, share, folded, shared)
    place = jnp.stack([row, mem, pair, par]).astype(jnp.int32)

    planes = jnp.transpose(potentials, (1, 2, 0, 3))
    even, odd = planes[:, 0::2], planes[:, ::-1][:, 0::2]
    mine = jnp.where(row == 0, even, odd)
    theirs = jnp.where(row == 0, odd, even)
    native, native_out = (jnp.where(par == 0, a[0], a[1]) for a in (mine, theirs))
    other, other_out = (jnp.where(par == 0, a[1], a[0]) for a in (mine, theirs))
    tiles = native.shape[0]
    swap = [(0, 1), (1, 0)]
    ahead = [(2 * i, 2 * i - 2) for i in range(1, pairs)] + [(2 * i + 1, 2 * i + 3) for i in range(pairs - 1)]
    ahead_across = [(2 * pairs * r + a, 2 * pairs * (1 - r) + b) for r in range(2) for a, b in ahead]
    first = [
        lax.ppermute(other_out, "par", swap),
        lax.ppermute(native_out, "row", swap),
        lax.ppermute(native_out, ("row", "pair", "par"), ahead_across),
        lax.ppermute(native, ("pair", "par"), ahead),
    ]
    piece = coupling_piece(place, quadrupoles, residuals.reshape(1, -1), shape)
    turns = rotations(piece, "pair")
    (relay, across, halo_across, halo), other, _ = lax.optimization_barrier((first, other, piece))
    second_across = lax.ppermute(relay, "row", swap)
    second = lax.ppermute(other, "par", swap)
    moved = native, across, second, second_across, halo, halo_across, turns
    *held, turns = lax.optimization_barrier(moved)

    column = jnp.stack([piece] + turns)
    by_row = lax.ppermute(column, "row", swap)
    by_par = lax.ppermute(column, "par", swap)
    pieces = []
    for array in held:
        pieces += [array] + rotations(array, "mem")
    field = assemble(place, pieces, (0, 1, 0, 1, 0, 1), rows, electrodes)

    sums = jnp.zeros((6 * tiles, 8, 128), jnp.float32)
    half = BLOCK // 2
    near = [(column, 0, 0, 0)]
    staged = rows == 4
    if staged:
        sums = gradient_sums(place, field, sums, near, shape, window, False)
        by_row, by_par, sums = lax.optimization_barrier((by_row, by_par, sums))
    corner = [
        lax.ppermute(by_row[..., :half], "par", swap),
        lax.ppermute(by_par[..., half:], "row", swap),
    ]
    beside = [[(by_row, 1, 0, 0)], [(by_par, 0, 1, 0)]]
    if staged:
        for part in beside:
            sums = gradient_sums(place, field, sums, part, shape, window, False)
        corner, sums = lax.optimization_barrier((corner, sums))
    far = [(corner[0], 1, 1, 0), (corner[1], 1, 1, half)]
    part = far if staged else near + beside[0] + beside[1] + far
    sums = gradient_sums(place, field, sums, part, shape, window, True)

    sums = jnp.where(par == 0, sums, sums[::-1])
    sums = jnp.where(row == 0, sums, sums[:, ::-1])
    kept = jnp.where(par == 0, sums[:2], sums[2:])
    given = jnp.where(par == 0, sums[2:], sums[:2])
    total = kept + lax.ppermute(kept, "row", swap) + lax.ppermute(given, "par", swap)
    total = total + lax.ppermute(given, ("row", "par"), [(0, 3), (1, 2), (2, 1), (3, 0)])
    for turn in rotations(total, "mem"):
        total = total + turn
    return total * cell_weight


def solution(mesh):
    elec, space = mesh.devices.shape
    names = ("row", "mem", "pair", "par")
    finer = Mesh(mesh.devices.reshape(2, elec // 2, space // 2, 2), names)
    e, s = names[:2], names[2:]
    placed = (P(e, s, None, None), P(), P(), P(s, None, None))
    return jax.shard_map(local, mesh=finer, in_specs=placed, out_specs=P(s, None, None), check_vma=False)
```

time: 101 us -> 91.2 us (0.903); the launches traced: 101 us -> 89.9 us
  Pallas kernels: 41.6 us -> 29.3 us
  waiting for transfers between devices: 23.7 us -> 27.4 us
  starting transfers between devices: 29.9 us -> 28.1 us
    ppermute x1, waiting for transfers between devices: 0.01 us -> 8.33 us  [local(): by_row = lax.ppermute(column, 'row', swap)]
    pallas_call x4, Pallas kernels: 18.5 us -> 11.6 us  [gradient_sums(): pl.pallas_call(lambda *refs: gradient_kernel(shape, parts, last, *refs),...]
    pallas_call x2 -> x1, Pallas kernels: 22.1 us -> 16.8 us  [coupling_piece(): pl.pallas_call(lambda *refs: coupling_kernel(shape, *refs), out_shape=jax...]
    ppermute x8 -> x7, waiting for transfers between devices: 10.7 us -> 5.6 us  [the longest x1 2.46 us: local(): lax.ppermute(given, ('row', 'par'), [(0, 3), (1, 2), (2, 1), (3, 0)])]
    ppermute x13 -> x10, waiting for transfers between devices: 10.1 us -> 12.2 us  [rotations(): lax.ppermute(value, axis, [(i, (i + k) % size) for i in range(size)])]
    ppermute x1, waiting for transfers between devices: 2.81 us -> 1.05 us  [local(): lax.ppermute(native, ('pair', 'par'), ahead)]
    ppermute x13 -> x10, starting transfers between devices: 9.1 us -> 7.47 us  [rotations(): lax.ppermute(value, axis, [(i, (i + k) % size) for i in range(size)])]
    ppermute x1, starting transfers between devices: 1.74 us -> 0.64 us  [local(): by_par = lax.ppermute(column, 'par', swap)]
  transfers between devices with their start and end apart: 27 -> 23, of which waited for: 15 -> 16; matrix products, arithmetic and copies ran while one was open for 1% -> 0% of each run, Pallas kernels for 36% -> 29%
where the time goes in v2:
time: 91.2 us; the launch traced here: 89.9 us
  Pallas kernels  29.3 us (32%)
  starting transfers between devices  28.1 us (31%)
  waiting for transfers between devices  27.4 us (30%)
  other arithmetic  2.46 us (3%)
  local copies, waits for them, and re-layouts  2.35 us (3%)
    pallas_call x1, Pallas kernels, coupling_piece(): pl.pallas_call(lambda *refs: coupling_kernel(shape, *refs), out_shape=jax...  16.8 us
    ppermute x10, waiting for transfers between devices, rotations(): lax.ppermute(value, axis, [(i, (i + k) % size) for i in range(size)])  12.2 us
    pallas_call x4, Pallas kernels, gradient_sums(): pl.pallas_call(lambda *refs: gradient_kernel(shape, parts, last, *refs),...  11.6 us
    ppermute x1, waiting for transfers between devices, local(): by_row = lax.ppermute(column, 'row', swap)  8.33 us
    ppermute x10, starting transfers between devices, rotations(): lax.ppermute(value, axis, [(i, (i + k) % size) for i in range(size)])  7.47 us
    ppermute x1, starting transfers between devices, local(): lax.ppermute(other_out, 'par', swap)  5.97 us
    ppermute x1, starting transfers between devices, local(): lax.ppermute(native_out, 'row', swap)  2.94 us
    ppermute x1, waiting for transfers between devices, local(): lax.ppermute(given, ('row', 'par'), [(0, 3), (1, 2), (2, 1), (3, 0)])  2.46 us
  transfers between devices with their start and end apart: 23, of which 16 were waited for; matrix products, arithmetic and copies ran while one was open for 0% of the time, Pallas kernels for 29%

profile of v2, /device:TPU:0, one launch (start us, length us, event | category | flops | bytes accessed | tf_op | source)
XLA Modules:
  0.0 89.9 jit_solution(17167008721897175465)
XLA Ops:
  0.0 2.1 %copy.7 = bf16[512,2,8,128]{3,0,2,1:T(8,128)(2,1)S(1)} copy(bf16[512,2,8,128]{3,2,1,0:T(8,128)(2,1)} %param.4) | data formatting | bytes 4194304 | tf_op args[0]
  2.1 0.1 slice.40
  2.2 0.5 broadcast_select_fusion
  2.8 0.0 copy-start
  2.8 0.0 copy-start.1
  2.8 1.1 %select_bitcast_fusion.1 = (bf16[4,512,128]{2,1,0:T(8,128)(2,1)}, bf16[4,512,128]{2,1,0:T(8,128)(2,1)}) fusion(pred[]{:T(512)S(6)} %eq.4, bf16[2,4,512,128]{3,2,1,0:T(8,128)(2,1)S(1)} %get-tuple-element.45), kind=kLoop, calls=%fused_computation.5 | loop fusion | flops 524288 | bytes 2097153 | tf_op jit(solution)/shard_map/jit(_where)/select_n | solution.py:242
  3.9 2.9 %collective-permute-start.1 = (bf16[4,512,128]{2,1,0:T(8,128)(2,1)}, bf16[4,512,128]{2,1,0:T(8,128)(2,1)S(1)}, u32[]{:S(2)}, u32[]{:S(2)}) collective-permute-start(bf16[4,512,128]{2,1,0:T(8,128)(2,1)} %get-tuple-element.49), channel_id=1, source_target_pairs={{0,16},{16,0},{1,17},{17,1},{2,18},{18,2},{3,19},{19,3},{4,20},{20... | collective-permute-start | bytes 1572872 | tf_op jit(solution)/shard_map/ppermute | solution.py:250
  6.8 1.3 %collective-permute-start.2 = (bf16[4,512,128]{2,1,0:T(8,128)(2,1)}, bf16[4,512,128]{2,1,0:T(8,128)(2,1)S(1)}, u32[]{:S(2)}, u32[]{:S(2)}) collective-permute-start(bf16[4,512,128]{2,1,0:T(8,128)(2,1)} %get-tuple-element.49), channel_id=1, source_target_pairs={{2,16},{4,18},{6,20},{1,19},{3,21},{5,23},{18,0},{20,2},{22,4},{17... | collective-permute-start | bytes 1572872 | tf_op jit(solution)/shard_map/ppermute | solution.py:251
  8.1 0.1 select_bitcast_fusion
  8.2 1.3 %collective-permute-start.3 = (bf16[4,512,128]{2,1,0:T(8,128)(2,1)S(1)}, bf16[4,512,128]{2,1,0:T(8,128)(2,1)S(1)}, u32[]{:S(2)}, u32[]{:S(2)}) collective-permute-start(bf16[4,512,128]{2,1,0:T(8,128)(2,1)S(1)} %get-tuple-element.30.refs_1_), channel_id=1, source_target_pairs={{2,0},{4,2},{6,4},{1,3},{3,5},{5,7},{10,8},{12,10},{14,12},{9,11},... | collective-permute-start | bytes 1572872 | tf_op jit(solution)/shard_map/ppermute | solution.py:252
  9.5 6.0 %collective-permute-start = (bf16[4,512,128]{2,1,0:T(8,128)(2,1)}, bf16[4,512,128]{2,1,0:T(8,128)(2,1)}, u32[]{:S(2)}, u32[]{:S(2)}) collective-permute-start(bf16[4,512,128]{2,1,0:T(8,128)(2,1)} %get-tuple-element.50), channel_id=1, source_target_pairs={{0,1},{1,0},{2,3},{3,2},{4,5},{5,4},{6,7},{7,6},{8,9},{9,8},{10,11... | collective-permute-start | bytes 1572872 | tf_op jit(solution)/shard_map/ppermute | solution.py:249
  15.4 0.1 pad_add_fusion.refs_0_
  15.5 16.8 %coupling_piece.1 = bf16[320,256]{1,0:T(8,128)(2,1)S(1)} custom-call(s32[4]{0:T(128)S(1)} %pad_add_fusion.refs_0_, s32[4,32768]{1,0:T(4,128)S(1)} %copy-done, f32[1,32768]{1,0:T(1,128)S(1)} %bitcast.21), custom_call_target="tpu_custom_call" | custom-call | flops 8589934592 | bytes 1048576 | tf_op jit(solution)/shard_map/coupling_piece/pallas_call | solution.py:85
  32.3 0.0 collective-permute-done.2.refs_11_
  32.3 1.1 %collective-permute-done.3.refs_9_ = bf16[4,512,128]{2,1,0:T(8,128)(2,1)S(1)} collective-permute-done((bf16[4,512,128]{2,1,0:T(8,128)(2,1)S(1)}, bf16[4,512,128]{2,1,0:T(8,128)(2,1)S(1)}, u32[]{:S(2)}, u32[]{:S(2)}) %collective-permute-start.3) | collective-permute-done | bytes 524320 | tf_op jit(solution)/shard_map/ppermute | solution.py:252
  33.4 0.0 collective-permute-done
  33.4 0.7 collective-permute-start.4
  34.1 1.5 %collective-permute-start.5 = (bf16[4,512,128]{2,1,0:T(8,128)(2,1)}, bf16[4,512,128]{2,1,0:T(8,128)(2,1)S(1)}, u32[]{:S(2)}, u32[]{:S(2)}) collective-permute-start(bf16[4,512,128]{2,1,0:T(8,128)(2,1)} %collective-permute-done), channel_id=1, source_target_pairs={{0,16},{16,0},{1,17},{17,1},{2,18},{18,2},{3,19},{19,3},{4,20},{20... | collective-permute-start | bytes 1572872 | tf_op jit(solution)/shard_map/ppermute | solution.py:257
  35.6 2.5 %collective-permute-start.6 = (bf16[320,256]{1,0:T(8,128)(2,1)S(1)}, bf16[320,256]{1,0:T(8,128)(2,1)S(1)}, u32[]{:S(2)}, u32[]{:S(2)}) collective-permute-start(bf16[320,256]{1,0:T(8,128)(2,1)S(1)} %coupling_piece.1), channel_id=1, source_target_pairs={{0,2},{2,4},{4,6},{6,0},{1,3},{3,5},{5,7},{7,1},{8,10},{10,12},{12... | collective-permute-start | bytes 491528 | tf_op jit(solution)/shard_map/ppermute | solution.py:220
  38.1 2.6 %collective-permute-start.7 = (bf16[320,256]{1,0:T(8,128)(2,1)S(1)}, bf16[320,256]{1,0:T(8,128)(2,1)S(1)}, u32[]{:S(2)}, u32[]{:S(2)}) collective-permute-start(bf16[320,256]{1,0:T(8,128)(2,1)S(1)} %coupling_piece.1), channel_id=1, source_target_pairs={{0,4},{2,6},{4,0},{6,2},{1,5},{3,7},{5,1},{7,3},{8,12},{10,14},{12... | collective-permute-start | bytes 491528 | tf_op jit(solution)/shard_map/ppermute | solution.py:220
  40.7 1.3 %collective-permute-start.8 = (bf16[320,256]{1,0:T(8,128)(2,1)S(1)}, bf16[320,256]{1,0:T(8,128)(2,1)S(1)}, u32[]{:S(2)}, u32[]{:S(2)}) collective-permute-start(bf16[320,256]{1,0:T(8,128)(2,1)S(1)} %coupling_piece.1), channel_id=1, source_target_pairs={{0,6},{2,0},{4,2},{6,4},{1,7},{3,1},{5,3},{7,5},{8,14},{10,8},{12,... | collective-permute-start | bytes 491528 | tf_op jit(solution)/shard_map/ppermute | solution.py:220
  42.0 3.3 %collective-permute-done.6 = bf16[320,256]{1,0:T(8,128)(2,1)S(1)} collective-permute-done((bf16[320,256]{1,0:T(8,128)(2,1)S(1)}, bf16[320,256]{1,0:T(8,128)(2,1)S(1)}, u32[]{:S(2)}, u32[]{:S(2)}) %collective-permute-start.6) | collective-permute-done | bytes 163872 | tf_op jit(solution)/shard_map/ppermute | solution.py:220
  45.3 4.4 %collective-permute-done.7 = bf16[320,256]{1,0:T(8,128)(2,1)S(1)} collective-permute-done((bf16[320,256]{1,0:T(8,128)(2,1)S(1)}, bf16[320,256]{1,0:T(8,128)(2,1)S(1)}, u32[]{:S(2)}, u32[]{:S(2)}) %collective-permute-start.7) | collective-permute-done | bytes 163872 | tf_op jit(solution)/shard_map/ppermute | solution.py:220
  49.7 0.0 collective-permute-done.8
  49.7 0.0 collective-permute-done.4.refs_5_
  49.7 0.0 collective-permute-done.5.refs_7_
  49.8 0.1 collective-permute-start.10
  49.8 0.5 collective-permute-start.11
  50.3 0.1 collective-permute-start.12
  50.4 0.1 pad_maximum_fusion.refs_3_
  50.5 0.6 collective-permute-start.15
  51.1 0.6 collective-permute-start.16
  51.7 0.0 collective-permute-done.10.refs_4_
  51.7 0.1 collective-permute-start.13
  51.9 0.6 collective-permute-done.11.refs_6_
  52.5 0.1 collective-permute-start.14
  52.6 0.6 collective-permute-done.12.refs_8_
  53.2 0.1 collective-permute-start.9
  53.4 0.6 collective-permute-done.13.refs_10_
  54.0 0.7 collective-permute-done.14.refs_12_
  54.7 0.7 collective-permute-done.9.refs_2_
  55.5 1.0 %assemble_fields.1.refs_1_ = bf16[12,2048,128]{2,1,0:T(8,128)(2,1)S(1)} custom-call(s32[4]{0:T(128)S(1)} %pad_add_fusion.refs_0_, bf16[4,512,128]{2,1,0:T(8,128)(2,1)S(1)} %get-tuple-element.30.refs_1_, bf16[4,512,128]{2,1,0:T(8,128)(2,1)S(1)} %collective-permute-done.9.refs_2_, bf16[4,512,128]{2,1,0:T(8,128)(2,1)S(1)} %collective-permute-done.1.refs_3_, ...), custom_call_target="tpu_custom_call" | custom-call | bytes 4194304 | tf_op jit(solution)/shard_map/assemble_fields/pallas_call | solution.py:118
  56.5 2.8 %gradient_sums.4.refs_2_ = f32[24,8,128]{2,1,0:T(8,128)S(1)} custom-call(s32[4]{0:T(128)S(1)} %pad_add_fusion.refs_0_, bf16[12,2048,128]{2,1,0:T(8,128)(2,1)S(1)} %assemble_fields.1.refs_1_, f32[24,8,128]{2,1,0:T(8,128)S(1)} %broadcast_in_dim.3.refs_2_, bf16[4,320,256]{2,1,0:T(8,128)(2,1)S(1)} %pad_maximum_fusion.refs_3_), custom_call_target="tpu_custom_call" | custom-call | flops 1006632960 | bytes 8388608 | tf_op jit(solution)/shard_map/gradient_sums/pallas_call | solution.py:199
  59.3 8.3 %collective-permute-done.15.refs_3_ = bf16[4,320,256]{2,1,0:T(8,128)(2,1)S(1)} collective-permute-done((bf16[4,320,256]{2,1,0:T(8,128)(2,1)S(1)}, bf16[4,320,256]{2,1,0:T(8,128)(2,1)S(1)}, u32[]{:S(2)}, u32[]{:S(2)}) %collective-permute-start.15) | collective-permute-done | bytes 655392 | tf_op jit(solution)/shard_map/ppermute | solution.py:263
  67.6 0.3 collective-permute-done.16.refs_3_
  67.9 0.1 slice.46
  68.0 0.7 collective-permute-start.17
  68.7 0.1 slice.47
  68.7 1.4 %collective-permute-start.18 = (bf16[4,320,128]{2,1,0:T(8,128)(2,1)S(1)}, bf16[4,320,128]{2,1,0:T(8,128)(2,1)S(1)}, u32[]{:S(2)}, u32[]{:S(2)}) collective-permute-start(bf16[4,320,128]{2,1,0:T(8,128)(2,1)S(1)} %slice.47), channel_id=1, source_target_pairs={{0,16},{16,0},{1,17},{17,1},{2,18},{18,2},{3,19},{19,3},{4,20},{20... | collective-permute-start | bytes 983048 | tf_op jit(solution)/shard_map/ppermute | solution.py:279
  70.1 2.8 %gradient_sums.5.refs_2_ = f32[24,8,128]{2,1,0:T(8,128)S(1)} custom-call(s32[4]{0:T(128)S(1)} %pad_add_fusion.refs_0_, bf16[12,2048,128]{2,1,0:T(8,128)(2,1)S(1)} %assemble_fields.1.refs_1_, f32[24,8,128]{2,1,0:T(8,128)S(1)} %gradient_sums.4.refs_2_, bf16[4,320,256]{2,1,0:T(8,128)(2,1)S(1)} %collective-permute-done.15.refs_3_), custom_call_target="tpu_custom_call" | custom-call | flops 1006632960 | bytes 8388608 | tf_op jit(solution)/shard_map/gradient_sums/pallas_call | solution.py:199
  73.0 2.8 %gradient_sums.6.refs_2_ = f32[24,8,128]{2,1,0:T(8,128)S(1)} custom-call(s32[4]{0:T(128)S(1)} %pad_add_fusion.refs_0_, bf16[12,2048,128]{2,1,0:T(8,128)(2,1)S(1)} %assemble_fields.1.refs_1_, f32[24,8,128]{2,1,0:T(8,128)S(1)} %gradient_sums.5.refs_2_, bf16[4,320,256]{2,1,0:T(8,128)(2,1)S(1)} %collective-permute-done.16.refs_3_), custom_call_target="tpu_custom_call" | custom-call | flops 1006632960 | bytes 8388608 | tf_op jit(solution)/shard_map/gradient_sums/pallas_call | solution.py:199
  75.8 0.0 copy-start.2
  75.8 1.2 %collective-permute-done.17.refs_3_ = bf16[4,320,128]{2,1,0:T(8,128)(2,1)S(1)} collective-permute-done((bf16[4,320,128]{2,1,0:T(8,128)(2,1)S(1)}, bf16[4,320,128]{2,1,0:T(8,128)(2,1)S(1)}, u32[]{:S(2)}, u32[]{:S(2)}) %collective-permute-start.17) | collective-permute-done | bytes 327712 | tf_op jit(solution)/shard_map/ppermute | solution.py:278
  77.1 0.4 collective-permute-done.18.refs_4_
  77.5 3.1 %gradient_sums.7 = f32[4,8,128]{2,1,0:T(8,128)S(1)} custom-call(s32[4]{0:T(128)S(1)} %pad_add_fusion.refs_0_, bf16[12,2048,128]{2,1,0:T(8,128)(2,1)S(1)} %assemble_fields.1.refs_1_, f32[24,8,128]{2,1,0:T(8,128)S(1)} %gradient_sums.6.refs_2_, bf16[4,320,128]{2,1,0:T(8,128)(2,1)S(1)} %collective-permute-done.17.refs_3_, ...), custom_call_target="tpu_custom_call" | custom-call | flops 1006632960 | bytes 8388608 | tf_op jit(solution)/shard_map/gradient_sums/pallas_call | solution.py:199
  80.6 1.4 %collective-permute-start.19 = (f32[2,8,128]{2,1,0:T(8,128)S(1)}, f32[2,8,128]{2,1,0:T(8,128)S(1)}, u32[]{:S(2)}, u32[]{:S(2)}) collective-permute-start(f32[2,8,128]{2,1,0:T(8,128)S(1)} %get-tuple-element.51), channel_id=1, source_target_pairs={{0,16},{16,0},{1,17},{17,1},{2,18},{18,2},{3,19},{19,3},{4,20},{20... | collective-permute-start | bytes 24584 | tf_op jit(solution)/shard_map/ppermute | solution.py:294
  82.0 1.6 %collective-permute-start.20 = (f32[2,8,128]{2,1,0:T(8,128)S(1)}, f32[2,8,128]{2,1,0:T(8,128)S(1)}, u32[]{:S(2)}, u32[]{:S(2)}) collective-permute-start(f32[2,8,128]{2,1,0:T(8,128)S(1)} %get-tuple-element.52), channel_id=1, source_target_pairs={{0,1},{1,0},{2,3},{3,2},{4,5},{5,4},{6,7},{7,6},{8,9},{9,8},{10,11... | collective-permute-start | bytes 24584 | tf_op jit(solution)/shard_map/ppermute | solution.py:294
  83.5 0.6 collective-permute-start.21
  84.1 0.2 collective-permute-done.19
  84.3 1.3 %collective-permute-done.20 = f32[2,8,128]{2,1,0:T(8,128)S(1)} collective-permute-done((f32[2,8,128]{2,1,0:T(8,128)S(1)}, f32[2,8,128]{2,1,0:T(8,128)S(1)}, u32[]{:S(2)}, u32[]{:S(2)}) %collective-permute-start.20) | collective-permute-done | bytes 8224 | tf_op jit(solution)/shard_map/ppermute | solution.py:294
  85.6 2.5 %collective-permute-done.21 = f32[2,8,128]{2,1,0:T(8,128)S(1)} collective-permute-done((f32[2,8,128]{2,1,0:T(8,128)S(1)}, f32[2,8,128]{2,1,0:T(8,128)S(1)}, u32[]{:S(2)}, u32[]{:S(2)}) %collective-permute-start.21) | collective-permute-done | bytes 8224 | tf_op jit(solution)/shard_map/ppermute | solution.py:295
  88.1 0.0 collective-permute-start.22
  88.1 1.2 %collective-permute-done.22 = f32[2,8,128]{2,1,0:T(8,128)S(1)} collective-permute-done((f32[2,8,128]{2,1,0:T(8,128)S(1)}, f32[2,8,128]{2,1,0:T(8,128)S(1)}, u32[]{:S(2)}, u32[]{:S(2)}) %collective-permute-start.22) | collective-permute-done | bytes 8224 | tf_op jit(solution)/shard_map/ppermute | solution.py:220
  89.3 0.6 add_multiply_fusion
  (10 shorter events, 0.1 us)
Async XLA Ops:
  2.8 12.7 %copy-start = (s32[4,32768]{1,0:T(4,128)S(1)}, s32[4,32768]{1,0:T(4,128)}, u32[]{:S(2)}) copy-start(s32[4,32768]{1,0:T(4,128)} %refs_1_.1) | copy-start | bytes 1572868
  2.8 12.7 %copy-start.1 = (f32[32768]{0:T(1024)S(1)}, f32[32768]{0:T(1024)}, u32[]{:S(2)}) copy-start(f32[32768]{0:T(1024)} %param.6) | copy-start | bytes 393220
  3.9 28.5 %collective-permute-start.1 = (bf16[4,512,128]{2,1,0:T(8,128)(2,1)}, bf16[4,512,128]{2,1,0:T(8,128)(2,1)S(1)}, u32[]{:S(2)}, u32[]{:S(2)}) collective-permute-start(bf16[4,512,128]{2,1,0:T(8,128)(2,1)} %get-tuple-element.49), channel_id=1, source_target_pairs={{0,16},{16,0},{1,17},{17,1},{2,18},{18,2},{3,19},{19,3},{4,20},{20... | collective-permute-start | bytes 1572872 | tf_op jit(solution)/shard_map/ppermute | solution.py:250
  6.8 25.5 %collective-permute-start.2 = (bf16[4,512,128]{2,1,0:T(8,128)(2,1)}, bf16[4,512,128]{2,1,0:T(8,128)(2,1)S(1)}, u32[]{:S(2)}, u32[]{:S(2)}) collective-permute-start(bf16[4,512,128]{2,1,0:T(8,128)(2,1)} %get-tuple-element.49), channel_id=1, source_target_pairs={{2,16},{4,18},{6,20},{1,19},{3,21},{5,23},{18,0},{20,2},{22,4},{17... | collective-permute-start | bytes 1572872 | tf_op jit(solution)/shard_map/ppermute | solution.py:251
  8.2 25.2 %collective-permute-start.3 = (bf16[4,512,128]{2,1,0:T(8,128)(2,1)S(1)}, bf16[4,512,128]{2,1,0:T(8,128)(2,1)S(1)}, u32[]{:S(2)}, u32[]{:S(2)}) collective-permute-start(bf16[4,512,128]{2,1,0:T(8,128)(2,1)S(1)} %get-tuple-element.30.refs_1_), channel_id=1, source_target_pairs={{2,0},{4,2},{6,4},{1,3},{3,5},{5,7},{10,8},{12,10},{14,12},{9,11},... | collective-permute-start | bytes 1572872 | tf_op jit(solution)/shard_map/ppermute | solution.py:252
  9.5 23.9 %collective-permute-start = (bf16[4,512,128]{2,1,0:T(8,128)(2,1)}, bf16[4,512,128]{2,1,0:T(8,128)(2,1)}, u32[]{:S(2)}, u32[]{:S(2)}) collective-permute-start(bf16[4,512,128]{2,1,0:T(8,128)(2,1)} %get-tuple-element.50), channel_id=1, source_target_pairs={{0,1},{1,0},{2,3},{3,2},{4,5},{5,4},{6,7},{7,6},{8,9},{9,8},{10,11... | collective-permute-start | bytes 1572872 | tf_op jit(solution)/shard_map/ppermute | solution.py:249
  33.4 16.4 %collective-permute-start.4 = (bf16[4,512,128]{2,1,0:T(8,128)(2,1)S(1)}, bf16[4,512,128]{2,1,0:T(8,128)(2,1)S(1)}, u32[]{:S(2)}, u32[]{:S(2)}) collective-permute-start(bf16[4,512,128]{2,1,0:T(8,128)(2,1)S(1)} %get-tuple-element.26), channel_id=1, source_target_pairs={{0,1},{1,0},{2,3},{3,2},{4,5},{5,4},{6,7},{7,6},{8,9},{9,8},{10,11... | collective-permute-start | bytes 1572872 | tf_op jit(solution)/shard_map/ppermute | solution.py:258
  34.1 15.6 %collective-permute-start.5 = (bf16[4,512,128]{2,1,0:T(8,128)(2,1)}, bf16[4,512,128]{2,1,0:T(8,128)(2,1)S(1)}, u32[]{:S(2)}, u32[]{:S(2)}) collective-permute-start(bf16[4,512,128]{2,1,0:T(8,128)(2,1)} %collective-permute-done), channel_id=1, source_target_pairs={{0,16},{16,0},{1,17},{17,1},{2,18},{18,2},{3,19},{19,3},{4,20},{20... | collective-permute-start | bytes 1572872 | tf_op jit(solution)/shard_map/ppermute | solution.py:257
  35.6 9.7 %collective-permute-start.6 = (bf16[320,256]{1,0:T(8,128)(2,1)S(1)}, bf16[320,256]{1,0:T(8,128)(2,1)S(1)}, u32[]{:S(2)}, u32[]{:S(2)}) collective-permute-start(bf16[320,256]{1,0:T(8,128)(2,1)S(1)} %coupling_piece.1), channel_id=1, source_target_pairs={{0,2},{2,4},{4,6},{6,0},{1,3},{3,5},{5,7},{7,1},{8,10},{10,12},{12... | collective-permute-start | bytes 491528 | tf_op jit(solution)/shard_map/ppermute | solution.py:220
  38.1 11.6 %collective-permute-start.7 = (bf16[320,256]{1,0:T(8,128)(2,1)S(1)}, bf16[320,256]{1,0:T(8,128)(2,1)S(1)}, u32[]{:S(2)}, u32[]{:S(2)}) collective-permute-start(bf16[320,256]{1,0:T(8,128)(2,1)S(1)} %coupling_piece.1), channel_id=1, source_target_pairs={{0,4},{2,6},{4,0},{6,2},{1,5},{3,7},{5,1},{7,3},{8,12},{10,14},{12... | collective-permute-start | bytes 491528 | tf_op jit(solution)/shard_map/ppermute | solution.py:220
  40.7 9.0 %collective-permute-start.8 = (bf16[320,256]{1,0:T(8,128)(2,1)S(1)}, bf16[320,256]{1,0:T(8,128)(2,1)S(1)}, u32[]{:S(2)}, u32[]{:S(2)}) collective-permute-start(bf16[320,256]{1,0:T(8,128)(2,1)S(1)} %coupling_piece.1), channel_id=1, source_target_pairs={{0,6},{2,0},{4,2},{6,4},{1,7},{3,1},{5,3},{7,5},{8,14},{10,8},{12,... | collective-permute-start | bytes 491528 | tf_op jit(solution)/shard_map/ppermute | solution.py:220
  49.8 2.0 %collective-permute-start.10 = (bf16[4,512,128]{2,1,0:T(8,128)(2,1)S(1)}, bf16[4,512,128]{2,1,0:T(8,128)(2,1)S(1)}, u32[]{:S(2)}, u32[]{:S(2)}) collective-permute-start(bf16[4,512,128]{2,1,0:T(8,128)(2,1)S(1)} %collective-permute-done.1.refs_3_), channel_id=1, source_target_pairs={{0,8},{8,0},{1,9},{9,1},{2,10},{10,2},{3,11},{11,3},{4,12},{12,4},... | collective-permute-start | bytes 1572872 | tf_op jit(solution)/shard_map/ppermute | solution.py:220
  49.8 2.6 %collective-permute-start.11 = (bf16[4,512,128]{2,1,0:T(8,128)(2,1)S(1)}, bf16[4,512,128]{2,1,0:T(8,128)(2,1)S(1)}, u32[]{:S(2)}, u32[]{:S(2)}) collective-permute-start(bf16[4,512,128]{2,1,0:T(8,128)(2,1)S(1)} %collective-permute-done.4.refs_5_), channel_id=1, source_target_pairs={{0,8},{8,0},{1,9},{9,1},{2,10},{10,2},{3,11},{11,3},{4,12},{12,4},... | collective-permute-start | bytes 1572872 | tf_op jit(solution)/shard_map/ppermute | solution.py:220
  50.3 2.9 %collective-permute-start.12 = (bf16[4,512,128]{2,1,0:T(8,128)(2,1)S(1)}, bf16[4,512,128]{2,1,0:T(8,128)(2,1)S(1)}, u32[]{:S(2)}, u32[]{:S(2)}) collective-permute-start(bf16[4,512,128]{2,1,0:T(8,128)(2,1)S(1)} %collective-permute-done.5.refs_7_), channel_id=1, source_target_pairs={{0,8},{8,0},{1,9},{9,1},{2,10},{10,2},{3,11},{11,3},{4,12},{12,4},... | collective-permute-start | bytes 1572872 | tf_op jit(solution)/shard_map/ppermute | solution.py:220
  50.5 17.1 %collective-permute-start.15 = (bf16[4,320,256]{2,1,0:T(8,128)(2,1)S(1)}, bf16[4,320,256]{2,1,0:T(8,128)(2,1)S(1)}, u32[]{:S(2)}, u32[]{:S(2)}) collective-permute-start(bf16[4,320,256]{2,1,0:T(8,128)(2,1)S(1)} %pad_maximum_fusion.refs_3_), channel_id=1, source_target_pairs={{0,16},{16,0},{1,17},{17,1},{2,18},{18,2},{3,19},{19,3},{4,20},{20... | collective-permute-start | bytes 1966088 | tf_op jit(solution)/shard_map/ppermute | solution.py:263
  51.1 16.8 %collective-permute-start.16 = (bf16[4,320,256]{2,1,0:T(8,128)(2,1)S(1)}, bf16[4,320,256]{2,1,0:T(8,128)(2,1)S(1)}, u32[]{:S(2)}, u32[]{:S(2)}) collective-permute-start(bf16[4,320,256]{2,1,0:T(8,128)(2,1)S(1)} %pad_maximum_fusion.refs_3_), channel_id=1, source_target_pairs={{0,1},{1,0},{2,3},{3,2},{4,5},{5,4},{6,7},{7,6},{8,9},{9,8},{10,11... | collective-permute-start | bytes 1966088 | tf_op jit(solution)/shard_map/ppermute | solution.py:264
  51.7 2.2 %collective-permute-start.13 = (bf16[4,512,128]{2,1,0:T(8,128)(2,1)S(1)}, bf16[4,512,128]{2,1,0:T(8,128)(2,1)S(1)}, u32[]{:S(2)}, u32[]{:S(2)}) collective-permute-start(bf16[4,512,128]{2,1,0:T(8,128)(2,1)S(1)} %collective-permute-done.3.refs_9_), channel_id=1, source_target_pairs={{0,8},{8,0},{1,9},{9,1},{2,10},{10,2},{3,11},{11,3},{4,12},{12,4},... | collective-permute-start | bytes 1572872 | tf_op jit(solution)/shard_map/ppermute | solution.py:220
  52.5 2.2 %collective-permute-start.14 = (bf16[4,512,128]{2,1,0:T(8,128)(2,1)S(1)}, bf16[4,512,128]{2,1,0:T(8,128)(2,1)S(1)}, u32[]{:S(2)}, u32[]{:S(2)}) collective-permute-start(bf16[4,512,128]{2,1,0:T(8,128)(2,1)S(1)} %collective-permute-done.2.refs_11_), channel_id=1, source_target_pairs={{0,8},{8,0},{1,9},{9,1},{2,10},{10,2},{3,11},{11,3},{4,12},{12,4},... | collective-permute-start | bytes 1572872 | tf_op jit(solution)/shard_map/ppermute | solution.py:220
  53.2 2.2 %collective-permute-start.9 = (bf16[4,512,128]{2,1,0:T(8,128)(2,1)S(1)}, bf16[4,512,128]{2,1,0:T(8,128)(2,1)S(1)}, u32[]{:S(2)}, u32[]{:S(2)}) collective-permute-start(bf16[4,512,128]{2,1,0:T(8,128)(2,1)S(1)} %get-tuple-element.30.refs_1_), channel_id=1, source_target_pairs={{0,8},{8,0},{1,9},{9,1},{2,10},{10,2},{3,11},{11,3},{4,12},{12,4},... | collective-permute-start | bytes 1572872 | tf_op jit(solution)/shard_map/ppermute | solution.py:220
  68.0 9.1 %collective-permute-start.17 = (bf16[4,320,128]{2,1,0:T(8,128)(2,1)S(1)}, bf16[4,320,128]{2,1,0:T(8,128)(2,1)S(1)}, u32[]{:S(2)}, u32[]{:S(2)}) collective-permute-start(bf16[4,320,128]{2,1,0:T(8,128)(2,1)S(1)} %slice.46), channel_id=1, source_target_pairs={{0,1},{1,0},{2,3},{3,2},{4,5},{5,4},{6,7},{7,6},{8,9},{9,8},{10,11... | collective-permute-start | bytes 983048 | tf_op jit(solution)/shard_map/ppermute | solution.py:278
  68.7 8.7 %collective-permute-start.18 = (bf16[4,320,128]{2,1,0:T(8,128)(2,1)S(1)}, bf16[4,320,128]{2,1,0:T(8,128)(2,1)S(1)}, u32[]{:S(2)}, u32[]{:S(2)}) collective-permute-start(bf16[4,320,128]{2,1,0:T(8,128)(2,1)S(1)} %slice.47), channel_id=1, source_target_pairs={{0,16},{16,0},{1,17},{17,1},{2,18},{18,2},{3,19},{19,3},{4,20},{20... | collective-permute-start | bytes 983048 | tf_op jit(solution)/shard_map/ppermute | solution.py:279
  75.8 13.5 %copy-start.2 = (f32[2,8,128]{2,1,0:T(8,128)S(1)}, f32[2,8,128]{2,1,0:T(8,128)}, u32[]{:S(2)}) copy-start(f32[2,8,128]{2,1,0:T(8,128)} %param.7) | copy-start | bytes 24580
  80.6 3.7 %collective-permute-start.19 = (f32[2,8,128]{2,1,0:T(8,128)S(1)}, f32[2,8,128]{2,1,0:T(8,128)S(1)}, u32[]{:S(2)}, u32[]{:S(2)}) collective-permute-start(f32[2,8,128]{2,1,0:T(8,128)S(1)} %get-tuple-element.51), channel_id=1, source_target_pairs={{0,16},{16,0},{1,17},{17,1},{2,18},{18,2},{3,19},{19,3},{4,20},{20... | collective-permute-start | bytes 24584 | tf_op jit(solution)/shard_map/ppermute | solution.py:294
  82.0 3.7 %collective-permute-start.20 = (f32[2,8,128]{2,1,0:T(8,128)S(1)}, f32[2,8,128]{2,1,0:T(8,128)S(1)}, u32[]{:S(2)}, u32[]{:S(2)}) collective-permute-start(f32[2,8,128]{2,1,0:T(8,128)S(1)} %get-tuple-element.52), channel_id=1, source_target_pairs={{0,1},{1,0},{2,3},{3,2},{4,5},{5,4},{6,7},{7,6},{8,9},{9,8},{10,11... | collective-permute-start | bytes 24584 | tf_op jit(solution)/shard_map/ppermute | solution.py:294
  83.5 4.5 %collective-permute-start.21 = (f32[2,8,128]{2,1,0:T(8,128)S(1)}, f32[2,8,128]{2,1,0:T(8,128)S(1)}, u32[]{:S(2)}, u32[]{:S(2)}) collective-permute-start(f32[2,8,128]{2,1,0:T(8,128)S(1)} %get-tuple-element.52), channel_id=1, source_target_pairs={{0,17},{1,16},{16,1},{17,0},{2,19},{3,18},{18,3},{19,2},{4,21},{5,... | collective-permute-start | bytes 24584 | tf_op jit(solution)/shard_map/ppermute | solution.py:295
  88.1 1.2 %collective-permute-start.22 = (f32[2,8,128]{2,1,0:T(8,128)S(1)}, f32[2,8,128]{2,1,0:T(8,128)S(1)}, u32[]{:S(2)}, u32[]{:S(2)}) collective-permute-start(f32[2,8,128]{2,1,0:T(8,128)S(1)} %add_add_fusion), channel_id=1, source_target_pairs={{0,8},{8,0},{1,9},{9,1},{2,10},{10,2},{3,11},{11,3},{4,12},{12,4},... | collective-permute-start | bytes 24584 | tf_op jit(solution)/shard_map/ppermute | solution.py:220

commit v3 on v2

--- a/solution.py
+++ b/solution.py
@@ -6,7 +6,7 @@
 from jax.sharding import Mesh, PartitionSpec as P
 
 BLOCK = 256
-CHUNK = 1024
+CHUNK = 512
 
 
 def onehots(dest, first, rows, plus, minus, up, down):
@@ -101,23 +101,23 @@
 def assemble_kernel(rows, far, place, *refs):
     pieces, field = refs[:-1], refs[-1]
     electrodes = field.shape[1]
-    tiles, count, _ = pieces[0].shape
-    members = len(pieces) // len(far)
-    for index, piece in enumerate(pieces):
-        slot, k = index // members, index % members
-        row = 1 - place[0] if far[slot] else place[0]
+    members = len(pieces)
+    total, count, _ = pieces[0].shape
+    tiles = total // len(far)
+    for k, piece in enumerate(pieces):
         member = (place[1] + members - k) % members
-        first = (row * members + member) * count - place[1] * rows * BLOCK
-        first = pl.multiple_of((first + electrodes) % electrodes, count)
-        for tile in range(tiles):
-            field[tiles * (slot // 2) + tile, pl.ds(first, count)] = piece[tile]
+        for slot, other in enumerate(far):
+            row = 1 - place[0] if other else place[0]
+            first = (row * members + member) * count - place[1] * rows * BLOCK
+            first = pl.multiple_of((first + electrodes) % electrodes, count)
+            for tile in range(tiles):
+                field[tiles * (slot // 2) + tile, pl.ds(first, count)] = piece[tiles * slot + tile]
 
 
 def assemble(place, pieces, far, rows, electrodes):
-    tiles = pieces[0].shape[0]
     return pl.pallas_call(
         lambda *refs: assemble_kernel(rows, far, *refs),
-        out_shape=jax.ShapeDtypeStruct((tiles * (len(far) // 2), electrodes, 128), jnp.bfloat16),
+        out_shape=jax.ShapeDtypeStruct((pieces[0].shape[0] // 2, electrodes, 128), jnp.bfloat16),
         in_specs=[SMEM] + [VMEM] * len(pieces),
         out_specs=VMEM,
         compiler_params=pltpu.CompilerParams(vmem_limit_bytes=16 << 20),
@@ -133,11 +133,11 @@
     tiles = field.shape[0] // 3
     window = turned.shape[1]
     for kind, source, cols in (("folded", 0, folded), ("shared", folded, shared)):
-        for array, (far_row, far_par, lane) in zip(arrays, parts):
+        for array, (far_row, far_par, lane, turn) in zip(arrays, parts):
             row = 1 - place[0] if far_row else place[0]
             par = 1 - place[3] if far_par else place[3]
-            for k in range(pairs):
-                group = (2 * row + par) * pairs + (place[2] + pairs - k) % pairs
+            for k in range(array.shape[0]):
+                group = (2 * row + par) * pairs + (place[2] + pairs - turn - k) % pairs
                 at = pl.multiple_of(segment(kind, group % share, cols, electrodes), 16)
                 joined[pl.ds(at, cols), pl.ds(lane, array.shape[2])] = array[k, source : source + cols]
     first = pl.multiple_of((group // share) * BLOCK, BLOCK)
@@ -177,7 +177,7 @@
 
         base = 3 * tiles * plane
         start = tuple(before[base + j] for j in range(3 * tiles))
-        totals = lax.fori_loop(0, BLOCK // 16, step, start, unroll=4)
+        totals = lax.fori_loop(0, BLOCK // 16, step, start, unroll=8)
         if not last:
             for j in range(3 * tiles):
                 out[base + j] = totals[j]
@@ -254,36 +254,42 @@
     piece = coupling_piece(place, quadrupoles, residuals.reshape(1, -1), shape)
     turns = rotations(piece, "pair")
     (relay, across, halo_across, halo), other, _ = lax.optimization_barrier((first, other, piece))
-    second_across = lax.ppermute(relay, "row", swap)
-    second = lax.ppermute(other, "par", swap)
-    moved = native, across, second, second_across, halo, halo_across, turns
-    *held, turns = lax.optimization_barrier(moved)
-
-    column = jnp.stack([piece] + turns)
+    half = BLOCK // 2
+    cols = folded + shared
+    sides = [piece[:, :half], piece[:, half:]]
+    packed = [jnp.concatenate([a.reshape(-1, 128)] + sides) for a in (relay, other)]
+    crossed = lax.ppermute(packed[0], "row", swap), lax.ppermute(packed[1], "par", swap)
+    moved = native, across, halo, halo_across, turns, crossed
+    native, across, halo, halo_across, turns, crossed = lax.optimization_barrier(moved)
+    size = tiles * count
+    second_across, second = (a[:size].reshape(native.shape) for a in crossed)
+    own_by_row, own_by_par = ([a[size : size + cols][None], a[size + cols :][None]] for a in crossed)
+    held = native, across, second, second_across, halo, halo_across
+
+    column = jnp.stack(turns)
     by_row = lax.ppermute(column, "row", swap)
     by_par = lax.ppermute(column, "par", swap)
-    pieces = []
-    for array in held:
-        pieces += [array] + rotations(array, "mem")
-    field = assemble(place, pieces, (0, 1, 0, 1, 0, 1), rows, electrodes)
+    held = jnp.concatenate(held)
+    field = assemble(place, [held] + rotations(held, "mem"), (0, 1, 0, 1, 0, 1), rows, electrodes)
 
     sums = jnp.zeros((6 * tiles, 8, 128), jnp.float32)
-    half = BLOCK // 2
-    near = [(column, 0, 0, 0)]
+    near = [(piece[None], 0, 0, 0, 0), (column, 0, 0, 0, 1)]
     staged = rows == 4
     if staged:
         sums = gradient_sums(place, field, sums, near, shape, window, False)
         by_row, by_par, sums = lax.optimization_barrier((by_row, by_par, sums))
-    corner = [
-        lax.ppermute(by_row[..., :half], "par", swap),
-        lax.ppermute(by_par[..., half:], "row", swap),
+    lower = jnp.concatenate([own_by_row[0], by_row[..., :half]])
+    upper = jnp.concatenate([own_by_par[1], by_par[..., half:]])
+    corner = lax.ppermute(lower, "par", swap), lax.ppermute(upper, "row", swap)
+    beside = [
+        [(own_by_row[0], 1, 0, 0, 0), (own_by_row[1], 1, 0, half, 0), (by_row, 1, 0, 0, 1)],
+        [(own_by_par[0], 0, 1, 0, 0), (own_by_par[1], 0, 1, half, 0), (by_par, 0, 1, 0, 1)],
     ]
-    beside = [[(by_row, 1, 0, 0)], [(by_par, 0, 1, 0)]]
     if staged:
         for part in beside:
             sums = gradient_sums(place, field, sums, part, shape, window, False)
         corner, sums = lax.optimization_barrier((corner, sums))
-    far = [(corner[0], 1, 1, 0), (corner[1], 1, 1, half)]
+    far = [(corner[0], 1, 1, 0, 0), (corner[1], 1, 1, half, 0)]
     part = far if staged else near + beside[0] + beside[1] + far
     sums = gradient_sums(place, field, sums, part, shape, window, True)
 

time: 91.2 us -> 90.7 us (level)
  local copies, waits for them, and re-layouts: 2.35 us -> 5.94 us
  starting transfers between devices: 28.1 us -> 25.3 us
  Pallas kernels: 29.3 us -> 30.6 us
    ppermute x4, waiting for transfers between devices: 1.66 us -> 5.49 us  [the longest x1 1.95 us: local(): lax.ppermute(upper, 'row', swap)]
    ppermute x1, waiting for transfers between devices: 8.33 us -> 4.54 us  [local(): by_row = lax.ppermute(column, 'row', swap)]
    unnamed x7 -> x12, local copies, waits for them, and re-layouts: 2.15 us -> 4.55 us
    ppermute x10 -> x5, starting transfers between devices: 7.47 us -> 5.13 us  [rotations(): lax.ppermute(value, axis, [(i, (i + k) % size) for i in range(size)])]
    pallas_call x1, Pallas kernels: 16.8 us -> 19.1 us  [coupling_piece(): pl.pallas_call(lambda *refs: coupling_kernel(shape, *refs), out_shape=jax...]
    ppermute x10 -> x5, waiting for transfers between devices: 12.2 us -> 14.3 us  [rotations(): lax.ppermute(value, axis, [(i, (i + k) % size) for i in range(size)])]
    ppermute x1, starting transfers between devices: 0.61 us -> 2.6 us  [local(): lax.ppermute(given, ('row', 'par'), [(0, 3), (1, 2), (2, 1), (3, 0)])]
    ppermute x1, starting transfers between devices: 1.56 us -> 0.29 us  [local(): lax.ppermute(given, 'par', swap)]
  transfers between devices with their start and end apart: 23 -> 18, of which waited for: 16 -> 13; matrix products, arithmetic and copies ran while one was open for 0% -> 0% of each run, Pallas kernels for 29% -> 31%
where the time goes in v3:
time: 90.7 us; the launch traced here: 90.3 us
  Pallas kernels  30.6 us (34%)
  waiting for transfers between devices  26.6 us (29%)
  starting transfers between devices  25.3 us (28%)
  local copies, waits for them, and re-layouts  5.94 us (7%)
  other arithmetic  1.6 us (2%)
    pallas_call x1, Pallas kernels, coupling_piece(): pl.pallas_call(lambda *refs: coupling_kernel(shape, *refs), out_shape=jax...  19.1 us
    ppermute x5, waiting for transfers between devices, rotations(): lax.ppermute(value, axis, [(i, (i + k) % size) for i in range(size)])  14.3 us
    pallas_call x4, Pallas kernels, gradient_sums(): pl.pallas_call(lambda *refs: gradient_kernel(shape, parts, last, *refs),...  10.5 us
    ppermute x1, starting transfers between devices, local(): lax.ppermute(other_out, 'par', swap)  6.68 us
    ppermute x5, starting transfers between devices, rotations(): lax.ppermute(value, axis, [(i, (i + k) % size) for i in range(size)])  5.13 us
    unnamed x12, local copies, waits for them, and re-layouts  4.55 us
    ppermute x1, waiting for transfers between devices, local(): by_row = lax.ppermute(column, 'row', swap)  4.54 us
    ppermute x1, starting transfers between devices, local(): lax.ppermute(native_out, 'row', swap)  3 us
  transfers between devices with their start and end apart: 18, of which 13 were waited for; matrix products, arithmetic and copies ran while one was open for 0% of the time, Pallas kernels for 31%

profile of v3, /device:TPU:0, one launch (start us, length us, event | category | flops | bytes accessed | tf_op | source)
XLA Modules:
  0.0 90.3 jit_solution(8234382143362197088)
XLA Ops:
  0.0 2.1 %copy.7 = bf16[512,2,8,128]{3,0,2,1:T(8,128)(2,1)S(1)} copy(bf16[512,2,8,128]{3,2,1,0:T(8,128)(2,1)} %param.4) | data formatting | bytes 4194304 | tf_op args[0]
  2.1 0.1 slice.64
  2.2 0.5 broadcast_select_fusion
  2.8 0.0 copy-start
  2.8 0.0 copy-start.1
  2.8 0.1 select_bitcast_fusion.1
  2.9 3.0 %collective-permute-start.1 = (bf16[4,512,128]{2,1,0:T(8,128)(2,1)S(1)}, bf16[4,512,128]{2,1,0:T(8,128)(2,1)}, u32[]{:S(2)}, u32[]{:S(2)}) collective-permute-start(bf16[4,512,128]{2,1,0:T(8,128)(2,1)S(1)} %get-tuple-element.49), channel_id=1, source_target_pairs={{0,16},{16,0},{1,17},{17,1},{2,18},{18,2},{3,19},{19,3},{4,20},{20... | collective-permute-start | bytes 1572872 | tf_op jit(solution)/shard_map/ppermute | solution.py:250
  5.9 1.3 %collective-permute-start.2 = (bf16[4,512,128]{2,1,0:T(8,128)(2,1)S(1)}, bf16[4,512,128]{2,1,0:T(8,128)(2,1)}, u32[]{:S(2)}, u32[]{:S(2)}) collective-permute-start(bf16[4,512,128]{2,1,0:T(8,128)(2,1)S(1)} %get-tuple-element.49), channel_id=1, source_target_pairs={{2,16},{4,18},{6,20},{1,19},{3,21},{5,23},{18,0},{20,2},{22,4},{17... | collective-permute-start | bytes 1572872 | tf_op jit(solution)/shard_map/ppermute | solution.py:251
  7.2 0.1 select_bitcast_fusion
  7.2 1.3 %collective-permute-start.3 = (bf16[4,512,128]{2,1,0:T(8,128)(2,1)S(1)}, bf16[4,512,128]{2,1,0:T(8,128)(2,1)}, u32[]{:S(2)}, u32[]{:S(2)}) collective-permute-start(bf16[4,512,128]{2,1,0:T(8,128)(2,1)S(1)} %get-tuple-element.30), channel_id=1, source_target_pairs={{2,0},{4,2},{6,4},{1,3},{3,5},{5,7},{10,8},{12,10},{14,12},{9,11},... | collective-permute-start | bytes 1572872 | tf_op jit(solution)/shard_map/ppermute | solution.py:252
  8.5 6.7 %collective-permute-start = (bf16[4,512,128]{2,1,0:T(8,128)(2,1)S(1)}, bf16[4,512,128]{2,1,0:T(8,128)(2,1)S(1)}, u32[]{:S(2)}, u32[]{:S(2)}) collective-permute-start(bf16[4,512,128]{2,1,0:T(8,128)(2,1)S(1)} %get-tuple-element.50), channel_id=1, source_target_pairs={{0,1},{1,0},{2,3},{3,2},{4,5},{5,4},{6,7},{7,6},{8,9},{9,8},{10,11... | collective-permute-start | bytes 1572872 | tf_op jit(solution)/shard_map/ppermute | solution.py:249
  15.2 0.1 pad_add_fusion.refs_0_
  15.3 0.0 copy-done
  15.3 0.0 copy-done.1
  15.3 19.1 %coupling_piece.1 = bf16[320,256]{1,0:T(8,128)(2,1)S(1)} custom-call(s32[4]{0:T(128)S(1)} %pad_add_fusion.refs_0_, s32[4,32768]{1,0:T(4,128)S(1)} %copy-done, f32[1,32768]{1,0:T(1,128)S(1)} %bitcast.33), custom_call_target="tpu_custom_call" | custom-call | flops 8589934592 | bytes 1048576 | tf_op jit(solution)/shard_map/coupling_piece/pallas_call | solution.py:85
  34.4 0.0 collective-permute-done.1
  34.4 0.0 collective-permute-done.2
  34.4 0.0 collective-permute-done.3
  34.5 0.0 collective-permute-done
  34.5 0.1 pad_maximum_fusion
  34.6 1.6 %collective-permute-start.7 = (bf16[2688,128]{1,0:T(8,128)(2,1)S(1)}, bf16[2688,128]{1,0:T(8,128)(2,1)S(1)}, u32[]{:S(2)}, u32[]{:S(2)}) collective-permute-start(bf16[2688,128]{1,0:T(8,128)(2,1)S(1)} %get-tuple-element.56), channel_id=1, source_target_pairs={{0,16},{16,0},{1,17},{17,1},{2,18},{18,2},{3,19},{19,3},{4,20},{20... | collective-permute-start | bytes 2064392 | tf_op jit(solution)/shard_map/ppermute | solution.py:261
  36.1 0.0 collective-permute-start.8
  36.1 1.1 %collective-permute-start.4 = (bf16[320,256]{1,0:T(8,128)(2,1)S(1)}, bf16[320,256]{1,0:T(8,128)(2,1)S(1)}, u32[]{:S(2)}, u32[]{:S(2)}) collective-permute-start(bf16[320,256]{1,0:T(8,128)(2,1)S(1)} %coupling_piece.1), channel_id=1, source_target_pairs={{0,2},{2,4},{4,6},{6,0},{1,3},{3,5},{5,7},{7,1},{8,10},{10,12},{12... | collective-permute-start | bytes 491528 | tf_op jit(solution)/shard_map/ppermute | solution.py:220
  37.2 2.6 %collective-permute-start.5 = (bf16[320,256]{1,0:T(8,128)(2,1)S(1)}, bf16[320,256]{1,0:T(8,128)(2,1)S(1)}, u32[]{:S(2)}, u32[]{:S(2)}) collective-permute-start(bf16[320,256]{1,0:T(8,128)(2,1)S(1)} %coupling_piece.1), channel_id=1, source_target_pairs={{0,4},{2,6},{4,0},{6,2},{1,5},{3,7},{5,1},{7,3},{8,12},{10,14},{12... | collective-permute-start | bytes 491528 | tf_op jit(solution)/shard_map/ppermute | solution.py:220
  39.8 1.3 %collective-permute-start.6 = (bf16[320,256]{1,0:T(8,128)(2,1)S(1)}, bf16[320,256]{1,0:T(8,128)(2,1)S(1)}, u32[]{:S(2)}, u32[]{:S(2)}) collective-permute-start(bf16[320,256]{1,0:T(8,128)(2,1)S(1)} %coupling_piece.1), channel_id=1, source_target_pairs={{0,6},{2,0},{4,2},{6,4},{1,7},{3,1},{5,3},{7,5},{8,14},{10,8},{12,... | collective-permute-start | bytes 491528 | tf_op jit(solution)/shard_map/ppermute | solution.py:220
  41.2 4.0 %collective-permute-done.4 = bf16[320,256]{1,0:T(8,128)(2,1)S(1)} collective-permute-done((bf16[320,256]{1,0:T(8,128)(2,1)S(1)}, bf16[320,256]{1,0:T(8,128)(2,1)S(1)}, u32[]{:S(2)}, u32[]{:S(2)}) %collective-permute-start.4) | collective-permute-done | bytes 163872 | tf_op jit(solution)/shard_map/ppermute | solution.py:220
  45.2 4.5 %collective-permute-done.5 = bf16[320,256]{1,0:T(8,128)(2,1)S(1)} collective-permute-done((bf16[320,256]{1,0:T(8,128)(2,1)S(1)}, bf16[320,256]{1,0:T(8,128)(2,1)S(1)}, u32[]{:S(2)}, u32[]{:S(2)}) %collective-permute-start.5) | collective-permute-done | bytes 163872 | tf_op jit(solution)/shard_map/ppermute | solution.py:220
  49.7 0.0 collective-permute-done.6
  49.7 1.0 %collective-permute-done.7 = bf16[2688,128]{1,0:T(8,128)(2,1)S(1)} collective-permute-done((bf16[2688,128]{1,0:T(8,128)(2,1)S(1)}, bf16[2688,128]{1,0:T(8,128)(2,1)S(1)}, u32[]{:S(2)}, u32[]{:S(2)}) %collective-permute-start.7) | collective-permute-done | bytes 688160 | tf_op jit(solution)/shard_map/ppermute | solution.py:261
  50.7 1.2 %collective-permute-done.8 = bf16[2688,128]{1,0:T(8,128)(2,1)S(1)} collective-permute-done((bf16[2688,128]{1,0:T(8,128)(2,1)S(1)}, bf16[2688,128]{1,0:T(8,128)(2,1)S(1)}, u32[]{:S(2)}, u32[]{:S(2)}) %collective-permute-start.8) | collective-permute-done | bytes 688160 | tf_op jit(solution)/shard_map/ppermute | solution.py:261
  52.0 1.1 %constant_dynamic-update-slice_fusion.4 = bf16[24,512,128]{2,1,0:T(8,128)(2,1)S(1)} fusion(bf16[24,512,128]{2,1,0:T(8,128)(2,1)S(1)} %constant_dynamic-update-slice_fusion.5, bf16[4,512,128]{2,1,0:T(8,128)(2,1)} %collective-permute-done.1), kind=kLoop, calls=%fused_computation.23 | loop fusion | bytes 1048576
  53.1 0.1 constant_dynamic-update-slice_fusion.3
  53.2 0.1 constant_dynamic-update-slice_fusion.2
  53.3 1.1 %constant_dynamic-update-slice_fusion.1 = bf16[24,512,128]{2,1,0:T(8,128)(2,1)S(1)} fusion(bf16[24,512,128]{2,1,0:T(8,128)(2,1)S(1)} %constant_dynamic-update-slice_fusion.2, bf16[4,512,128]{2,1,0:T(8,128)(2,1)} %collective-permute-done.3), kind=kLoop, calls=%fused_computation.20 | loop fusion | bytes 1048576
  54.4 1.1 %constant_dynamic-update-slice_fusion.refs_1_ = bf16[24,512,128]{2,1,0:T(8,128)(2,1)S(1)} fusion(bf16[24,512,128]{2,1,0:T(8,128)(2,1)S(1)} %constant_dynamic-update-slice_fusion.1, bf16[4,512,128]{2,1,0:T(8,128)(2,1)} %collective-permute-done.2), kind=kLoop, calls=%fused_computation.19 | loop fusion | bytes 1048576 | tf_op jit(solution)/shard_map/concatenate | solution.py:272
  55.5 0.1 collective-permute-start.9
  55.6 0.1 pad_maximum_fusion.4.refs_4_
  55.7 0.6 collective-permute-start.10
  56.3 0.3 collective-permute-start.11
  56.6 4.7 %collective-permute-done.9.refs_2_ = bf16[24,512,128]{2,1,0:T(8,128)(2,1)S(1)} collective-permute-done((bf16[24,512,128]{2,1,0:T(8,128)(2,1)S(1)}, bf16[24,512,128]{2,1,0:T(8,128)(2,1)S(1)}, u32[]{:S(2)}, u32[]{:S(2)}) %collective-permute-start.9) | collective-permute-done | bytes 3145760 | tf_op jit(solution)/shard_map/ppermute | solution.py:220
  61.2 1.0 %assemble_fields.1.refs_1_ = bf16[12,2048,128]{2,1,0:T(8,128)(2,1)S(1)} custom-call(s32[4]{0:T(128)S(1)} %pad_add_fusion.refs_0_, bf16[24,512,128]{2,1,0:T(8,128)(2,1)S(1)} %constant_dynamic-update-slice_fusion.refs_1_, bf16[24,512,128]{2,1,0:T(8,128)(2,1)S(1)} %collective-permute-done.9.refs_2_), custom_call_target="tpu_custom_call" | custom-call | bytes 4194304 | tf_op jit(solution)/shard_map/assemble_fields/pallas_call | solution.py:118
  62.2 2.6 %gradient_sums.4.refs_2_ = f32[24,8,128]{2,1,0:T(8,128)S(1)} custom-call(s32[4]{0:T(128)S(1)} %pad_add_fusion.refs_0_, bf16[12,2048,128]{2,1,0:T(8,128)(2,1)S(1)} %assemble_fields.1.refs_1_, f32[24,8,128]{2,1,0:T(8,128)S(1)} %broadcast_in_dim.19.refs_2_, bf16[1,320,256]{2,1,0:T(8,128)(2,1)S(1)} %bitcast.32, bf16[3,320,256]{2,1,0:T(8,128)(2,1)S(1)} %pad_maximum_fusion.4.refs_4_), custom_call_target="tpu_custom_call" | custom-call | flops 1006632960 | bytes 8388608 | tf_op jit(solution)/shard_map/gradient_sums/pallas_call | solution.py:199
  64.8 4.5 %collective-permute-done.10.refs_5_ = bf16[3,320,256]{2,1,0:T(8,128)(2,1)S(1)} collective-permute-done((bf16[3,320,256]{2,1,0:T(8,128)(2,1)S(1)}, bf16[3,320,256]{2,1,0:T(8,128)(2,1)S(1)}, u32[]{:S(2)}, u32[]{:S(2)}) %collective-permute-start.10) | collective-permute-done | bytes 491552 | tf_op jit(solution)/shard_map/ppermute | solution.py:270
  69.3 0.3 collective-permute-done.11.refs_5_
  69.7 1.6 %collective-permute-start.13 = (bf16[4,320,128]{2,1,0:T(8,128)(2,1)S(1)}, bf16[4,320,128]{2,1,0:T(8,128)(2,1)S(1)}, u32[]{:S(2)}, u32[]{:S(2)}) collective-permute-start(bf16[4,320,128]{2,1,0:T(8,128)(2,1)S(1)} %pad_maximum_fusion.6), channel_id=1, source_target_pairs={{0,16},{16,0},{1,17},{17,1},{2,18},{18,2},{3,19},{19,3},{4,20},{20... | collective-permute-start | bytes 983048 | tf_op jit(solution)/shard_map/ppermute | solution.py:283
  71.3 0.4 collective-permute-start.12
  71.7 2.6 %gradient_sums.5.refs_2_ = f32[24,8,128]{2,1,0:T(8,128)S(1)} custom-call(s32[4]{0:T(128)S(1)} %pad_add_fusion.refs_0_, bf16[12,2048,128]{2,1,0:T(8,128)(2,1)S(1)} %assemble_fields.1.refs_1_, f32[24,8,128]{2,1,0:T(8,128)S(1)} %gradient_sums.4.refs_2_, bf16[1,320,128]{2,1,0:T(8,128)(2,1)S(1)} %get-tuple-element.61.refs_3_, ...), custom_call_target="tpu_custom_call" | custom-call | flops 1006632960 | bytes 8388608 | tf_op jit(solution)/shard_map/gradient_sums/pallas_call | solution.py:199
  74.3 2.6 %gradient_sums.6.refs_2_ = f32[24,8,128]{2,1,0:T(8,128)S(1)} custom-call(s32[4]{0:T(128)S(1)} %pad_add_fusion.refs_0_, bf16[12,2048,128]{2,1,0:T(8,128)(2,1)S(1)} %assemble_fields.1.refs_1_, f32[24,8,128]{2,1,0:T(8,128)S(1)} %gradient_sums.5.refs_2_, bf16[1,320,128]{2,1,0:T(8,128)(2,1)S(1)} %get-tuple-element.51.refs_3_, ...), custom_call_target="tpu_custom_call" | custom-call | flops 1006632960 | bytes 8388608 | tf_op jit(solution)/shard_map/gradient_sums/pallas_call | solution.py:199
  76.9 0.0 copy-start.2
  76.9 2.0 %collective-permute-done.13.refs_4_ = bf16[4,320,128]{2,1,0:T(8,128)(2,1)S(1)} collective-permute-done((bf16[4,320,128]{2,1,0:T(8,128)(2,1)S(1)}, bf16[4,320,128]{2,1,0:T(8,128)(2,1)S(1)}, u32[]{:S(2)}, u32[]{:S(2)}) %collective-permute-start.13) | collective-permute-done | bytes 327712 | tf_op jit(solution)/shard_map/ppermute | solution.py:283
  78.8 1.3 %collective-permute-done.12.refs_3_ = bf16[4,320,128]{2,1,0:T(8,128)(2,1)S(1)} collective-permute-done((bf16[4,320,128]{2,1,0:T(8,128)(2,1)S(1)}, bf16[4,320,128]{2,1,0:T(8,128)(2,1)S(1)}, u32[]{:S(2)}, u32[]{:S(2)}) %collective-permute-start.12) | collective-permute-done | bytes 327712 | tf_op jit(solution)/shard_map/ppermute | solution.py:283
  80.1 2.8 %gradient_sums.7 = f32[4,8,128]{2,1,0:T(8,128)S(1)} custom-call(s32[4]{0:T(128)S(1)} %pad_add_fusion.refs_0_, bf16[12,2048,128]{2,1,0:T(8,128)(2,1)S(1)} %assemble_fields.1.refs_1_, f32[24,8,128]{2,1,0:T(8,128)S(1)} %gradient_sums.6.refs_2_, bf16[4,320,128]{2,1,0:T(8,128)(2,1)S(1)} %collective-permute-done.12.refs_3_, ...), custom_call_target="tpu_custom_call" | custom-call | flops 1006632960 | bytes 8388608 | tf_op jit(solution)/shard_map/gradient_sums/pallas_call | solution.py:199
  83.0 0.7 collective-permute-start.14
  83.6 0.3 collective-permute-start.15
  83.9 2.6 %collective-permute-start.16 = (f32[2,8,128]{2,1,0:T(8,128)S(1)}, f32[2,8,128]{2,1,0:T(8,128)S(1)}, u32[]{:S(2)}, u32[]{:S(2)}) collective-permute-start(f32[2,8,128]{2,1,0:T(8,128)S(1)} %get-tuple-element.60), channel_id=1, source_target_pairs={{0,17},{1,16},{16,1},{17,0},{2,19},{3,18},{18,3},{19,2},{4,21},{5,... | collective-permute-start | bytes 24584 | tf_op jit(solution)/shard_map/ppermute | solution.py:301
  86.5 0.2 collective-permute-done.14
  86.7 0.6 collective-permute-done.15
  87.3 1.2 %collective-permute-done.16 = f32[2,8,128]{2,1,0:T(8,128)S(1)} collective-permute-done((f32[2,8,128]{2,1,0:T(8,128)S(1)}, f32[2,8,128]{2,1,0:T(8,128)S(1)}, u32[]{:S(2)}, u32[]{:S(2)}) %collective-permute-start.16) | collective-permute-done | bytes 8224 | tf_op jit(solution)/shard_map/ppermute | solution.py:301
  88.5 0.0 collective-permute-start.17
  88.5 1.2 %collective-permute-done.17 = f32[2,8,128]{2,1,0:T(8,128)S(1)} collective-permute-done((f32[2,8,128]{2,1,0:T(8,128)S(1)}, f32[2,8,128]{2,1,0:T(8,128)S(1)}, u32[]{:S(2)}, u32[]{:S(2)}) %collective-permute-start.17) | collective-permute-done | bytes 8224 | tf_op jit(solution)/shard_map/ppermute | solution.py:220
  89.7 0.0 copy-done.2
  89.7 0.6 add_multiply_fusion
  (15 shorter events, 0.3 us)
Async XLA Ops:
  2.8 12.5 %copy-start = (s32[4,32768]{1,0:T(4,128)S(1)}, s32[4,32768]{1,0:T(4,128)}, u32[]{:S(2)}) copy-start(s32[4,32768]{1,0:T(4,128)} %refs_1_.1) | copy-start | bytes 1572868
  2.8 12.5 %copy-start.1 = (f32[32768]{0:T(1024)S(1)}, f32[32768]{0:T(1024)}, u32[]{:S(2)}) copy-start(f32[32768]{0:T(1024)} %param.6) | copy-start | bytes 393220
  2.9 31.6 %collective-permute-start.1 = (bf16[4,512,128]{2,1,0:T(8,128)(2,1)S(1)}, bf16[4,512,128]{2,1,0:T(8,128)(2,1)}, u32[]{:S(2)}, u32[]{:S(2)}) collective-permute-start(bf16[4,512,128]{2,1,0:T(8,128)(2,1)S(1)} %get-tuple-element.49), channel_id=1, source_target_pairs={{0,16},{16,0},{1,17},{17,1},{2,18},{18,2},{3,19},{19,3},{4,20},{20... | collective-permute-start | bytes 1572872 | tf_op jit(solution)/shard_map/ppermute | solution.py:250
  5.9 28.6 %collective-permute-start.2 = (bf16[4,512,128]{2,1,0:T(8,128)(2,1)S(1)}, bf16[4,512,128]{2,1,0:T(8,128)(2,1)}, u32[]{:S(2)}, u32[]{:S(2)}) collective-permute-start(bf16[4,512,128]{2,1,0:T(8,128)(2,1)S(1)} %get-tuple-element.49), channel_id=1, source_target_pairs={{2,16},{4,18},{6,20},{1,19},{3,21},{5,23},{18,0},{20,2},{22,4},{17... | collective-permute-start | bytes 1572872 | tf_op jit(solution)/shard_map/ppermute | solution.py:251
  7.2 27.2 %collective-permute-start.3 = (bf16[4,512,128]{2,1,0:T(8,128)(2,1)S(1)}, bf16[4,512,128]{2,1,0:T(8,128)(2,1)}, u32[]{:S(2)}, u32[]{:S(2)}) collective-permute-start(bf16[4,512,128]{2,1,0:T(8,128)(2,1)S(1)} %get-tuple-element.30), channel_id=1, source_target_pairs={{2,0},{4,2},{6,4},{1,3},{3,5},{5,7},{10,8},{12,10},{14,12},{9,11},... | collective-permute-start | bytes 1572872 | tf_op jit(solution)/shard_map/ppermute | solution.py:252
  8.5 25.9 %collective-permute-start = (bf16[4,512,128]{2,1,0:T(8,128)(2,1)S(1)}, bf16[4,512,128]{2,1,0:T(8,128)(2,1)S(1)}, u32[]{:S(2)}, u32[]{:S(2)}) collective-permute-start(bf16[4,512,128]{2,1,0:T(8,128)(2,1)S(1)} %get-tuple-element.50), channel_id=1, source_target_pairs={{0,1},{1,0},{2,3},{3,2},{4,5},{5,4},{6,7},{7,6},{8,9},{9,8},{10,11... | collective-permute-start | bytes 1572872 | tf_op jit(solution)/shard_map/ppermute | solution.py:249
  34.6 16.1 %collective-permute-start.7 = (bf16[2688,128]{1,0:T(8,128)(2,1)S(1)}, bf16[2688,128]{1,0:T(8,128)(2,1)S(1)}, u32[]{:S(2)}, u32[]{:S(2)}) collective-permute-start(bf16[2688,128]{1,0:T(8,128)(2,1)S(1)} %get-tuple-element.56), channel_id=1, source_target_pairs={{0,16},{16,0},{1,17},{17,1},{2,18},{18,2},{3,19},{19,3},{4,20},{20... | collective-permute-start | bytes 2064392 | tf_op jit(solution)/shard_map/ppermute | solution.py:261
  36.1 15.8 %collective-permute-start.8 = (bf16[2688,128]{1,0:T(8,128)(2,1)S(1)}, bf16[2688,128]{1,0:T(8,128)(2,1)S(1)}, u32[]{:S(2)}, u32[]{:S(2)}) collective-permute-start(bf16[2688,128]{1,0:T(8,128)(2,1)S(1)} %get-tuple-element.55), channel_id=1, source_target_pairs={{0,1},{1,0},{2,3},{3,2},{4,5},{5,4},{6,7},{7,6},{8,9},{9,8},{10,11... | collective-permute-start | bytes 2064392 | tf_op jit(solution)/shard_map/ppermute | solution.py:261
  36.1 9.0 %collective-permute-start.4 = (bf16[320,256]{1,0:T(8,128)(2,1)S(1)}, bf16[320,256]{1,0:T(8,128)(2,1)S(1)}, u32[]{:S(2)}, u32[]{:S(2)}) collective-permute-start(bf16[320,256]{1,0:T(8,128)(2,1)S(1)} %coupling_piece.1), channel_id=1, source_target_pairs={{0,2},{2,4},{4,6},{6,0},{1,3},{3,5},{5,7},{7,1},{8,10},{10,12},{12... | collective-permute-start | bytes 491528 | tf_op jit(solution)/shard_map/ppermute | solution.py:220
  37.2 12.4 %collective-permute-start.5 = (bf16[320,256]{1,0:T(8,128)(2,1)S(1)}, bf16[320,256]{1,0:T(8,128)(2,1)S(1)}, u32[]{:S(2)}, u32[]{:S(2)}) collective-permute-start(bf16[320,256]{1,0:T(8,128)(2,1)S(1)} %coupling_piece.1), channel_id=1, source_target_pairs={{0,4},{2,6},{4,0},{6,2},{1,5},{3,7},{5,1},{7,3},{8,12},{10,14},{12... | collective-permute-start | bytes 491528 | tf_op jit(solution)/shard_map/ppermute | solution.py:220
  39.8 9.8 %collective-permute-start.6 = (bf16[320,256]{1,0:T(8,128)(2,1)S(1)}, bf16[320,256]{1,0:T(8,128)(2,1)S(1)}, u32[]{:S(2)}, u32[]{:S(2)}) collective-permute-start(bf16[320,256]{1,0:T(8,128)(2,1)S(1)} %coupling_piece.1), channel_id=1, source_target_pairs={{0,6},{2,0},{4,2},{6,4},{1,7},{3,1},{5,3},{7,5},{8,14},{10,8},{12,... | collective-permute-start | bytes 491528 | tf_op jit(solution)/shard_map/ppermute | solution.py:220
  55.5 5.7 %collective-permute-start.9 = (bf16[24,512,128]{2,1,0:T(8,128)(2,1)S(1)}, bf16[24,512,128]{2,1,0:T(8,128)(2,1)S(1)}, u32[]{:S(2)}, u32[]{:S(2)}) collective-permute-start(bf16[24,512,128]{2,1,0:T(8,128)(2,1)S(1)} %constant_dynamic-update-slice_fusion.refs_1_), channel_id=1, source_target_pairs={{0,8},{8,0},{1,9},{9,1},{2,10},{10,2},{3,11},{11,3},{4,12},{12,4},... | collective-permute-start | bytes 9437192 | tf_op jit(solution)/shard_map/ppermute | solution.py:220
  55.7 13.7 %collective-permute-start.10 = (bf16[3,320,256]{2,1,0:T(8,128)(2,1)S(1)}, bf16[3,320,256]{2,1,0:T(8,128)(2,1)S(1)}, u32[]{:S(2)}, u32[]{:S(2)}) collective-permute-start(bf16[3,320,256]{2,1,0:T(8,128)(2,1)S(1)} %pad_maximum_fusion.4.refs_4_), channel_id=1, source_target_pairs={{0,16},{16,0},{1,17},{17,1},{2,18},{18,2},{3,19},{19,3},{4,20},{20... | collective-permute-start | bytes 1474568 | tf_op jit(solution)/shard_map/ppermute | solution.py:270
  56.3 13.3 %collective-permute-start.11 = (bf16[3,320,256]{2,1,0:T(8,128)(2,1)S(1)}, bf16[3,320,256]{2,1,0:T(8,128)(2,1)S(1)}, u32[]{:S(2)}, u32[]{:S(2)}) collective-permute-start(bf16[3,320,256]{2,1,0:T(8,128)(2,1)S(1)} %pad_maximum_fusion.4.refs_4_), channel_id=1, source_target_pairs={{0,1},{1,0},{2,3},{3,2},{4,5},{5,4},{6,7},{7,6},{8,9},{9,8},{10,11... | collective-permute-start | bytes 1474568 | tf_op jit(solution)/shard_map/ppermute | solution.py:271
  69.7 9.1 %collective-permute-start.13 = (bf16[4,320,128]{2,1,0:T(8,128)(2,1)S(1)}, bf16[4,320,128]{2,1,0:T(8,128)(2,1)S(1)}, u32[]{:S(2)}, u32[]{:S(2)}) collective-permute-start(bf16[4,320,128]{2,1,0:T(8,128)(2,1)S(1)} %pad_maximum_fusion.6), channel_id=1, source_target_pairs={{0,16},{16,0},{1,17},{17,1},{2,18},{18,2},{3,19},{19,3},{4,20},{20... | collective-permute-start | bytes 983048 | tf_op jit(solution)/shard_map/ppermute | solution.py:283
  71.3 8.8 %collective-permute-start.12 = (bf16[4,320,128]{2,1,0:T(8,128)(2,1)S(1)}, bf16[4,320,128]{2,1,0:T(8,128)(2,1)S(1)}, u32[]{:S(2)}, u32[]{:S(2)}) collective-permute-start(bf16[4,320,128]{2,1,0:T(8,128)(2,1)S(1)} %pad_maximum_fusion.5), channel_id=1, source_target_pairs={{0,1},{1,0},{2,3},{3,2},{4,5},{5,4},{6,7},{7,6},{8,9},{9,8},{10,11... | collective-permute-start | bytes 983048 | tf_op jit(solution)/shard_map/ppermute | solution.py:283
  76.9 12.8 %copy-start.2 = (f32[2,8,128]{2,1,0:T(8,128)S(1)}, f32[2,8,128]{2,1,0:T(8,128)}, u32[]{:S(2)}) copy-start(f32[2,8,128]{2,1,0:T(8,128)} %param.7) | copy-start | bytes 24580
  83.0 3.7 %collective-permute-start.14 = (f32[2,8,128]{2,1,0:T(8,128)S(1)}, f32[2,8,128]{2,1,0:T(8,128)S(1)}, u32[]{:S(2)}, u32[]{:S(2)}) collective-permute-start(f32[2,8,128]{2,1,0:T(8,128)S(1)} %get-tuple-element.59), channel_id=1, source_target_pairs={{0,16},{16,0},{1,17},{17,1},{2,18},{18,2},{3,19},{19,3},{4,20},{20... | collective-permute-start | bytes 24584 | tf_op jit(solution)/shard_map/ppermute | solution.py:300
  83.6 3.7 %collective-permute-start.15 = (f32[2,8,128]{2,1,0:T(8,128)S(1)}, f32[2,8,128]{2,1,0:T(8,128)S(1)}, u32[]{:S(2)}, u32[]{:S(2)}) collective-permute-start(f32[2,8,128]{2,1,0:T(8,128)S(1)} %get-tuple-element.60), channel_id=1, source_target_pairs={{0,1},{1,0},{2,3},{3,2},{4,5},{5,4},{6,7},{7,6},{8,9},{9,8},{10,11... | collective-permute-start | bytes 24584 | tf_op jit(solution)/shard_map/ppermute | solution.py:300
  83.9 4.5 %collective-permute-start.16 = (f32[2,8,128]{2,1,0:T(8,128)S(1)}, f32[2,8,128]{2,1,0:T(8,128)S(1)}, u32[]{:S(2)}, u32[]{:S(2)}) collective-permute-start(f32[2,8,128]{2,1,0:T(8,128)S(1)} %get-tuple-element.60), channel_id=1, source_target_pairs={{0,17},{1,16},{16,1},{17,0},{2,19},{3,18},{18,3},{19,2},{4,21},{5,... | collective-permute-start | bytes 24584 | tf_op jit(solution)/shard_map/ppermute | solution.py:301
  88.5 1.2 %collective-permute-start.17 = (f32[2,8,128]{2,1,0:T(8,128)S(1)}, f32[2,8,128]{2,1,0:T(8,128)S(1)}, u32[]{:S(2)}, u32[]{:S(2)}) collective-permute-start(f32[2,8,128]{2,1,0:T(8,128)S(1)} %add_add_fusion), channel_id=1, source_target_pairs={{0,8},{8,0},{1,9},{9,1},{2,10},{10,2},{3,11},{11,3},{4,12},{12,4},... | collective-permute-start | bytes 24584 | tf_op jit(solution)/shard_map/ppermute | solution.py:220

commit v4 on v3

--- a/solution.py
+++ b/solution.py
@@ -6,7 +6,7 @@
 from jax.sharding import Mesh, PartitionSpec as P
 
 BLOCK = 256
-CHUNK = 512
+CHUNK = 2048
 
 
 def onehots(dest, first, rows, plus, minus, up, down):
@@ -98,6 +98,28 @@
     )(place, quadrupoles, residuals)
 
 
+def join_kernel(*refs):
+    pieces, out = refs[:-1], refs[-1]
+    tiles, count = out.shape[0] // len(pieces), out.shape[1]
+    for slot, piece in enumerate(pieces):
+        for tile in range(tiles):
+            part = piece[tile] if len(piece.shape) == 3 else piece[count * tile : count * (tile + 1)]
+            out[tiles * slot + tile] = part
+
+
+def join(pieces):
+    tiles, count, lanes = pieces[0].shape
+    return pl.pallas_call(
+        join_kernel,
+        out_shape=jax.ShapeDtypeStruct((tiles * len(pieces), count, lanes), jnp.bfloat16),
+        in_specs=[VMEM] * len(pieces),
+        out_specs=VMEM,
+        compiler_params=pltpu.CompilerParams(vmem_limit_bytes=16 << 20),
+        cost_estimate=pl.CostEstimate(flops=0, bytes_accessed=1 << 10, transcendentals=0),
+        name="join_pieces",
+    )(*pieces)
+
+
 def assemble_kernel(rows, far, place, *refs):
     pieces, field = refs[:-1], refs[-1]
     electrodes = field.shape[1]
@@ -121,7 +143,7 @@
         in_specs=[SMEM] + [VMEM] * len(pieces),
         out_specs=VMEM,
         compiler_params=pltpu.CompilerParams(vmem_limit_bytes=16 << 20),
-        cost_estimate=pl.CostEstimate(flops=0, bytes_accessed=4 << 20, transcendentals=0),
+        cost_estimate=pl.CostEstimate(flops=0, bytes_accessed=1 << 10, transcendentals=0),
         name="assemble_fields",
     )(place, *pieces)
 
@@ -208,7 +230,7 @@
         ],
         compiler_params=pltpu.CompilerParams(vmem_limit_bytes=16 << 20),
         cost_estimate=pl.CostEstimate(
-            flops=2 * BLOCK * window * 3 * tiles * 128, bytes_accessed=8 << 20, transcendentals=0
+            flops=0, bytes_accessed=1 << 10, transcendentals=0
         ),
         name="gradient_sums",
     )(place, field, before, *arrays)
@@ -260,16 +282,13 @@
     packed = [jnp.concatenate([a.reshape(-1, 128)] + sides) for a in (relay, other)]
     crossed = lax.ppermute(packed[0], "row", swap), lax.ppermute(packed[1], "par", swap)
     moved = native, across, halo, halo_across, turns, crossed
-    native, across, halo, halo_across, turns, crossed = lax.optimization_barrier(moved)
+    native, across, halo, halo_across, _, crossed = lax.optimization_barrier(moved)
     size = tiles * count
-    second_across, second = (a[:size].reshape(native.shape) for a in crossed)
     own_by_row, own_by_par = ([a[size : size + cols][None], a[size + cols :][None]] for a in crossed)
-    held = native, across, second, second_across, halo, halo_across
-
     column = jnp.stack(turns)
     by_row = lax.ppermute(column, "row", swap)
     by_par = lax.ppermute(column, "par", swap)
-    held = jnp.concatenate(held)
+    held = join([native, across, crossed[1], crossed[0], halo, halo_across])
     field = assemble(place, [held] + rotations(held, "mem"), (0, 1, 0, 1, 0, 1), rows, electrodes)
 
     sums = jnp.zeros((6 * tiles, 8, 128), jnp.float32)

time: 90.7 us -> 87.7 us (0.967)
  local copies, waits for them, and re-layouts: 5.94 us -> 2.36 us
  Pallas kernels: 30.6 us -> 27.2 us
  other arithmetic: 1.6 us -> 3.65 us
  starting transfers between devices: 25.3 us -> 27.1 us
    pallas_call x1, Pallas kernels: 19.1 us -> 15.5 us  [coupling_piece(): pl.pallas_call(lambda *refs: coupling_kernel(shape, *refs), out_shape=jax...]
    unnamed x12 -> x7, local copies, waits for them, and re-layouts: 4.55 us -> 2.14 us
    ppermute x1, waiting for transfers between devices: 0.01 us -> 2.36 us  [local(): lax.ppermute(native, ('pair', 'par'), ahead)]
    ppermute x5, starting transfers between devices: 5.13 us -> 6.49 us  [rotations(): lax.ppermute(value, axis, [(i, (i + k) % size) for i in range(size)])]
    concatenate x1 -> x0, local copies, waits for them, and re-layouts: 1.11 us -> none  [local(): held = jnp.concatenate(held)]
    ppermute x5, waiting for transfers between devices: 14.3 us -> 13.2 us  [rotations(): lax.ppermute(value, axis, [(i, (i + k) % size) for i in range(size)])]
    concatenate x1, other arithmetic: 0.09 us -> 1.13 us  [local(): jnp.concatenate([a.reshape(-1, 128)] + sides)]
    ppermute x1, waiting for transfers between devices: 1.03 us -> 0.01 us  [local(): lax.ppermute(packed[0], 'row', swap)]
  transfers between devices with their start and end apart: 18 -> 18, of which waited for: 13 -> 13; matrix products, arithmetic and copies ran while one was open for 0% -> 0% of each run, Pallas kernels for 31% -> 28%
where the time goes in v4:
time: 87.7 us; the launch traced here: 87.2 us
  Pallas kernels  27.2 us (31%)
  starting transfers between devices  27.1 us (31%)
  waiting for transfers between devices  26.8 us (31%)
  other arithmetic  3.65 us (4%)
  local copies, waits for them, and re-layouts  2.36 us (3%)
    pallas_call x1, Pallas kernels, coupling_piece(): pl.pallas_call(lambda *refs: coupling_kernel(shape, *refs), out_shape=jax...  15.5 us
    ppermute x5, waiting for transfers between devices, rotations(): lax.ppermute(value, axis, [(i, (i + k) % size) for i in range(size)])  13.2 us
    pallas_call x4, Pallas kernels, gradient_sums(): pl.pallas_call(lambda *refs: gradient_kernel(shape, parts, last, *refs),...  10.6 us
    ppermute x5, starting transfers between devices, rotations(): lax.ppermute(value, axis, [(i, (i + k) % size) for i in range(size)])  6.49 us
    ppermute x1, starting transfers between devices, local(): lax.ppermute(other_out, 'par', swap)  5.97 us
    ppermute x1, waiting for transfers between devices, local(): by_row = lax.ppermute(column, 'row', swap)  4.53 us
    ppermute x1, starting transfers between devices, local(): lax.ppermute(native_out, 'row', swap)  2.94 us
    ppermute x1, waiting for transfers between devices, local(): lax.ppermute(native, ('pair', 'par'), ahead)  2.36 us
  transfers between devices with their start and end apart: 18, of which 13 were waited for; matrix products, arithmetic and copies ran while one was open for 0% of the time, Pallas kernels for 28%

profile of v4, /device:TPU:0, one launch (start us, length us, event | category | flops | bytes accessed | tf_op | source)
XLA Modules:
  0.0 87.2 jit_solution(5448480777341778049)
XLA Ops:
  0.0 2.1 %copy.7 = bf16[512,2,8,128]{3,0,2,1:T(8,128)(2,1)S(1)} copy(bf16[512,2,8,128]{3,2,1,0:T(8,128)(2,1)} %param.4) | data formatting | bytes 4194304 | tf_op args[0]
  2.1 0.1 slice.58
  2.2 0.5 broadcast_select_fusion
  2.8 1.1 %select_bitcast_fusion.1 = (bf16[4,512,128]{2,1,0:T(8,128)(2,1)}, bf16[4,512,128]{2,1,0:T(8,128)(2,1)}) fusion(pred[]{:T(512)S(6)} %eq.4, bf16[2,4,512,128]{3,2,1,0:T(8,128)(2,1)S(1)} %get-tuple-element.39), kind=kLoop, calls=%fused_computation.8 | loop fusion | flops 524288 | bytes 2097153 | tf_op jit(solution)/shard_map/jit(_where)/select_n | solution.py:264
  3.9 0.0 copy-start
  3.9 0.0 copy-start.1
  3.9 2.9 %collective-permute-start.1 = (bf16[4,512,128]{2,1,0:T(8,128)(2,1)}, bf16[4,512,128]{2,1,0:T(8,128)(2,1)S(1)}, u32[]{:S(2)}, u32[]{:S(2)}) collective-permute-start(bf16[4,512,128]{2,1,0:T(8,128)(2,1)} %get-tuple-element.43), channel_id=1, source_target_pairs={{0,16},{16,0},{1,17},{17,1},{2,18},{18,2},{3,19},{19,3},{4,20},{20... | collective-permute-start | bytes 1572872 | tf_op jit(solution)/shard_map/ppermute | solution.py:272
  6.8 1.3 %collective-permute-start.2 = (bf16[4,512,128]{2,1,0:T(8,128)(2,1)}, bf16[4,512,128]{2,1,0:T(8,128)(2,1)S(1)}, u32[]{:S(2)}, u32[]{:S(2)}) collective-permute-start(bf16[4,512,128]{2,1,0:T(8,128)(2,1)} %get-tuple-element.43), channel_id=1, source_target_pairs={{2,16},{4,18},{6,20},{1,19},{3,21},{5,23},{18,0},{20,2},{22,4},{17... | collective-permute-start | bytes 1572872 | tf_op jit(solution)/shard_map/ppermute | solution.py:273
  8.1 0.1 select_bitcast_fusion
  8.2 1.3 %collective-permute-start.3 = (bf16[4,512,128]{2,1,0:T(8,128)(2,1)S(1)}, bf16[4,512,128]{2,1,0:T(8,128)(2,1)S(1)}, u32[]{:S(2)}, u32[]{:S(2)}) collective-permute-start(bf16[4,512,128]{2,1,0:T(8,128)(2,1)S(1)} %get-tuple-element.27.refs_0_), channel_id=1, source_target_pairs={{2,0},{4,2},{6,4},{1,3},{3,5},{5,7},{10,8},{12,10},{14,12},{9,11},... | collective-permute-start | bytes 1572872 | tf_op jit(solution)/shard_map/ppermute | solution.py:274
  9.5 6.0 %collective-permute-start = (bf16[4,512,128]{2,1,0:T(8,128)(2,1)}, bf16[4,512,128]{2,1,0:T(8,128)(2,1)}, u32[]{:S(2)}, u32[]{:S(2)}) collective-permute-start(bf16[4,512,128]{2,1,0:T(8,128)(2,1)} %get-tuple-element.44), channel_id=1, source_target_pairs={{0,1},{1,0},{2,3},{3,2},{4,5},{5,4},{6,7},{7,6},{8,9},{9,8},{10,11... | collective-permute-start | bytes 1572872 | tf_op jit(solution)/shard_map/ppermute | solution.py:271
  15.4 0.1 pad_add_fusion.refs_0_
  15.5 0.0 copy-done
  15.5 0.0 copy-done.1
  15.5 15.5 %coupling_piece.1 = bf16[320,256]{1,0:T(8,128)(2,1)S(1)} custom-call(s32[4]{0:T(128)S(1)} %pad_add_fusion.refs_0_, s32[4,32768]{1,0:T(4,128)S(1)} %copy-done, f32[1,32768]{1,0:T(1,128)S(1)} %bitcast.31), custom_call_target="tpu_custom_call" | custom-call | flops 8589934592 | bytes 1048576 | tf_op jit(solution)/shard_map/coupling_piece/pallas_call | solution.py:85
  31.0 0.0 collective-permute-done.1.refs_1_
  31.0 0.0 collective-permute-done.2.refs_5_
  31.0 2.4 %collective-permute-done.3.refs_4_ = bf16[4,512,128]{2,1,0:T(8,128)(2,1)S(1)} collective-permute-done((bf16[4,512,128]{2,1,0:T(8,128)(2,1)S(1)}, bf16[4,512,128]{2,1,0:T(8,128)(2,1)S(1)}, u32[]{:S(2)}, u32[]{:S(2)}) %collective-permute-start.3) | collective-permute-done | bytes 524320 | tf_op jit(solution)/shard_map/ppermute | solution.py:274
  33.4 0.0 collective-permute-done
  33.4 1.1 %pad_maximum_fusion = (bf16[2688,128]{1,0:T(8,128)(2,1)S(1)}, bf16[2688,128]{1,0:T(8,128)(2,1)S(1)}) fusion(bf16[320,128]{1,0:T(8,128)(2,1)S(1)} %get-tuple-element.52, bf16[320,128]{1,0:T(8,128)(2,1)S(1)} %get-tuple-element.51, bf16[2048,128]{1,0:T(8,128)(2,1)S(1)} %bitcast.34, bf16[2048,128]{1,0:T(8,128)(2,1)} %bitcast.10), kind=kLoop, calls=%fused_computation.3 | loop fusion | flops 3440640 | bytes 2588672 | tf_op jit(solution)/shard_map/concatenate | solution.py:282
  34.5 1.7 %collective-permute-start.7 = (bf16[2688,128]{1,0:T(8,128)(2,1)S(1)}, bf16[2688,128]{1,0:T(8,128)(2,1)S(1)}, u32[]{:S(2)}, u32[]{:S(2)}) collective-permute-start(bf16[2688,128]{1,0:T(8,128)(2,1)S(1)} %get-tuple-element.50), channel_id=1, source_target_pairs={{0,16},{16,0},{1,17},{17,1},{2,18},{18,2},{3,19},{19,3},{4,20},{20... | collective-permute-start | bytes 2064392 | tf_op jit(solution)/shard_map/ppermute | solution.py:283
  36.2 0.6 collective-permute-start.8
  36.8 2.5 %collective-permute-start.4 = (bf16[320,256]{1,0:T(8,128)(2,1)S(1)}, bf16[320,256]{1,0:T(8,128)(2,1)S(1)}, u32[]{:S(2)}, u32[]{:S(2)}) collective-permute-start(bf16[320,256]{1,0:T(8,128)(2,1)S(1)} %coupling_piece.1), channel_id=1, source_target_pairs={{0,2},{2,4},{4,6},{6,0},{1,3},{3,5},{5,7},{7,1},{8,10},{10,12},{12... | collective-permute-start | bytes 491528 | tf_op jit(solution)/shard_map/ppermute | solution.py:242
  39.3 2.6 %collective-permute-start.5 = (bf16[320,256]{1,0:T(8,128)(2,1)S(1)}, bf16[320,256]{1,0:T(8,128)(2,1)S(1)}, u32[]{:S(2)}, u32[]{:S(2)}) collective-permute-start(bf16[320,256]{1,0:T(8,128)(2,1)S(1)} %coupling_piece.1), channel_id=1, source_target_pairs={{0,4},{2,6},{4,0},{6,2},{1,5},{3,7},{5,1},{7,3},{8,12},{10,14},{12... | collective-permute-start | bytes 491528 | tf_op jit(solution)/shard_map/ppermute | solution.py:242
  41.9 1.3 %collective-permute-start.6 = (bf16[320,256]{1,0:T(8,128)(2,1)S(1)}, bf16[320,256]{1,0:T(8,128)(2,1)S(1)}, u32[]{:S(2)}, u32[]{:S(2)}) collective-permute-start(bf16[320,256]{1,0:T(8,128)(2,1)S(1)} %coupling_piece.1), channel_id=1, source_target_pairs={{0,6},{2,0},{4,2},{6,4},{1,7},{3,1},{5,3},{7,5},{8,14},{10,8},{12,... | collective-permute-start | bytes 491528 | tf_op jit(solution)/shard_map/ppermute | solution.py:242
  43.3 3.3 %collective-permute-done.4 = bf16[320,256]{1,0:T(8,128)(2,1)S(1)} collective-permute-done((bf16[320,256]{1,0:T(8,128)(2,1)S(1)}, bf16[320,256]{1,0:T(8,128)(2,1)S(1)}, u32[]{:S(2)}, u32[]{:S(2)}) %collective-permute-start.4) | collective-permute-done | bytes 163872 | tf_op jit(solution)/shard_map/ppermute | solution.py:242
  46.5 4.4 %collective-permute-done.5 = bf16[320,256]{1,0:T(8,128)(2,1)S(1)} collective-permute-done((bf16[320,256]{1,0:T(8,128)(2,1)S(1)}, bf16[320,256]{1,0:T(8,128)(2,1)S(1)}, u32[]{:S(2)}, u32[]{:S(2)}) %collective-permute-start.5) | collective-permute-done | bytes 163872 | tf_op jit(solution)/shard_map/ppermute | solution.py:242
  50.9 0.0 collective-permute-done.6
  50.9 0.0 collective-permute-done.7.refs_3_
  51.0 1.0 %collective-permute-done.8.refs_2_ = bf16[2688,128]{1,0:T(8,128)(2,1)S(1)} collective-permute-done((bf16[2688,128]{1,0:T(8,128)(2,1)S(1)}, bf16[2688,128]{1,0:T(8,128)(2,1)S(1)}, u32[]{:S(2)}, u32[]{:S(2)}) %collective-permute-start.8) | collective-permute-done | bytes 688160 | tf_op jit(solution)/shard_map/ppermute | solution.py:283
  52.0 0.2 join_pieces.1.refs_1_
  52.2 0.1 collective-permute-start.9
  52.3 0.1 pad_maximum_fusion.4.refs_4_
  52.3 0.8 collective-permute-start.10
  53.1 0.4 collective-permute-start.11
  53.6 4.3 %collective-permute-done.9.refs_2_ = bf16[24,512,128]{2,1,0:T(8,128)(2,1)S(1)} collective-permute-done((bf16[24,512,128]{2,1,0:T(8,128)(2,1)S(1)}, bf16[24,512,128]{2,1,0:T(8,128)(2,1)S(1)}, u32[]{:S(2)}, u32[]{:S(2)}) %collective-permute-start.9) | collective-permute-done | bytes 3145760 | tf_op jit(solution)/shard_map/ppermute | solution.py:242
  57.9 1.0 %assemble_fields.1.refs_1_ = bf16[12,2048,128]{2,1,0:T(8,128)(2,1)S(1)} custom-call(s32[4]{0:T(128)S(1)} %pad_add_fusion.refs_0_, bf16[24,512,128]{2,1,0:T(8,128)(2,1)S(1)} %join_pieces.1.refs_1_, bf16[24,512,128]{2,1,0:T(8,128)(2,1)S(1)} %collective-permute-done.9.refs_2_), custom_call_target="tpu_custom_call" | custom-call | bytes 1024 | tf_op jit(solution)/shard_map/assemble_fields/pallas_call | solution.py:140
  58.9 2.6 %gradient_sums.4.refs_2_ = f32[24,8,128]{2,1,0:T(8,128)S(1)} custom-call(s32[4]{0:T(128)S(1)} %pad_add_fusion.refs_0_, bf16[12,2048,128]{2,1,0:T(8,128)(2,1)S(1)} %assemble_fields.1.refs_1_, f32[24,8,128]{2,1,0:T(8,128)S(1)} %broadcast_in_dim.19.refs_2_, bf16[1,320,256]{2,1,0:T(8,128)(2,1)S(1)} %bitcast.30, bf16[3,320,256]{2,1,0:T(8,128)(2,1)S(1)} %pad_maximum_fusion.4.refs_4_), custom_call_target="tpu_custom_call" | custom-call | bytes 1024 | tf_op jit(solution)/shard_map/gradient_sums/pallas_call | solution.py:221
  61.5 4.5 %collective-permute-done.10.refs_5_ = bf16[3,320,256]{2,1,0:T(8,128)(2,1)S(1)} collective-permute-done((bf16[3,320,256]{2,1,0:T(8,128)(2,1)S(1)}, bf16[3,320,256]{2,1,0:T(8,128)(2,1)S(1)}, u32[]{:S(2)}, u32[]{:S(2)}) %collective-permute-start.10) | collective-permute-done | bytes 491552 | tf_op jit(solution)/shard_map/ppermute | solution.py:289
  66.0 0.5 collective-permute-done.11.refs_5_
  66.5 1.4 %collective-permute-start.13 = (bf16[4,320,128]{2,1,0:T(8,128)(2,1)S(1)}, bf16[4,320,128]{2,1,0:T(8,128)(2,1)S(1)}, u32[]{:S(2)}, u32[]{:S(2)}) collective-permute-start(bf16[4,320,128]{2,1,0:T(8,128)(2,1)S(1)} %pad_maximum_fusion.6), channel_id=1, source_target_pairs={{0,16},{16,0},{1,17},{17,1},{2,18},{18,2},{3,19},{19,3},{4,20},{20... | collective-permute-start | bytes 983048 | tf_op jit(solution)/shard_map/ppermute | solution.py:302
  68.0 0.7 collective-permute-start.12
  68.7 2.6 %gradient_sums.5.refs_2_ = f32[24,8,128]{2,1,0:T(8,128)S(1)} custom-call(s32[4]{0:T(128)S(1)} %pad_add_fusion.refs_0_, bf16[12,2048,128]{2,1,0:T(8,128)(2,1)S(1)} %assemble_fields.1.refs_1_, f32[24,8,128]{2,1,0:T(8,128)S(1)} %gradient_sums.4.refs_2_, bf16[1,320,128]{2,1,0:T(8,128)(2,1)S(1)} %get-tuple-element.55.refs_3_, ...), custom_call_target="tpu_custom_call" | custom-call | bytes 1024 | tf_op jit(solution)/shard_map/gradient_sums/pallas_call | solution.py:221
  71.3 2.6 %gradient_sums.6.refs_2_ = f32[24,8,128]{2,1,0:T(8,128)S(1)} custom-call(s32[4]{0:T(128)S(1)} %pad_add_fusion.refs_0_, bf16[12,2048,128]{2,1,0:T(8,128)(2,1)S(1)} %assemble_fields.1.refs_1_, f32[24,8,128]{2,1,0:T(8,128)S(1)} %gradient_sums.5.refs_2_, bf16[1,320,128]{2,1,0:T(8,128)(2,1)S(1)} %get-tuple-element.45.refs_3_, ...), custom_call_target="tpu_custom_call" | custom-call | bytes 1024 | tf_op jit(solution)/shard_map/gradient_sums/pallas_call | solution.py:221
  73.9 0.0 copy-start.2
  73.9 1.7 %collective-permute-done.13.refs_4_ = bf16[4,320,128]{2,1,0:T(8,128)(2,1)S(1)} collective-permute-done((bf16[4,320,128]{2,1,0:T(8,128)(2,1)S(1)}, bf16[4,320,128]{2,1,0:T(8,128)(2,1)S(1)}, u32[]{:S(2)}, u32[]{:S(2)}) %collective-permute-start.13) | collective-permute-done | bytes 327712 | tf_op jit(solution)/shard_map/ppermute | solution.py:302
  75.6 1.2 %collective-permute-done.12.refs_3_ = bf16[4,320,128]{2,1,0:T(8,128)(2,1)S(1)} collective-permute-done((bf16[4,320,128]{2,1,0:T(8,128)(2,1)S(1)}, bf16[4,320,128]{2,1,0:T(8,128)(2,1)S(1)}, u32[]{:S(2)}, u32[]{:S(2)}) %collective-permute-start.12) | collective-permute-done | bytes 327712 | tf_op jit(solution)/shard_map/ppermute | solution.py:302
  76.8 2.8 %gradient_sums.7 = f32[4,8,128]{2,1,0:T(8,128)S(1)} custom-call(s32[4]{0:T(128)S(1)} %pad_add_fusion.refs_0_, bf16[12,2048,128]{2,1,0:T(8,128)(2,1)S(1)} %assemble_fields.1.refs_1_, f32[24,8,128]{2,1,0:T(8,128)S(1)} %gradient_sums.6.refs_2_, bf16[4,320,128]{2,1,0:T(8,128)(2,1)S(1)} %collective-permute-done.12.refs_3_, ...), custom_call_target="tpu_custom_call" | custom-call | bytes 1024 | tf_op jit(solution)/shard_map/gradient_sums/pallas_call | solution.py:221
  79.6 0.8 collective-permute-start.14
  80.4 0.5 collective-permute-start.15
  80.9 2.3 %collective-permute-start.16 = (f32[2,8,128]{2,1,0:T(8,128)S(1)}, f32[2,8,128]{2,1,0:T(8,128)S(1)}, u32[]{:S(2)}, u32[]{:S(2)}) collective-permute-start(f32[2,8,128]{2,1,0:T(8,128)S(1)} %get-tuple-element.54), channel_id=1, source_target_pairs={{0,17},{1,16},{16,1},{17,0},{2,19},{3,18},{18,3},{19,2},{4,21},{5,... | collective-permute-start | bytes 24584 | tf_op jit(solution)/shard_map/ppermute | solution.py:320
  83.2 0.2 collective-permute-done.14
  83.3 0.7 collective-permute-done.15
  84.1 1.4 %collective-permute-done.16 = f32[2,8,128]{2,1,0:T(8,128)S(1)} collective-permute-done((f32[2,8,128]{2,1,0:T(8,128)S(1)}, f32[2,8,128]{2,1,0:T(8,128)S(1)}, u32[]{:S(2)}, u32[]{:S(2)}) %collective-permute-start.16) | collective-permute-done | bytes 8224 | tf_op jit(solution)/shard_map/ppermute | solution.py:320
  85.5 0.0 collective-permute-start.17
  85.5 1.2 %collective-permute-done.17 = f32[2,8,128]{2,1,0:T(8,128)S(1)} collective-permute-done((f32[2,8,128]{2,1,0:T(8,128)S(1)}, f32[2,8,128]{2,1,0:T(8,128)S(1)}, u32[]{:S(2)}, u32[]{:S(2)}) %collective-permute-start.17) | collective-permute-done | bytes 8224 | tf_op jit(solution)/shard_map/ppermute | solution.py:242
  86.6 0.0 copy-done.2
  86.6 0.6 add_multiply_fusion
  (12 shorter events, 0.2 us)
Async XLA Ops:
  3.9 11.7 %copy-start = (s32[4,32768]{1,0:T(4,128)S(1)}, s32[4,32768]{1,0:T(4,128)}, u32[]{:S(2)}) copy-start(s32[4,32768]{1,0:T(4,128)} %refs_1_.1) | copy-start | bytes 1572868
  3.9 11.7 %copy-start.1 = (f32[32768]{0:T(1024)S(1)}, f32[32768]{0:T(1024)}, u32[]{:S(2)}) copy-start(f32[32768]{0:T(1024)} %param.6) | copy-start | bytes 393220
  3.9 27.2 %collective-permute-start.1 = (bf16[4,512,128]{2,1,0:T(8,128)(2,1)}, bf16[4,512,128]{2,1,0:T(8,128)(2,1)S(1)}, u32[]{:S(2)}, u32[]{:S(2)}) collective-permute-start(bf16[4,512,128]{2,1,0:T(8,128)(2,1)} %get-tuple-element.43), channel_id=1, source_target_pairs={{0,16},{16,0},{1,17},{17,1},{2,18},{18,2},{3,19},{19,3},{4,20},{20... | collective-permute-start | bytes 1572872 | tf_op jit(solution)/shard_map/ppermute | solution.py:272
  6.8 24.2 %collective-permute-start.2 = (bf16[4,512,128]{2,1,0:T(8,128)(2,1)}, bf16[4,512,128]{2,1,0:T(8,128)(2,1)S(1)}, u32[]{:S(2)}, u32[]{:S(2)}) collective-permute-start(bf16[4,512,128]{2,1,0:T(8,128)(2,1)} %get-tuple-element.43), channel_id=1, source_target_pairs={{2,16},{4,18},{6,20},{1,19},{3,21},{5,23},{18,0},{20,2},{22,4},{17... | collective-permute-start | bytes 1572872 | tf_op jit(solution)/shard_map/ppermute | solution.py:273
  8.2 25.2 %collective-permute-start.3 = (bf16[4,512,128]{2,1,0:T(8,128)(2,1)S(1)}, bf16[4,512,128]{2,1,0:T(8,128)(2,1)S(1)}, u32[]{:S(2)}, u32[]{:S(2)}) collective-permute-start(bf16[4,512,128]{2,1,0:T(8,128)(2,1)S(1)} %get-tuple-element.27.refs_0_), channel_id=1, source_target_pairs={{2,0},{4,2},{6,4},{1,3},{3,5},{5,7},{10,8},{12,10},{14,12},{9,11},... | collective-permute-start | bytes 1572872 | tf_op jit(solution)/shard_map/ppermute | solution.py:274
  9.5 23.9 %collective-permute-start = (bf16[4,512,128]{2,1,0:T(8,128)(2,1)}, bf16[4,512,128]{2,1,0:T(8,128)(2,1)}, u32[]{:S(2)}, u32[]{:S(2)}) collective-permute-start(bf16[4,512,128]{2,1,0:T(8,128)(2,1)} %get-tuple-element.44), channel_id=1, source_target_pairs={{0,1},{1,0},{2,3},{3,2},{4,5},{5,4},{6,7},{7,6},{8,9},{9,8},{10,11... | collective-permute-start | bytes 1572872 | tf_op jit(solution)/shard_map/ppermute | solution.py:271
  34.5 16.4 %collective-permute-start.7 = (bf16[2688,128]{1,0:T(8,128)(2,1)S(1)}, bf16[2688,128]{1,0:T(8,128)(2,1)S(1)}, u32[]{:S(2)}, u32[]{:S(2)}) collective-permute-start(bf16[2688,128]{1,0:T(8,128)(2,1)S(1)} %get-tuple-element.50), channel_id=1, source_target_pairs={{0,16},{16,0},{1,17},{17,1},{2,18},{18,2},{3,19},{19,3},{4,20},{20... | collective-permute-start | bytes 2064392 | tf_op jit(solution)/shard_map/ppermute | solution.py:283
  36.2 15.7 %collective-permute-start.8 = (bf16[2688,128]{1,0:T(8,128)(2,1)S(1)}, bf16[2688,128]{1,0:T(8,128)(2,1)S(1)}, u32[]{:S(2)}, u32[]{:S(2)}) collective-permute-start(bf16[2688,128]{1,0:T(8,128)(2,1)S(1)} %get-tuple-element.49), channel_id=1, source_target_pairs={{0,1},{1,0},{2,3},{3,2},{4,5},{5,4},{6,7},{7,6},{8,9},{9,8},{10,11... | collective-permute-start | bytes 2064392 | tf_op jit(solution)/shard_map/ppermute | solution.py:283
  36.8 9.7 %collective-permute-start.4 = (bf16[320,256]{1,0:T(8,128)(2,1)S(1)}, bf16[320,256]{1,0:T(8,128)(2,1)S(1)}, u32[]{:S(2)}, u32[]{:S(2)}) collective-permute-start(bf16[320,256]{1,0:T(8,128)(2,1)S(1)} %coupling_piece.1), channel_id=1, source_target_pairs={{0,2},{2,4},{4,6},{6,0},{1,3},{3,5},{5,7},{7,1},{8,10},{10,12},{12... | collective-permute-start | bytes 491528 | tf_op jit(solution)/shard_map/ppermute | solution.py:242
  39.3 11.6 %collective-permute-start.5 = (bf16[320,256]{1,0:T(8,128)(2,1)S(1)}, bf16[320,256]{1,0:T(8,128)(2,1)S(1)}, u32[]{:S(2)}, u32[]{:S(2)}) collective-permute-start(bf16[320,256]{1,0:T(8,128)(2,1)S(1)} %coupling_piece.1), channel_id=1, source_target_pairs={{0,4},{2,6},{4,0},{6,2},{1,5},{3,7},{5,1},{7,3},{8,12},{10,14},{12... | collective-permute-start | bytes 491528 | tf_op jit(solution)/shard_map/ppermute | solution.py:242
  41.9 9.0 %collective-permute-start.6 = (bf16[320,256]{1,0:T(8,128)(2,1)S(1)}, bf16[320,256]{1,0:T(8,128)(2,1)S(1)}, u32[]{:S(2)}, u32[]{:S(2)}) collective-permute-start(bf16[320,256]{1,0:T(8,128)(2,1)S(1)} %coupling_piece.1), channel_id=1, source_target_pairs={{0,6},{2,0},{4,2},{6,4},{1,7},{3,1},{5,3},{7,5},{8,14},{10,8},{12,... | collective-permute-start | bytes 491528 | tf_op jit(solution)/shard_map/ppermute | solution.py:242
  52.2 5.7 %collective-permute-start.9 = (bf16[24,512,128]{2,1,0:T(8,128)(2,1)S(1)}, bf16[24,512,128]{2,1,0:T(8,128)(2,1)S(1)}, u32[]{:S(2)}, u32[]{:S(2)}) collective-permute-start(bf16[24,512,128]{2,1,0:T(8,128)(2,1)S(1)} %join_pieces.1.refs_1_), channel_id=1, source_target_pairs={{0,8},{8,0},{1,9},{9,1},{2,10},{10,2},{3,11},{11,3},{4,12},{12,4},... | collective-permute-start | bytes 9437192 | tf_op jit(solution)/shard_map/ppermute | solution.py:242
  52.3 13.7 %collective-permute-start.10 = (bf16[3,320,256]{2,1,0:T(8,128)(2,1)S(1)}, bf16[3,320,256]{2,1,0:T(8,128)(2,1)S(1)}, u32[]{:S(2)}, u32[]{:S(2)}) collective-permute-start(bf16[3,320,256]{2,1,0:T(8,128)(2,1)S(1)} %pad_maximum_fusion.4.refs_4_), channel_id=1, source_target_pairs={{0,16},{16,0},{1,17},{17,1},{2,18},{18,2},{3,19},{19,3},{4,20},{20... | collective-permute-start | bytes 1474568 | tf_op jit(solution)/shard_map/ppermute | solution.py:289
  53.1 13.3 %collective-permute-start.11 = (bf16[3,320,256]{2,1,0:T(8,128)(2,1)S(1)}, bf16[3,320,256]{2,1,0:T(8,128)(2,1)S(1)}, u32[]{:S(2)}, u32[]{:S(2)}) collective-permute-start(bf16[3,320,256]{2,1,0:T(8,128)(2,1)S(1)} %pad_maximum_fusion.4.refs_4_), channel_id=1, source_target_pairs={{0,1},{1,0},{2,3},{3,2},{4,5},{5,4},{6,7},{7,6},{8,9},{9,8},{10,11... | collective-permute-start | bytes 1474568 | tf_op jit(solution)/shard_map/ppermute | solution.py:290
  66.5 9.1 %collective-permute-start.13 = (bf16[4,320,128]{2,1,0:T(8,128)(2,1)S(1)}, bf16[4,320,128]{2,1,0:T(8,128)(2,1)S(1)}, u32[]{:S(2)}, u32[]{:S(2)}) collective-permute-start(bf16[4,320,128]{2,1,0:T(8,128)(2,1)S(1)} %pad_maximum_fusion.6), channel_id=1, source_target_pairs={{0,16},{16,0},{1,17},{17,1},{2,18},{18,2},{3,19},{19,3},{4,20},{20... | collective-permute-start | bytes 983048 | tf_op jit(solution)/shard_map/ppermute | solution.py:302
  68.0 8.8 %collective-permute-start.12 = (bf16[4,320,128]{2,1,0:T(8,128)(2,1)S(1)}, bf16[4,320,128]{2,1,0:T(8,128)(2,1)S(1)}, u32[]{:S(2)}, u32[]{:S(2)}) collective-permute-start(bf16[4,320,128]{2,1,0:T(8,128)(2,1)S(1)} %pad_maximum_fusion.5), channel_id=1, source_target_pairs={{0,1},{1,0},{2,3},{3,2},{4,5},{5,4},{6,7},{7,6},{8,9},{9,8},{10,11... | collective-permute-start | bytes 983048 | tf_op jit(solution)/shard_map/ppermute | solution.py:302
  73.9 12.8 %copy-start.2 = (f32[2,8,128]{2,1,0:T(8,128)S(1)}, f32[2,8,128]{2,1,0:T(8,128)}, u32[]{:S(2)}) copy-start(f32[2,8,128]{2,1,0:T(8,128)} %param.7) | copy-start | bytes 24580
  79.6 3.7 %collective-permute-start.14 = (f32[2,8,128]{2,1,0:T(8,128)S(1)}, f32[2,8,128]{2,1,0:T(8,128)S(1)}, u32[]{:S(2)}, u32[]{:S(2)}) collective-permute-start(f32[2,8,128]{2,1,0:T(8,128)S(1)} %get-tuple-element.53), channel_id=1, source_target_pairs={{0,16},{16,0},{1,17},{17,1},{2,18},{18,2},{3,19},{19,3},{4,20},{20... | collective-permute-start | bytes 24584 | tf_op jit(solution)/shard_map/ppermute | solution.py:319
  80.4 3.7 %collective-permute-start.15 = (f32[2,8,128]{2,1,0:T(8,128)S(1)}, f32[2,8,128]{2,1,0:T(8,128)S(1)}, u32[]{:S(2)}, u32[]{:S(2)}) collective-permute-start(f32[2,8,128]{2,1,0:T(8,128)S(1)} %get-tuple-element.54), channel_id=1, source_target_pairs={{0,1},{1,0},{2,3},{3,2},{4,5},{5,4},{6,7},{7,6},{8,9},{9,8},{10,11... | collective-permute-start | bytes 24584 | tf_op jit(solution)/shard_map/ppermute | solution.py:319
  80.9 4.5 %collective-permute-start.16 = (f32[2,8,128]{2,1,0:T(8,128)S(1)}, f32[2,8,128]{2,1,0:T(8,128)S(1)}, u32[]{:S(2)}, u32[]{:S(2)}) collective-permute-start(f32[2,8,128]{2,1,0:T(8,128)S(1)} %get-tuple-element.54), channel_id=1, source_target_pairs={{0,17},{1,16},{16,1},{17,0},{2,19},{3,18},{18,3},{19,2},{4,21},{5,... | collective-permute-start | bytes 24584 | tf_op jit(solution)/shard_map/ppermute | solution.py:320
  85.5 1.2 %collective-permute-start.17 = (f32[2,8,128]{2,1,0:T(8,128)S(1)}, f32[2,8,128]{2,1,0:T(8,128)S(1)}, u32[]{:S(2)}, u32[]{:S(2)}) collective-permute-start(f32[2,8,128]{2,1,0:T(8,128)S(1)} %add_add_fusion), channel_id=1, source_target_pairs={{0,8},{8,0},{1,9},{9,1},{2,10},{10,2},{3,11},{11,3},{4,12},{12,4},... | collective-permute-start | bytes 24584 | tf_op jit(solution)/shard_map/ppermute | solution.py:242

commit v5 on v4

--- a/solution.py
+++ b/solution.py
@@ -6,7 +6,7 @@
 from jax.sharding import Mesh, PartitionSpec as P
 
 BLOCK = 256
-CHUNK = 2048
+CHUNK = 4096
 
 
 def onehots(dest, first, rows, plus, minus, up, down):
@@ -88,7 +88,7 @@
         in_specs=[SMEM, VMEM, VMEM],
         out_specs=VMEM,
         scratch_shapes=hot + hot,
-        compiler_params=pltpu.CompilerParams(vmem_limit_bytes=16 << 20),
+        compiler_params=pltpu.CompilerParams(vmem_limit_bytes=28 << 20),
         cost_estimate=pl.CostEstimate(
             flops=2 * (2 * folded + shared) * BLOCK * quadrupoles.shape[1],
             bytes_accessed=1 << 20,
@@ -100,11 +100,10 @@
 
 def join_kernel(*refs):
     pieces, out = refs[:-1], refs[-1]
-    tiles, count = out.shape[0] // len(pieces), out.shape[1]
+    tiles = pieces[0].shape[0]
     for slot, piece in enumerate(pieces):
         for tile in range(tiles):
-            part = piece[tile] if len(piece.shape) == 3 else piece[count * tile : count * (tile + 1)]
-            out[tiles * slot + tile] = part
+            out[tiles * slot + tile] = piece[tile]
 
 
 def join(pieces):
@@ -120,26 +119,26 @@
     )(*pieces)
 
 
-def assemble_kernel(rows, far, place, *refs):
+def assemble_kernel(rows, tiles, groups, place, *refs):
     pieces, field = refs[:-1], refs[-1]
     electrodes = field.shape[1]
-    members = len(pieces)
-    total, count, _ = pieces[0].shape
-    tiles = total // len(far)
-    for k, piece in enumerate(pieces):
+    members = len(pieces) // len(groups)
+    count = pieces[0].shape[1]
+    for index, piece in enumerate(pieces):
+        k = index % members
         member = (place[1] + members - k) % members
-        for slot, other in enumerate(far):
+        for position, (slot, other) in enumerate(groups[index // members]):
             row = 1 - place[0] if other else place[0]
             first = (row * members + member) * count - place[1] * rows * BLOCK
             first = pl.multiple_of((first + electrodes) % electrodes, count)
             for tile in range(tiles):
-                field[tiles * (slot // 2) + tile, pl.ds(first, count)] = piece[tiles * slot + tile]
-
-
-def assemble(place, pieces, far, rows, electrodes):
+                field[tiles * slot + tile, pl.ds(first, count)] = piece[tiles * position + tile]
+
+
+def assemble(place, pieces, groups, tiles, rows, electrodes):
     return pl.pallas_call(
-        lambda *refs: assemble_kernel(rows, far, *refs),
-        out_shape=jax.ShapeDtypeStruct((pieces[0].shape[0] // 2, electrodes, 128), jnp.bfloat16),
+        lambda *refs: assemble_kernel(rows, tiles, groups, *refs),
+        out_shape=jax.ShapeDtypeStruct((3 * tiles, electrodes, 128), jnp.bfloat16),
         in_specs=[SMEM] + [VMEM] * len(pieces),
         out_specs=VMEM,
         compiler_params=pltpu.CompilerParams(vmem_limit_bytes=16 << 20),
@@ -266,43 +265,42 @@
     tiles = native.shape[0]
     swap = [(0, 1), (1, 0)]
     ahead = [(2 * i, 2 * i - 2) for i in range(1, pairs)] + [(2 * i + 1, 2 * i + 3) for i in range(pairs - 1)]
-    ahead_across = [(2 * pairs * r + a, 2 * pairs * (1 - r) + b) for r in range(2) for a, b in ahead]
     first = [
-        lax.ppermute(other_out, "par", swap),
         lax.ppermute(native_out, "row", swap),
-        lax.ppermute(native_out, ("row", "pair", "par"), ahead_across),
+        lax.ppermute(other_out, ("row", "par"), [(0, 3), (1, 2), (2, 1), (3, 0)]),
+        lax.ppermute(other, "par", swap),
         lax.ppermute(native, ("pair", "par"), ahead),
     ]
     piece = coupling_piece(place, quadrupoles, residuals.reshape(1, -1), shape)
     turns = rotations(piece, "pair")
-    (relay, across, halo_across, halo), other, _ = lax.optimization_barrier((first, other, piece))
-    half = BLOCK // 2
-    cols = folded + shared
-    sides = [piece[:, :half], piece[:, half:]]
-    packed = [jnp.concatenate([a.reshape(-1, 128)] + sides) for a in (relay, other)]
-    crossed = lax.ppermute(packed[0], "row", swap), lax.ppermute(packed[1], "par", swap)
-    moved = native, across, halo, halo_across, turns, crossed
-    native, across, halo, halo_across, _, crossed = lax.optimization_barrier(moved)
-    size = tiles * count
-    own_by_row, own_by_par = ([a[size : size + cols][None], a[size + cols :][None]] for a in crossed)
+    own = piece[None]
+    own_by_row, own_by_par = lax.ppermute(own, "row", swap), lax.ppermute(own, "par", swap)
+    first, _ = lax.optimization_barrier((first, piece))
     column = jnp.stack(turns)
     by_row = lax.ppermute(column, "row", swap)
     by_par = lax.ppermute(column, "par", swap)
-    held = join([native, across, crossed[1], crossed[0], halo, halo_across])
-    field = assemble(place, [held] + rotations(held, "mem"), (0, 1, 0, 1, 0, 1), rows, electrodes)
+
+    moved = first, native, turns, own_by_row, own_by_par
+    first, native, _, own_by_row, own_by_par = lax.optimization_barrier(moved)
+    across, second_across, second, halo = first
+    halo_across = lax.ppermute(across, ("pair", "par"), ahead)
+    held = join([native, across, second, second_across, halo])
+    pieces = [held] + rotations(held, "mem") + [halo_across] + rotations(halo_across, "mem")
+    groups = ((0, 0), (0, 1), (1, 0), (1, 1), (2, 0)), ((2, 1),)
+    field = assemble(place, pieces, groups, tiles, rows, electrodes)
 
     sums = jnp.zeros((6 * tiles, 8, 128), jnp.float32)
-    near = [(piece[None], 0, 0, 0, 0), (column, 0, 0, 0, 1)]
+    half = BLOCK // 2
+    near = [(own, 0, 0, 0, 0), (column, 0, 0, 0, 1)]
     staged = rows == 4
     if staged:
         sums = gradient_sums(place, field, sums, near, shape, window, False)
-        by_row, by_par, sums = lax.optimization_barrier((by_row, by_par, sums))
-    lower = jnp.concatenate([own_by_row[0], by_row[..., :half]])
-    upper = jnp.concatenate([own_by_par[1], by_par[..., half:]])
+    lower = jnp.concatenate([own_by_row[..., :half], by_row[..., :half]])
+    upper = jnp.concatenate([own_by_par[..., half:], by_par[..., half:]])
     corner = lax.ppermute(lower, "par", swap), lax.ppermute(upper, "row", swap)
     beside = [
-        [(own_by_row[0], 1, 0, 0, 0), (own_by_row[1], 1, 0, half, 0), (by_row, 1, 0, 0, 1)],
-        [(own_by_par[0], 0, 1, 0, 0), (own_by_par[1], 0, 1, half, 0), (by_par, 0, 1, 0, 1)],
+        [(own_by_row, 1, 0, 0, 0), (by_row, 1, 0, 0, 1)],
+        [(own_by_par, 0, 1, 0, 0), (by_par, 0, 1, 0, 1)],
     ]
     if staged:
         for part in beside:

time: 87.7 us -> 86.2 us (0.983)
  waiting for transfers between devices: 26.8 us -> 23.9 us
  starting transfers between devices: 27.1 us -> 29.3 us
    ppermute x5 -> x6, waiting for transfers between devices: 13.2 us -> 6.64 us  [rotations(): lax.ppermute(value, axis, [(i, (i + k) % size) for i in range(size)])]
    ppermute x4 -> x5, waiting for transfers between devices: 1.02 us -> 5.36 us  [the longest x1 2.77 us: local(): lax.ppermute(other_out, ('row', 'par'), [(0, 3), (1, 2), (2, 1), (3, 0)])]
    ppermute x1, waiting for transfers between devices: 4.53 us -> 8.78 us  [local(): by_row = lax.ppermute(column, 'row', swap)]
    ppermute x1, starting transfers between devices: 0.41 us -> 3.65 us  [local(): by_par = lax.ppermute(column, 'par', swap)]
    ppermute x1, waiting for transfers between devices: 2.36 us -> 0.01 us  [local(): lax.ppermute(native, ('pair', 'par'), ahead)]
    ppermute x1, starting transfers between devices: 2.94 us -> 1.49 us  [local(): lax.ppermute(native_out, 'row', swap)]
    ppermute x1, waiting for transfers between devices: 1.75 us -> 0.53 us  [local(): lax.ppermute(upper, 'row', swap)]
    ppermute x1, waiting for transfers between devices: 1.16 us -> 0.01 us  [local(): lax.ppermute(lower, 'par', swap)]
  transfers between devices with their start and end apart: 18 -> 20, of which waited for: 13 -> 11; matrix products, arithmetic and copies ran while one was open for 0% -> 2% of each run, Pallas kernels for 28% -> 28%
where the time goes in v5:
time: 86.2 us; the launch traced here: 86 us
  starting transfers between devices  29.3 us (34%)
  Pallas kernels  26.9 us (31%)
  waiting for transfers between devices  23.9 us (28%)
  other arithmetic  3.33 us (4%)
  local copies, waits for them, and re-layouts  2.34 us (3%)
    pallas_call x1, Pallas kernels, coupling_piece(): pl.pallas_call(lambda *refs: coupling_kernel(shape, *refs), out_shape=jax...  15.2 us
    pallas_call x4, Pallas kernels, gradient_sums(): pl.pallas_call(lambda *refs: gradient_kernel(shape, parts, last, *refs),...  10.5 us
    ppermute x1, waiting for transfers between devices, local(): by_row = lax.ppermute(column, 'row', swap)  8.78 us
    ppermute x6, waiting for transfers between devices, rotations(): lax.ppermute(value, axis, [(i, (i + k) % size) for i in range(size)])  6.64 us
    ppermute x6, starting transfers between devices, rotations(): lax.ppermute(value, axis, [(i, (i + k) % size) for i in range(size)])  5.69 us
    ppermute x1, starting transfers between devices, local(): lax.ppermute(other, 'par', swap)  5.25 us
    ppermute x1, starting transfers between devices, local(): by_par = lax.ppermute(column, 'par', swap)  3.65 us
    ppermute x1, waiting for transfers between devices, local(): lax.ppermute(other_out, ('row', 'par'), [(0, 3), (1, 2), (2, 1), (3, 0)])  2.77 us
  transfers between devices with their start and end apart: 20, of which 11 were waited for; matrix products, arithmetic and copies ran while one was open for 2% of the time, Pallas kernels for 28%

profile of v5, /device:TPU:0, one launch (start us, length us, event | category | flops | bytes accessed | tf_op | source)
XLA Modules:
  0.0 86.0 jit_solution(12121912206892382951)
XLA Ops:
  0.0 2.1 %copy.7 = bf16[512,2,8,128]{3,0,2,1:T(8,128)(2,1)S(1)} copy(bf16[512,2,8,128]{3,2,1,0:T(8,128)(2,1)} %param.4) | data formatting | bytes 4194304 | tf_op args[0]
  2.1 0.1 slice.45
  2.2 0.5 broadcast_select_fusion
  2.8 0.0 copy-start
  2.8 0.0 copy-start.1
  2.8 0.9 %select_bitcast_fusion = (bf16[4,512,128]{2,1,0:T(8,128)(2,1)S(1)}, bf16[4,512,128]{2,1,0:T(8,128)(2,1)}) fusion(pred[]{:T(512)S(6)} %eq.4, bf16[2,4,512,128]{3,2,1,0:T(8,128)(2,1)S(1)} %get-tuple-element.33), kind=kLoop, calls=%fused_computation.3 | loop fusion | flops 524288 | bytes 2097153 | tf_op jit(solution)/shard_map/jit(_where)/select_n | solution.py:263
  3.7 1.3 %collective-permute-start.3 = (bf16[4,512,128]{2,1,0:T(8,128)(2,1)S(1)}, bf16[4,512,128]{2,1,0:T(8,128)(2,1)S(1)}, u32[]{:S(2)}, u32[]{:S(2)}) collective-permute-start(bf16[4,512,128]{2,1,0:T(8,128)(2,1)S(1)} %get-tuple-element.23.refs_0_), channel_id=1, source_target_pairs={{2,0},{4,2},{6,4},{1,3},{3,5},{5,7},{10,8},{12,10},{14,12},{9,11},... | collective-permute-start | bytes 1572872 | tf_op jit(solution)/shard_map/ppermute | solution.py:272
  4.9 5.3 %collective-permute-start.2 = (bf16[4,512,128]{2,1,0:T(8,128)(2,1)}, bf16[4,512,128]{2,1,0:T(8,128)(2,1)S(1)}, u32[]{:S(2)}, u32[]{:S(2)}) collective-permute-start(bf16[4,512,128]{2,1,0:T(8,128)(2,1)} %get-tuple-element.36), channel_id=1, source_target_pairs={{0,1},{1,0},{2,3},{3,2},{4,5},{5,4},{6,7},{7,6},{8,9},{9,8},{10,11... | collective-permute-start | bytes 1572872 | tf_op jit(solution)/shard_map/ppermute | solution.py:271
  10.2 1.1 %select_bitcast_fusion.2 = (bf16[4,512,128]{2,1,0:T(8,128)(2,1)}, bf16[4,512,128]{2,1,0:T(8,128)(2,1)}) fusion(pred[]{:T(512)S(6)} %eq.4, bf16[2,4,512,128]{3,2,1,0:T(8,128)(2,1)S(1)} %get-tuple-element.34), kind=kLoop, calls=%fused_computation.5 | loop fusion | flops 524288 | bytes 2097153 | tf_op jit(solution)/shard_map/jit(_where)/select_n | solution.py:264
  11.3 1.5 %collective-permute-start = (bf16[4,512,128]{2,1,0:T(8,128)(2,1)}, bf16[4,512,128]{2,1,0:T(8,128)(2,1)S(1)}, u32[]{:S(2)}, u32[]{:S(2)}) collective-permute-start(bf16[4,512,128]{2,1,0:T(8,128)(2,1)} %get-tuple-element.38), channel_id=1, source_target_pairs={{0,16},{16,0},{1,17},{17,1},{2,18},{18,2},{3,19},{19,3},{4,20},{20... | collective-permute-start | bytes 1572872 | tf_op jit(solution)/shard_map/ppermute | solution.py:269
  12.8 0.0 collective-permute-start.1
  12.8 0.1 pad_add_fusion.refs_0_
  12.9 0.0 copy-done
  12.9 0.0 copy-done.1
  12.9 15.2 %coupling_piece.1 = bf16[320,256]{1,0:T(8,128)(2,1)S(1)} custom-call(s32[4]{0:T(128)S(1)} %pad_add_fusion.refs_0_, s32[4,32768]{1,0:T(4,128)S(1)} %copy-done, f32[1,32768]{1,0:T(1,128)S(1)} %bitcast.23), custom_call_target="tpu_custom_call" | custom-call | flops 8589934592 | bytes 1048576 | tf_op jit(solution)/shard_map/coupling_piece/pallas_call | solution.py:85
  28.1 1.5 %collective-permute-start.7 = (bf16[1,320,256]{2,1,0:T(8,128)(2,1)S(1)}, bf16[1,320,256]{2,1,0:T(8,128)(2,1)S(1)}, u32[]{:S(2)}, u32[]{:S(2)}) collective-permute-start(bf16[1,320,256]{2,1,0:T(8,128)(2,1)S(1)} %bitcast.20), channel_id=1, source_target_pairs={{0,16},{16,0},{1,17},{17,1},{2,18},{18,2},{3,19},{19,3},{4,20},{20... | collective-permute-start | bytes 491528 | tf_op jit(solution)/shard_map/ppermute | solution.py:277
  29.7 0.0 collective-permute-done.3.refs_4_
  29.7 2.0 %collective-permute-start.8 = (bf16[1,320,256]{2,1,0:T(8,128)(2,1)S(1)}, bf16[1,320,256]{2,1,0:T(8,128)(2,1)S(1)}, u32[]{:S(2)}, u32[]{:S(2)}) collective-permute-start(bf16[1,320,256]{2,1,0:T(8,128)(2,1)S(1)} %bitcast.21), channel_id=1, source_target_pairs={{0,1},{1,0},{2,3},{3,2},{4,5},{5,4},{6,7},{7,6},{8,9},{9,8},{10,11... | collective-permute-start | bytes 491528 | tf_op jit(solution)/shard_map/ppermute | solution.py:277
  31.7 0.0 collective-permute-done.2.refs_2_
  31.7 1.6 %collective-permute-start.4 = (bf16[320,256]{1,0:T(8,128)(2,1)S(1)}, bf16[320,256]{1,0:T(8,128)(2,1)S(1)}, u32[]{:S(2)}, u32[]{:S(2)}) collective-permute-start(bf16[320,256]{1,0:T(8,128)(2,1)S(1)} %coupling_piece.1), channel_id=1, source_target_pairs={{0,2},{2,4},{4,6},{6,0},{1,3},{3,5},{5,7},{7,1},{8,10},{10,12},{12... | collective-permute-start | bytes 491528 | tf_op jit(solution)/shard_map/ppermute | solution.py:241
  33.2 0.0 collective-permute-done.refs_1_
  33.2 1.1 %collective-permute-start.5 = (bf16[320,256]{1,0:T(8,128)(2,1)S(1)}, bf16[320,256]{1,0:T(8,128)(2,1)S(1)}, u32[]{:S(2)}, u32[]{:S(2)}) collective-permute-start(bf16[320,256]{1,0:T(8,128)(2,1)S(1)} %coupling_piece.1), channel_id=1, source_target_pairs={{0,4},{2,6},{4,0},{6,2},{1,5},{3,7},{5,1},{7,3},{8,12},{10,14},{12... | collective-permute-start | bytes 491528 | tf_op jit(solution)/shard_map/ppermute | solution.py:241
  34.3 2.8 %collective-permute-done.1.refs_3_ = bf16[4,512,128]{2,1,0:T(8,128)(2,1)S(1)} collective-permute-done((bf16[4,512,128]{2,1,0:T(8,128)(2,1)}, bf16[4,512,128]{2,1,0:T(8,128)(2,1)S(1)}, u32[]{:S(2)}, u32[]{:S(2)}) %collective-permute-start.1) | collective-permute-done | bytes 524320 | tf_op jit(solution)/shard_map/ppermute | solution.py:270
  37.1 3.0 %collective-permute-start.6 = (bf16[320,256]{1,0:T(8,128)(2,1)S(1)}, bf16[320,256]{1,0:T(8,128)(2,1)S(1)}, u32[]{:S(2)}, u32[]{:S(2)}) collective-permute-start(bf16[320,256]{1,0:T(8,128)(2,1)S(1)} %coupling_piece.1), channel_id=1, source_target_pairs={{0,6},{2,0},{4,2},{6,4},{1,7},{3,1},{5,3},{7,5},{8,14},{10,8},{12,... | collective-permute-start | bytes 491528 | tf_op jit(solution)/shard_map/ppermute | solution.py:241
  40.1 0.0 collective-permute-done.7.refs_3_
  40.1 0.0 collective-permute-done.8.refs_3_
  40.1 0.1 collective-permute-done.4
  40.2 4.7 %collective-permute-done.5 = bf16[320,256]{1,0:T(8,128)(2,1)S(1)} collective-permute-done((bf16[320,256]{1,0:T(8,128)(2,1)S(1)}, bf16[320,256]{1,0:T(8,128)(2,1)S(1)}, u32[]{:S(2)}, u32[]{:S(2)}) %collective-permute-start.5) | collective-permute-done | bytes 163872 | tf_op jit(solution)/shard_map/ppermute | solution.py:241
  44.9 0.6 collective-permute-done.6
  45.5 0.2 join_pieces.1.refs_1_
  45.7 0.1 collective-permute-start.9
  45.8 1.5 %collective-permute-start.10 = (bf16[4,512,128]{2,1,0:T(8,128)(2,1)S(1)}, bf16[4,512,128]{2,1,0:T(8,128)(2,1)S(1)}, u32[]{:S(2)}, u32[]{:S(2)}) collective-permute-start(bf16[4,512,128]{2,1,0:T(8,128)(2,1)S(1)} %collective-permute-done.refs_1_), channel_id=1, source_target_pairs={{2,0},{4,2},{6,4},{1,3},{3,5},{5,7},{10,8},{12,10},{14,12},{9,11},... | collective-permute-start | bytes 1572872 | tf_op jit(solution)/shard_map/ppermute | solution.py:286
  47.3 0.1 pad_maximum_fusion.refs_4_
  47.3 1.2 %collective-permute-start.12 = (bf16[3,320,256]{2,1,0:T(8,128)(2,1)S(1)}, bf16[3,320,256]{2,1,0:T(8,128)(2,1)S(1)}, u32[]{:S(2)}, u32[]{:S(2)}) collective-permute-start(bf16[3,320,256]{2,1,0:T(8,128)(2,1)S(1)} %pad_maximum_fusion.refs_4_), channel_id=1, source_target_pairs={{0,16},{16,0},{1,17},{17,1},{2,18},{18,2},{3,19},{19,3},{4,20},{20... | collective-permute-start | bytes 1474568 | tf_op jit(solution)/shard_map/ppermute | solution.py:280
  48.6 3.6 %collective-permute-start.14 = (bf16[3,320,256]{2,1,0:T(8,128)(2,1)S(1)}, bf16[3,320,256]{2,1,0:T(8,128)(2,1)S(1)}, u32[]{:S(2)}, u32[]{:S(2)}) collective-permute-start(bf16[3,320,256]{2,1,0:T(8,128)(2,1)S(1)} %pad_maximum_fusion.refs_4_), channel_id=1, source_target_pairs={{0,1},{1,0},{2,3},{3,2},{4,5},{5,4},{6,7},{7,6},{8,9},{9,8},{10,11... | collective-permute-start | bytes 1474568 | tf_op jit(solution)/shard_map/ppermute | solution.py:281
  52.2 8.8 %collective-permute-done.12.refs_4_ = bf16[3,320,256]{2,1,0:T(8,128)(2,1)S(1)} collective-permute-done((bf16[3,320,256]{2,1,0:T(8,128)(2,1)S(1)}, bf16[3,320,256]{2,1,0:T(8,128)(2,1)S(1)}, u32[]{:S(2)}, u32[]{:S(2)}) %collective-permute-start.12) | collective-permute-done | bytes 491552 | tf_op jit(solution)/shard_map/ppermute | solution.py:280
  61.1 2.6 %collective-permute-done.10.refs_3_ = bf16[4,512,128]{2,1,0:T(8,128)(2,1)S(1)} collective-permute-done((bf16[4,512,128]{2,1,0:T(8,128)(2,1)S(1)}, bf16[4,512,128]{2,1,0:T(8,128)(2,1)S(1)}, u32[]{:S(2)}, u32[]{:S(2)}) %collective-permute-start.10) | collective-permute-done | bytes 524320 | tf_op jit(solution)/shard_map/ppermute | solution.py:286
  63.7 0.0 collective-permute-start.11
  63.7 1.6 %collective-permute-start.13 = (bf16[4,320,128]{2,1,0:T(8,128)(2,1)S(1)}, bf16[4,320,128]{2,1,0:T(8,128)(2,1)S(1)}, u32[]{:S(2)}, u32[]{:S(2)}) collective-permute-start(bf16[4,320,128]{2,1,0:T(8,128)(2,1)S(1)} %pad_maximum_fusion.1), channel_id=1, source_target_pairs={{0,1},{1,0},{2,3},{3,2},{4,5},{5,4},{6,7},{7,6},{8,9},{9,8},{10,11... | collective-permute-start | bytes 983048 | tf_op jit(solution)/shard_map/ppermute | solution.py:300
  65.3 0.0 collective-permute-done.14.refs_4_
  65.3 0.6 collective-permute-start.15
  66.0 0.0 collective-permute-done.11.refs_4_
  66.0 0.0 collective-permute-done.9.refs_2_
  66.0 1.0 %assemble_fields.1.refs_1_ = bf16[12,2048,128]{2,1,0:T(8,128)(2,1)S(1)} custom-call(s32[4]{0:T(128)S(1)} %pad_add_fusion.refs_0_, bf16[20,512,128]{2,1,0:T(8,128)(2,1)S(1)} %join_pieces.1.refs_1_, bf16[20,512,128]{2,1,0:T(8,128)(2,1)S(1)} %collective-permute-done.9.refs_2_, bf16[4,512,128]{2,1,0:T(8,128)(2,1)S(1)} %collective-permute-done.10.refs_3_, ...), custom_call_target="tpu_custom_call" | custom-call | bytes 1024 | tf_op jit(solution)/shard_map/assemble_fields/pallas_call | solution.py:139
  66.9 2.6 %gradient_sums.4.refs_2_ = f32[24,8,128]{2,1,0:T(8,128)S(1)} custom-call(s32[4]{0:T(128)S(1)} %pad_add_fusion.refs_0_, bf16[12,2048,128]{2,1,0:T(8,128)(2,1)S(1)} %assemble_fields.1.refs_1_, f32[24,8,128]{2,1,0:T(8,128)S(1)} %broadcast_in_dim.7.refs_2_, bf16[1,320,256]{2,1,0:T(8,128)(2,1)S(1)} %bitcast.22, bf16[3,320,256]{2,1,0:T(8,128)(2,1)S(1)} %pad_maximum_fusion.refs_4_), custom_call_target="tpu_custom_call" | custom-call | bytes 1024 | tf_op jit(solution)/shard_map/gradient_sums/pallas_call | solution.py:220
  69.5 2.6 %gradient_sums.5.refs_2_ = f32[24,8,128]{2,1,0:T(8,128)S(1)} custom-call(s32[4]{0:T(128)S(1)} %pad_add_fusion.refs_0_, bf16[12,2048,128]{2,1,0:T(8,128)(2,1)S(1)} %assemble_fields.1.refs_1_, f32[24,8,128]{2,1,0:T(8,128)S(1)} %gradient_sums.4.refs_2_, bf16[1,320,256]{2,1,0:T(8,128)(2,1)S(1)} %collective-permute-done.7.refs_3_, ...), custom_call_target="tpu_custom_call" | custom-call | bytes 1024 | tf_op jit(solution)/shard_map/gradient_sums/pallas_call | solution.py:220
  72.1 2.6 %gradient_sums.6.refs_2_ = f32[24,8,128]{2,1,0:T(8,128)S(1)} custom-call(s32[4]{0:T(128)S(1)} %pad_add_fusion.refs_0_, bf16[12,2048,128]{2,1,0:T(8,128)(2,1)S(1)} %assemble_fields.1.refs_1_, f32[24,8,128]{2,1,0:T(8,128)S(1)} %gradient_sums.5.refs_2_, bf16[1,320,256]{2,1,0:T(8,128)(2,1)S(1)} %collective-permute-done.8.refs_3_, ...), custom_call_target="tpu_custom_call" | custom-call | bytes 1024 | tf_op jit(solution)/shard_map/gradient_sums/pallas_call | solution.py:220
  74.7 0.0 copy-start.2
  74.7 0.0 collective-permute-done.13.refs_3_
  74.7 0.5 collective-permute-done.15.refs_4_
  75.2 2.8 %gradient_sums.7 = f32[4,8,128]{2,1,0:T(8,128)S(1)} custom-call(s32[4]{0:T(128)S(1)} %pad_add_fusion.refs_0_, bf16[12,2048,128]{2,1,0:T(8,128)(2,1)S(1)} %assemble_fields.1.refs_1_, f32[24,8,128]{2,1,0:T(8,128)S(1)} %gradient_sums.6.refs_2_, bf16[4,320,128]{2,1,0:T(8,128)(2,1)S(1)} %collective-permute-done.13.refs_3_, ...), custom_call_target="tpu_custom_call" | custom-call | bytes 1024 | tf_op jit(solution)/shard_map/gradient_sums/pallas_call | solution.py:220
  78.1 1.0 %collective-permute-start.16 = (f32[2,8,128]{2,1,0:T(8,128)S(1)}, f32[2,8,128]{2,1,0:T(8,128)S(1)}, u32[]{:S(2)}, u32[]{:S(2)}) collective-permute-start(f32[2,8,128]{2,1,0:T(8,128)S(1)} %get-tuple-element.39), channel_id=1, source_target_pairs={{0,16},{16,0},{1,17},{17,1},{2,18},{18,2},{3,19},{19,3},{4,20},{20... | collective-permute-start | bytes 24584 | tf_op jit(solution)/shard_map/ppermute | solution.py:317
  79.1 0.5 collective-permute-start.17
  79.7 2.0 %collective-permute-start.18 = (f32[2,8,128]{2,1,0:T(8,128)S(1)}, f32[2,8,128]{2,1,0:T(8,128)S(1)}, u32[]{:S(2)}, u32[]{:S(2)}) collective-permute-start(f32[2,8,128]{2,1,0:T(8,128)S(1)} %get-tuple-element.40), channel_id=1, source_target_pairs={{0,17},{1,16},{16,1},{17,0},{2,19},{3,18},{18,3},{19,2},{4,21},{5,... | collective-permute-start | bytes 24584 | tf_op jit(solution)/shard_map/ppermute | solution.py:318
  81.6 0.2 collective-permute-done.16
  81.8 1.0 %collective-permute-done.17 = f32[2,8,128]{2,1,0:T(8,128)S(1)} collective-permute-done((f32[2,8,128]{2,1,0:T(8,128)S(1)}, f32[2,8,128]{2,1,0:T(8,128)S(1)}, u32[]{:S(2)}, u32[]{:S(2)}) %collective-permute-start.17) | collective-permute-done | bytes 8224 | tf_op jit(solution)/shard_map/ppermute | solution.py:317
  82.8 1.4 %collective-permute-done.18 = f32[2,8,128]{2,1,0:T(8,128)S(1)} collective-permute-done((f32[2,8,128]{2,1,0:T(8,128)S(1)}, f32[2,8,128]{2,1,0:T(8,128)S(1)}, u32[]{:S(2)}, u32[]{:S(2)}) %collective-permute-start.18) | collective-permute-done | bytes 8224 | tf_op jit(solution)/shard_map/ppermute | solution.py:318
  84.2 0.0 collective-permute-start.19
  84.2 1.2 %collective-permute-done.19 = f32[2,8,128]{2,1,0:T(8,128)S(1)} collective-permute-done((f32[2,8,128]{2,1,0:T(8,128)S(1)}, f32[2,8,128]{2,1,0:T(8,128)S(1)}, u32[]{:S(2)}, u32[]{:S(2)}) %collective-permute-start.19) | collective-permute-done | bytes 8224 | tf_op jit(solution)/shard_map/ppermute | solution.py:241
  85.4 0.0 copy-done.2
  85.4 0.6 add_multiply_fusion
  (12 shorter events, 0.2 us)
Async XLA Ops:
  2.8 10.1 %copy-start = (s32[4,32768]{1,0:T(4,128)S(1)}, s32[4,32768]{1,0:T(4,128)}, u32[]{:S(2)}) copy-start(s32[4,32768]{1,0:T(4,128)} %refs_1_.1) | copy-start | bytes 1572868
  2.8 10.1 %copy-start.1 = (f32[32768]{0:T(1024)S(1)}, f32[32768]{0:T(1024)}, u32[]{:S(2)}) copy-start(f32[32768]{0:T(1024)} %param.6) | copy-start | bytes 393220
  3.7 26.0 %collective-permute-start.3 = (bf16[4,512,128]{2,1,0:T(8,128)(2,1)S(1)}, bf16[4,512,128]{2,1,0:T(8,128)(2,1)S(1)}, u32[]{:S(2)}, u32[]{:S(2)}) collective-permute-start(bf16[4,512,128]{2,1,0:T(8,128)(2,1)S(1)} %get-tuple-element.23.refs_0_), channel_id=1, source_target_pairs={{2,0},{4,2},{6,4},{1,3},{3,5},{5,7},{10,8},{12,10},{14,12},{9,11},... | collective-permute-start | bytes 1572872 | tf_op jit(solution)/shard_map/ppermute | solution.py:272
  4.9 26.7 %collective-permute-start.2 = (bf16[4,512,128]{2,1,0:T(8,128)(2,1)}, bf16[4,512,128]{2,1,0:T(8,128)(2,1)S(1)}, u32[]{:S(2)}, u32[]{:S(2)}) collective-permute-start(bf16[4,512,128]{2,1,0:T(8,128)(2,1)} %get-tuple-element.36), channel_id=1, source_target_pairs={{0,1},{1,0},{2,3},{3,2},{4,5},{5,4},{6,7},{7,6},{8,9},{9,8},{10,11... | collective-permute-start | bytes 1572872 | tf_op jit(solution)/shard_map/ppermute | solution.py:271
  11.3 21.9 %collective-permute-start = (bf16[4,512,128]{2,1,0:T(8,128)(2,1)}, bf16[4,512,128]{2,1,0:T(8,128)(2,1)S(1)}, u32[]{:S(2)}, u32[]{:S(2)}) collective-permute-start(bf16[4,512,128]{2,1,0:T(8,128)(2,1)} %get-tuple-element.38), channel_id=1, source_target_pairs={{0,16},{16,0},{1,17},{17,1},{2,18},{18,2},{3,19},{19,3},{4,20},{20... | collective-permute-start | bytes 1572872 | tf_op jit(solution)/shard_map/ppermute | solution.py:269
  12.8 24.3 %collective-permute-start.1 = (bf16[4,512,128]{2,1,0:T(8,128)(2,1)}, bf16[4,512,128]{2,1,0:T(8,128)(2,1)S(1)}, u32[]{:S(2)}, u32[]{:S(2)}) collective-permute-start(bf16[4,512,128]{2,1,0:T(8,128)(2,1)} %get-tuple-element.37), channel_id=1, source_target_pairs={{0,17},{1,16},{16,1},{17,0},{2,19},{3,18},{18,3},{19,2},{4,21},{5,... | collective-permute-start | bytes 1572872 | tf_op jit(solution)/shard_map/ppermute | solution.py:270
  28.1 11.9 %collective-permute-start.7 = (bf16[1,320,256]{2,1,0:T(8,128)(2,1)S(1)}, bf16[1,320,256]{2,1,0:T(8,128)(2,1)S(1)}, u32[]{:S(2)}, u32[]{:S(2)}) collective-permute-start(bf16[1,320,256]{2,1,0:T(8,128)(2,1)S(1)} %bitcast.20), channel_id=1, source_target_pairs={{0,16},{16,0},{1,17},{17,1},{2,18},{18,2},{3,19},{19,3},{4,20},{20... | collective-permute-start | bytes 491528 | tf_op jit(solution)/shard_map/ppermute | solution.py:277
  29.7 10.4 %collective-permute-start.8 = (bf16[1,320,256]{2,1,0:T(8,128)(2,1)S(1)}, bf16[1,320,256]{2,1,0:T(8,128)(2,1)S(1)}, u32[]{:S(2)}, u32[]{:S(2)}) collective-permute-start(bf16[1,320,256]{2,1,0:T(8,128)(2,1)S(1)} %bitcast.21), channel_id=1, source_target_pairs={{0,1},{1,0},{2,3},{3,2},{4,5},{5,4},{6,7},{7,6},{8,9},{9,8},{10,11... | collective-permute-start | bytes 491528 | tf_op jit(solution)/shard_map/ppermute | solution.py:277
  31.7 8.5 %collective-permute-start.4 = (bf16[320,256]{1,0:T(8,128)(2,1)S(1)}, bf16[320,256]{1,0:T(8,128)(2,1)S(1)}, u32[]{:S(2)}, u32[]{:S(2)}) collective-permute-start(bf16[320,256]{1,0:T(8,128)(2,1)S(1)} %coupling_piece.1), channel_id=1, source_target_pairs={{0,2},{2,4},{4,6},{6,0},{1,3},{3,5},{5,7},{7,1},{8,10},{10,12},{12... | collective-permute-start | bytes 491528 | tf_op jit(solution)/shard_map/ppermute | solution.py:241
  33.2 11.7 %collective-permute-start.5 = (bf16[320,256]{1,0:T(8,128)(2,1)S(1)}, bf16[320,256]{1,0:T(8,128)(2,1)S(1)}, u32[]{:S(2)}, u32[]{:S(2)}) collective-permute-start(bf16[320,256]{1,0:T(8,128)(2,1)S(1)} %coupling_piece.1), channel_id=1, source_target_pairs={{0,4},{2,6},{4,0},{6,2},{1,5},{3,7},{5,1},{7,3},{8,12},{10,14},{12... | collective-permute-start | bytes 491528 | tf_op jit(solution)/shard_map/ppermute | solution.py:241
  37.1 8.5 %collective-permute-start.6 = (bf16[320,256]{1,0:T(8,128)(2,1)S(1)}, bf16[320,256]{1,0:T(8,128)(2,1)S(1)}, u32[]{:S(2)}, u32[]{:S(2)}) collective-permute-start(bf16[320,256]{1,0:T(8,128)(2,1)S(1)} %coupling_piece.1), channel_id=1, source_target_pairs={{0,6},{2,0},{4,2},{6,4},{1,7},{3,1},{5,3},{7,5},{8,14},{10,8},{12,... | collective-permute-start | bytes 491528 | tf_op jit(solution)/shard_map/ppermute | solution.py:241
  45.7 20.2 %collective-permute-start.9 = (bf16[20,512,128]{2,1,0:T(8,128)(2,1)S(1)}, bf16[20,512,128]{2,1,0:T(8,128)(2,1)S(1)}, u32[]{:S(2)}, u32[]{:S(2)}) collective-permute-start(bf16[20,512,128]{2,1,0:T(8,128)(2,1)S(1)} %join_pieces.1.refs_1_), channel_id=1, source_target_pairs={{0,8},{8,0},{1,9},{9,1},{2,10},{10,2},{3,11},{11,3},{4,12},{12,4},... | collective-permute-start | bytes 7864328 | tf_op jit(solution)/shard_map/ppermute | solution.py:241
  45.8 17.9 %collective-permute-start.10 = (bf16[4,512,128]{2,1,0:T(8,128)(2,1)S(1)}, bf16[4,512,128]{2,1,0:T(8,128)(2,1)S(1)}, u32[]{:S(2)}, u32[]{:S(2)}) collective-permute-start(bf16[4,512,128]{2,1,0:T(8,128)(2,1)S(1)} %collective-permute-done.refs_1_), channel_id=1, source_target_pairs={{2,0},{4,2},{6,4},{1,3},{3,5},{5,7},{10,8},{12,10},{14,12},{9,11},... | collective-permute-start | bytes 1572872 | tf_op jit(solution)/shard_map/ppermute | solution.py:286
  47.3 13.7 %collective-permute-start.12 = (bf16[3,320,256]{2,1,0:T(8,128)(2,1)S(1)}, bf16[3,320,256]{2,1,0:T(8,128)(2,1)S(1)}, u32[]{:S(2)}, u32[]{:S(2)}) collective-permute-start(bf16[3,320,256]{2,1,0:T(8,128)(2,1)S(1)} %pad_maximum_fusion.refs_4_), channel_id=1, source_target_pairs={{0,16},{16,0},{1,17},{17,1},{2,18},{18,2},{3,19},{19,3},{4,20},{20... | collective-permute-start | bytes 1474568 | tf_op jit(solution)/shard_map/ppermute | solution.py:280
  48.6 16.7 %collective-permute-start.14 = (bf16[3,320,256]{2,1,0:T(8,128)(2,1)S(1)}, bf16[3,320,256]{2,1,0:T(8,128)(2,1)S(1)}, u32[]{:S(2)}, u32[]{:S(2)}) collective-permute-start(bf16[3,320,256]{2,1,0:T(8,128)(2,1)S(1)} %pad_maximum_fusion.refs_4_), channel_id=1, source_target_pairs={{0,1},{1,0},{2,3},{3,2},{4,5},{5,4},{6,7},{7,6},{8,9},{9,8},{10,11... | collective-permute-start | bytes 1474568 | tf_op jit(solution)/shard_map/ppermute | solution.py:281
  63.7 2.3 %collective-permute-start.11 = (bf16[4,512,128]{2,1,0:T(8,128)(2,1)S(1)}, bf16[4,512,128]{2,1,0:T(8,128)(2,1)S(1)}, u32[]{:S(2)}, u32[]{:S(2)}) collective-permute-start(bf16[4,512,128]{2,1,0:T(8,128)(2,1)S(1)} %collective-permute-done.10.refs_3_), channel_id=1, source_target_pairs={{0,8},{8,0},{1,9},{9,1},{2,10},{10,2},{3,11},{11,3},{4,12},{12,4},... | collective-permute-start | bytes 1572872 | tf_op jit(solution)/shard_map/ppermute | solution.py:241
  63.7 11.0 %collective-permute-start.13 = (bf16[4,320,128]{2,1,0:T(8,128)(2,1)S(1)}, bf16[4,320,128]{2,1,0:T(8,128)(2,1)S(1)}, u32[]{:S(2)}, u32[]{:S(2)}) collective-permute-start(bf16[4,320,128]{2,1,0:T(8,128)(2,1)S(1)} %pad_maximum_fusion.1), channel_id=1, source_target_pairs={{0,1},{1,0},{2,3},{3,2},{4,5},{5,4},{6,7},{7,6},{8,9},{9,8},{10,11... | collective-permute-start | bytes 983048 | tf_op jit(solution)/shard_map/ppermute | solution.py:300
  65.3 9.9 %collective-permute-start.15 = (bf16[4,320,128]{2,1,0:T(8,128)(2,1)S(1)}, bf16[4,320,128]{2,1,0:T(8,128)(2,1)S(1)}, u32[]{:S(2)}, u32[]{:S(2)}) collective-permute-start(bf16[4,320,128]{2,1,0:T(8,128)(2,1)S(1)} %pad_maximum_fusion.2), channel_id=1, source_target_pairs={{0,16},{16,0},{1,17},{17,1},{2,18},{18,2},{3,19},{19,3},{4,20},{20... | collective-permute-start | bytes 983048 | tf_op jit(solution)/shard_map/ppermute | solution.py:300
  74.7 10.7 %copy-start.2 = (f32[2,8,128]{2,1,0:T(8,128)S(1)}, f32[2,8,128]{2,1,0:T(8,128)}, u32[]{:S(2)}) copy-start(f32[2,8,128]{2,1,0:T(8,128)} %param.7) | copy-start | bytes 24580
  78.1 3.7 %collective-permute-start.16 = (f32[2,8,128]{2,1,0:T(8,128)S(1)}, f32[2,8,128]{2,1,0:T(8,128)S(1)}, u32[]{:S(2)}, u32[]{:S(2)}) collective-permute-start(f32[2,8,128]{2,1,0:T(8,128)S(1)} %get-tuple-element.39), channel_id=1, source_target_pairs={{0,16},{16,0},{1,17},{17,1},{2,18},{18,2},{3,19},{19,3},{4,20},{20... | collective-permute-start | bytes 24584 | tf_op jit(solution)/shard_map/ppermute | solution.py:317
  79.1 3.7 %collective-permute-start.17 = (f32[2,8,128]{2,1,0:T(8,128)S(1)}, f32[2,8,128]{2,1,0:T(8,128)S(1)}, u32[]{:S(2)}, u32[]{:S(2)}) collective-permute-start(f32[2,8,128]{2,1,0:T(8,128)S(1)} %get-tuple-element.40), channel_id=1, source_target_pairs={{0,1},{1,0},{2,3},{3,2},{4,5},{5,4},{6,7},{7,6},{8,9},{9,8},{10,11... | collective-permute-start | bytes 24584 | tf_op jit(solution)/shard_map/ppermute | solution.py:317
  79.7 4.5 %collective-permute-start.18 = (f32[2,8,128]{2,1,0:T(8,128)S(1)}, f32[2,8,128]{2,1,0:T(8,128)S(1)}, u32[]{:S(2)}, u32[]{:S(2)}) collective-permute-start(f32[2,8,128]{2,1,0:T(8,128)S(1)} %get-tuple-element.40), channel_id=1, source_target_pairs={{0,17},{1,16},{16,1},{17,0},{2,19},{3,18},{18,3},{19,2},{4,21},{5,... | collective-permute-start | bytes 24584 | tf_op jit(solution)/shard_map/ppermute | solution.py:318
  84.2 1.2 %collective-permute-start.19 = (f32[2,8,128]{2,1,0:T(8,128)S(1)}, f32[2,8,128]{2,1,0:T(8,128)S(1)}, u32[]{:S(2)}, u32[]{:S(2)}) collective-permute-start(f32[2,8,128]{2,1,0:T(8,128)S(1)} %add_add_fusion), channel_id=1, source_target_pairs={{0,8},{8,0},{1,9},{9,1},{2,10},{10,2},{3,11},{11,3},{4,12},{12,4},... | collective-permute-start | bytes 24584 | tf_op jit(solution)/shard_map/ppermute | solution.py:241

commit v6 on v5

--- a/solution.py
+++ b/solution.py
@@ -273,9 +273,8 @@
     ]
     piece = coupling_piece(place, quadrupoles, residuals.reshape(1, -1), shape)
     turns = rotations(piece, "pair")
-    own = piece[None]
+    first, own = lax.optimization_barrier((first, piece[None]))
     own_by_row, own_by_par = lax.ppermute(own, "row", swap), lax.ppermute(own, "par", swap)
-    first, _ = lax.optimization_barrier((first, piece))
     column = jnp.stack(turns)
     by_row = lax.ppermute(column, "row", swap)
     by_par = lax.ppermute(column, "par", swap)
@@ -284,6 +283,7 @@
     first, native, _, own_by_row, own_by_par = lax.optimization_barrier(moved)
     across, second_across, second, halo = first
     halo_across = lax.ppermute(across, ("pair", "par"), ahead)
+    halo_across, _ = lax.optimization_barrier((halo_across, (by_row, by_par)))
     held = join([native, across, second, second_across, halo])
     pieces = [held] + rotations(held, "mem") + [halo_across] + rotations(halo_across, "mem")
     groups = ((0, 0), (0, 1), (1, 0), (1, 1), (2, 0)), ((2, 1),)

time: 86.2 us -> 85.8 us (level)
  waiting for transfers between devices: 23.9 us -> 20.8 us
  starting transfers between devices: 29.3 us -> 32.1 us
    ppermute x1, waiting for transfers between devices: 0.01 us -> 5.28 us  [local(): by_par = lax.ppermute(column, 'par', swap)]
    ppermute x1, waiting for transfers between devices: 8.78 us -> 5.98 us  [local(): by_row = lax.ppermute(column, 'row', swap)]
    ppermute x1, starting transfers between devices: 3.65 us -> 6.34 us  [local(): by_par = lax.ppermute(column, 'par', swap)]
    ppermute x1, waiting for transfers between devices: 2.59 us -> 0.01 us  [local(): halo_across = lax.ppermute(across, ('pair', 'par'), ahead)]
    ppermute x6, waiting for transfers between devices: 6.64 us -> 4.56 us  [rotations(): lax.ppermute(value, axis, [(i, (i + k) % size) for i in range(size)])]
    ppermute x1, waiting for transfers between devices: 2.77 us -> 1.91 us  [local(): lax.ppermute(other_out, ('row', 'par'), [(0, 3), (1, 2), (2, 1), (3, 0)])]
  transfers between devices with their start and end apart: 20 -> 20, of which waited for: 11 -> 10; matrix products, arithmetic and copies ran while one was open for 2% -> 2% of each run, Pallas kernels for 28% -> 28%
where the time goes in v6:
time: 85.8 us; the launch traced here: 85.6 us
  starting transfers between devices  32.1 us (37%)
  Pallas kernels  26.9 us (31%)
  waiting for transfers between devices  20.8 us (24%)
  other arithmetic  3.33 us (4%)
  local copies, waits for them, and re-layouts  2.34 us (3%)
    pallas_call x1, Pallas kernels, coupling_piece(): pl.pallas_call(lambda *refs: coupling_kernel(shape, *refs), out_shape=jax...  15.2 us
    pallas_call x4, Pallas kernels, gradient_sums(): pl.pallas_call(lambda *refs: gradient_kernel(shape, parts, last, *refs),...  10.5 us
    ppermute x1, starting transfers between devices, local(): by_par = lax.ppermute(column, 'par', swap)  6.34 us
    ppermute x1, waiting for transfers between devices, local(): by_row = lax.ppermute(column, 'row', swap)  5.98 us
    ppermute x6, starting transfers between devices, rotations(): lax.ppermute(value, axis, [(i, (i + k) % size) for i in range(size)])  5.68 us
    ppermute x1, waiting for transfers between devices, local(): by_par = lax.ppermute(column, 'par', swap)  5.28 us
    ppermute x1, starting transfers between devices, local(): lax.ppermute(other, 'par', swap)  5.25 us
    ppermute x6, waiting for transfers between devices, rotations(): lax.ppermute(value, axis, [(i, (i + k) % size) for i in range(size)])  4.56 us
  transfers between devices with their start and end apart: 20, of which 10 were waited for; matrix products, arithmetic and copies ran while one was open for 2% of the time, Pallas kernels for 28%

profile of v6, /device:TPU:0, one launch (start us, length us, event | category | flops | bytes accessed | tf_op | source)
XLA Modules:
  0.0 85.6 jit_solution(16225041289245448788)
XLA Ops:
  0.0 2.1 %copy.7 = bf16[512,2,8,128]{3,0,2,1:T(8,128)(2,1)S(1)} copy(bf16[512,2,8,128]{3,2,1,0:T(8,128)(2,1)} %param.4) | data formatting | bytes 4194304 | tf_op args[0]
  2.1 0.1 slice.45
  2.2 0.5 broadcast_select_fusion
  2.8 0.0 copy-start
  2.8 0.0 copy-start.1
  2.8 0.9 %select_bitcast_fusion = (bf16[4,512,128]{2,1,0:T(8,128)(2,1)S(1)}, bf16[4,512,128]{2,1,0:T(8,128)(2,1)}) fusion(pred[]{:T(512)S(6)} %eq.4, bf16[2,4,512,128]{3,2,1,0:T(8,128)(2,1)S(1)} %get-tuple-element.37), kind=kLoop, calls=%fused_computation.3 | loop fusion | flops 524288 | bytes 2097153 | tf_op jit(solution)/shard_map/jit(_where)/select_n | solution.py:263
  3.7 1.3 %collective-permute-start.3 = (bf16[4,512,128]{2,1,0:T(8,128)(2,1)S(1)}, bf16[4,512,128]{2,1,0:T(8,128)(2,1)S(1)}, u32[]{:S(2)}, u32[]{:S(2)}) collective-permute-start(bf16[4,512,128]{2,1,0:T(8,128)(2,1)S(1)} %get-tuple-element.26.refs_0_), channel_id=1, source_target_pairs={{2,0},{4,2},{6,4},{1,3},{3,5},{5,7},{10,8},{12,10},{14,12},{9,11},... | collective-permute-start | bytes 1572872 | tf_op jit(solution)/shard_map/ppermute | solution.py:272
  4.9 5.3 %collective-permute-start.2 = (bf16[4,512,128]{2,1,0:T(8,128)(2,1)}, bf16[4,512,128]{2,1,0:T(8,128)(2,1)S(1)}, u32[]{:S(2)}, u32[]{:S(2)}) collective-permute-start(bf16[4,512,128]{2,1,0:T(8,128)(2,1)} %get-tuple-element.40), channel_id=1, source_target_pairs={{0,1},{1,0},{2,3},{3,2},{4,5},{5,4},{6,7},{7,6},{8,9},{9,8},{10,11... | collective-permute-start | bytes 1572872 | tf_op jit(solution)/shard_map/ppermute | solution.py:271
  10.2 1.1 %select_bitcast_fusion.2 = (bf16[4,512,128]{2,1,0:T(8,128)(2,1)}, bf16[4,512,128]{2,1,0:T(8,128)(2,1)}) fusion(pred[]{:T(512)S(6)} %eq.4, bf16[2,4,512,128]{3,2,1,0:T(8,128)(2,1)S(1)} %get-tuple-element.38), kind=kLoop, calls=%fused_computation.5 | loop fusion | flops 524288 | bytes 2097153 | tf_op jit(solution)/shard_map/jit(_where)/select_n | solution.py:264
  11.3 1.5 %collective-permute-start = (bf16[4,512,128]{2,1,0:T(8,128)(2,1)}, bf16[4,512,128]{2,1,0:T(8,128)(2,1)S(1)}, u32[]{:S(2)}, u32[]{:S(2)}) collective-permute-start(bf16[4,512,128]{2,1,0:T(8,128)(2,1)} %get-tuple-element.42), channel_id=1, source_target_pairs={{0,16},{16,0},{1,17},{17,1},{2,18},{18,2},{3,19},{19,3},{4,20},{20... | collective-permute-start | bytes 1572872 | tf_op jit(solution)/shard_map/ppermute | solution.py:269
  12.8 0.0 collective-permute-start.1
  12.8 0.1 pad_add_fusion.refs_0_
  12.9 0.0 copy-done
  12.9 0.0 copy-done.1
  12.9 15.2 %coupling_piece.1 = bf16[320,256]{1,0:T(8,128)(2,1)S(1)} custom-call(s32[4]{0:T(128)S(1)} %pad_add_fusion.refs_0_, s32[4,32768]{1,0:T(4,128)S(1)} %copy-done, f32[1,32768]{1,0:T(1,128)S(1)} %bitcast.23), custom_call_target="tpu_custom_call" | custom-call | flops 8589934592 | bytes 1048576 | tf_op jit(solution)/shard_map/coupling_piece/pallas_call | solution.py:85
  28.1 1.6 %collective-permute-start.4 = (bf16[320,256]{1,0:T(8,128)(2,1)S(1)}, bf16[320,256]{1,0:T(8,128)(2,1)S(1)}, u32[]{:S(2)}, u32[]{:S(2)}) collective-permute-start(bf16[320,256]{1,0:T(8,128)(2,1)S(1)} %coupling_piece.1), channel_id=1, source_target_pairs={{0,2},{2,4},{4,6},{6,0},{1,3},{3,5},{5,7},{7,1},{8,10},{10,12},{12... | collective-permute-start | bytes 491528 | tf_op jit(solution)/shard_map/ppermute | solution.py:241
  29.7 0.0 collective-permute-done.3.refs_4_
  29.7 2.0 %collective-permute-start.5 = (bf16[320,256]{1,0:T(8,128)(2,1)S(1)}, bf16[320,256]{1,0:T(8,128)(2,1)S(1)}, u32[]{:S(2)}, u32[]{:S(2)}) collective-permute-start(bf16[320,256]{1,0:T(8,128)(2,1)S(1)} %coupling_piece.1), channel_id=1, source_target_pairs={{0,4},{2,6},{4,0},{6,2},{1,5},{3,7},{5,1},{7,3},{8,12},{10,14},{12... | collective-permute-start | bytes 491528 | tf_op jit(solution)/shard_map/ppermute | solution.py:241
  31.7 0.0 collective-permute-done.2.refs_2_
  31.7 2.0 %collective-permute-start.6 = (bf16[320,256]{1,0:T(8,128)(2,1)S(1)}, bf16[320,256]{1,0:T(8,128)(2,1)S(1)}, u32[]{:S(2)}, u32[]{:S(2)}) collective-permute-start(bf16[320,256]{1,0:T(8,128)(2,1)S(1)} %coupling_piece.1), channel_id=1, source_target_pairs={{0,6},{2,0},{4,2},{6,4},{1,7},{3,1},{5,3},{7,5},{8,14},{10,8},{12,... | collective-permute-start | bytes 491528 | tf_op jit(solution)/shard_map/ppermute | solution.py:241
  33.7 0.0 collective-permute-done.refs_1_
  33.7 1.9 %collective-permute-done.1.refs_3_ = bf16[4,512,128]{2,1,0:T(8,128)(2,1)S(1)} collective-permute-done((bf16[4,512,128]{2,1,0:T(8,128)(2,1)}, bf16[4,512,128]{2,1,0:T(8,128)(2,1)S(1)}, u32[]{:S(2)}, u32[]{:S(2)}) %collective-permute-start.1) | collective-permute-done | bytes 524320 | tf_op jit(solution)/shard_map/ppermute | solution.py:270
  35.6 1.5 %collective-permute-start.7 = (bf16[1,320,256]{2,1,0:T(8,128)(2,1)S(1)}, bf16[1,320,256]{2,1,0:T(8,128)(2,1)S(1)}, u32[]{:S(2)}, u32[]{:S(2)}) collective-permute-start(bf16[1,320,256]{2,1,0:T(8,128)(2,1)S(1)} %bitcast.20), channel_id=1, source_target_pairs={{0,16},{16,0},{1,17},{17,1},{2,18},{18,2},{3,19},{19,3},{4,20},{20... | collective-permute-start | bytes 491528 | tf_op jit(solution)/shard_map/ppermute | solution.py:277
  37.1 1.7 %collective-permute-start.8 = (bf16[1,320,256]{2,1,0:T(8,128)(2,1)S(1)}, bf16[1,320,256]{2,1,0:T(8,128)(2,1)S(1)}, u32[]{:S(2)}, u32[]{:S(2)}) collective-permute-start(bf16[1,320,256]{2,1,0:T(8,128)(2,1)S(1)} %bitcast.21), channel_id=1, source_target_pairs={{0,1},{1,0},{2,3},{3,2},{4,5},{5,4},{6,7},{7,6},{8,9},{9,8},{10,11... | collective-permute-start | bytes 491528 | tf_op jit(solution)/shard_map/ppermute | solution.py:277
  38.8 0.0 collective-permute-done.4
  38.8 3.4 %collective-permute-done.5 = bf16[320,256]{1,0:T(8,128)(2,1)S(1)} collective-permute-done((bf16[320,256]{1,0:T(8,128)(2,1)S(1)}, bf16[320,256]{1,0:T(8,128)(2,1)S(1)}, u32[]{:S(2)}, u32[]{:S(2)}) %collective-permute-start.5) | collective-permute-done | bytes 163872 | tf_op jit(solution)/shard_map/ppermute | solution.py:241
  42.2 0.0 collective-permute-done.6
  42.2 0.0 collective-permute-done.7.refs_3_
  42.2 0.2 collective-permute-done.8.refs_3_
  42.4 0.2 join_pieces.1.refs_1_
  42.6 0.1 collective-permute-start.9
  42.6 1.5 %collective-permute-start.10 = (bf16[4,512,128]{2,1,0:T(8,128)(2,1)S(1)}, bf16[4,512,128]{2,1,0:T(8,128)(2,1)S(1)}, u32[]{:S(2)}, u32[]{:S(2)}) collective-permute-start(bf16[4,512,128]{2,1,0:T(8,128)(2,1)S(1)} %collective-permute-done.refs_1_), channel_id=1, source_target_pairs={{2,0},{4,2},{6,4},{1,3},{3,5},{5,7},{10,8},{12,10},{14,12},{9,11},... | collective-permute-start | bytes 1572872 | tf_op jit(solution)/shard_map/ppermute | solution.py:285
  44.1 0.1 pad_maximum_fusion.refs_4_
  44.2 1.4 %collective-permute-start.11 = (bf16[3,320,256]{2,1,0:T(8,128)(2,1)S(1)}, bf16[3,320,256]{2,1,0:T(8,128)(2,1)S(1)}, u32[]{:S(2)}, u32[]{:S(2)}) collective-permute-start(bf16[3,320,256]{2,1,0:T(8,128)(2,1)S(1)} %pad_maximum_fusion.refs_4_), channel_id=1, source_target_pairs={{0,16},{16,0},{1,17},{17,1},{2,18},{18,2},{3,19},{19,3},{4,20},{20... | collective-permute-start | bytes 1474568 | tf_op jit(solution)/shard_map/ppermute | solution.py:279
  45.5 6.3 %collective-permute-start.12 = (bf16[3,320,256]{2,1,0:T(8,128)(2,1)S(1)}, bf16[3,320,256]{2,1,0:T(8,128)(2,1)S(1)}, u32[]{:S(2)}, u32[]{:S(2)}) collective-permute-start(bf16[3,320,256]{2,1,0:T(8,128)(2,1)S(1)} %pad_maximum_fusion.refs_4_), channel_id=1, source_target_pairs={{0,1},{1,0},{2,3},{3,2},{4,5},{5,4},{6,7},{7,6},{8,9},{9,8},{10,11... | collective-permute-start | bytes 1474568 | tf_op jit(solution)/shard_map/ppermute | solution.py:280
  51.9 6.0 %collective-permute-done.11.refs_4_ = bf16[3,320,256]{2,1,0:T(8,128)(2,1)S(1)} collective-permute-done((bf16[3,320,256]{2,1,0:T(8,128)(2,1)S(1)}, bf16[3,320,256]{2,1,0:T(8,128)(2,1)S(1)}, u32[]{:S(2)}, u32[]{:S(2)}) %collective-permute-start.11) | collective-permute-done | bytes 491552 | tf_op jit(solution)/shard_map/ppermute | solution.py:279
  57.9 5.3 %collective-permute-done.12.refs_4_ = bf16[3,320,256]{2,1,0:T(8,128)(2,1)S(1)} collective-permute-done((bf16[3,320,256]{2,1,0:T(8,128)(2,1)S(1)}, bf16[3,320,256]{2,1,0:T(8,128)(2,1)S(1)}, u32[]{:S(2)}, u32[]{:S(2)}) %collective-permute-start.12) | collective-permute-done | bytes 491552 | tf_op jit(solution)/shard_map/ppermute | solution.py:280
  63.3 0.0 collective-permute-done.10.refs_3_
  63.3 0.1 collective-permute-start.13
  63.4 1.8 %collective-permute-start.14 = (bf16[4,320,128]{2,1,0:T(8,128)(2,1)S(1)}, bf16[4,320,128]{2,1,0:T(8,128)(2,1)S(1)}, u32[]{:S(2)}, u32[]{:S(2)}) collective-permute-start(bf16[4,320,128]{2,1,0:T(8,128)(2,1)S(1)} %pad_maximum_fusion.1), channel_id=1, source_target_pairs={{0,1},{1,0},{2,3},{3,2},{4,5},{5,4},{6,7},{7,6},{8,9},{9,8},{10,11... | collective-permute-start | bytes 983048 | tf_op jit(solution)/shard_map/ppermute | solution.py:300
  65.2 0.6 collective-permute-start.15
  65.8 0.0 collective-permute-done.13.refs_4_
  65.9 0.0 collective-permute-done.9.refs_2_
  65.9 1.0 %assemble_fields.1.refs_1_ = bf16[12,2048,128]{2,1,0:T(8,128)(2,1)S(1)} custom-call(s32[4]{0:T(128)S(1)} %pad_add_fusion.refs_0_, bf16[20,512,128]{2,1,0:T(8,128)(2,1)S(1)} %join_pieces.1.refs_1_, bf16[20,512,128]{2,1,0:T(8,128)(2,1)S(1)} %collective-permute-done.9.refs_2_, bf16[4,512,128]{2,1,0:T(8,128)(2,1)S(1)} %collective-permute-done.10.refs_3_, ...), custom_call_target="tpu_custom_call" | custom-call | bytes 1024 | tf_op jit(solution)/shard_map/assemble_fields/pallas_call | solution.py:139
  66.8 2.6 %gradient_sums.4.refs_2_ = f32[24,8,128]{2,1,0:T(8,128)S(1)} custom-call(s32[4]{0:T(128)S(1)} %pad_add_fusion.refs_0_, bf16[12,2048,128]{2,1,0:T(8,128)(2,1)S(1)} %assemble_fields.1.refs_1_, f32[24,8,128]{2,1,0:T(8,128)S(1)} %broadcast_in_dim.7.refs_2_, bf16[1,320,256]{2,1,0:T(8,128)(2,1)S(1)} %bitcast.22, bf16[3,320,256]{2,1,0:T(8,128)(2,1)S(1)} %pad_maximum_fusion.refs_4_), custom_call_target="tpu_custom_call" | custom-call | bytes 1024 | tf_op jit(solution)/shard_map/gradient_sums/pallas_call | solution.py:220
  69.4 2.6 %gradient_sums.5.refs_2_ = f32[24,8,128]{2,1,0:T(8,128)S(1)} custom-call(s32[4]{0:T(128)S(1)} %pad_add_fusion.refs_0_, bf16[12,2048,128]{2,1,0:T(8,128)(2,1)S(1)} %assemble_fields.1.refs_1_, f32[24,8,128]{2,1,0:T(8,128)S(1)} %gradient_sums.4.refs_2_, bf16[1,320,256]{2,1,0:T(8,128)(2,1)S(1)} %collective-permute-done.7.refs_3_, ...), custom_call_target="tpu_custom_call" | custom-call | bytes 1024 | tf_op jit(solution)/shard_map/gradient_sums/pallas_call | solution.py:220
  72.0 2.6 %gradient_sums.6.refs_2_ = f32[24,8,128]{2,1,0:T(8,128)S(1)} custom-call(s32[4]{0:T(128)S(1)} %pad_add_fusion.refs_0_, bf16[12,2048,128]{2,1,0:T(8,128)(2,1)S(1)} %assemble_fields.1.refs_1_, f32[24,8,128]{2,1,0:T(8,128)S(1)} %gradient_sums.5.refs_2_, bf16[1,320,256]{2,1,0:T(8,128)(2,1)S(1)} %collective-permute-done.8.refs_3_, ...), custom_call_target="tpu_custom_call" | custom-call | bytes 1024 | tf_op jit(solution)/shard_map/gradient_sums/pallas_call | solution.py:220
  74.6 0.0 copy-start.2
  74.6 0.0 collective-permute-done.14.refs_3_
  74.6 0.5 collective-permute-done.15.refs_4_
  75.1 2.8 %gradient_sums.7 = f32[4,8,128]{2,1,0:T(8,128)S(1)} custom-call(s32[4]{0:T(128)S(1)} %pad_add_fusion.refs_0_, bf16[12,2048,128]{2,1,0:T(8,128)(2,1)S(1)} %assemble_fields.1.refs_1_, f32[24,8,128]{2,1,0:T(8,128)S(1)} %gradient_sums.6.refs_2_, bf16[4,320,128]{2,1,0:T(8,128)(2,1)S(1)} %collective-permute-done.14.refs_3_, ...), custom_call_target="tpu_custom_call" | custom-call | bytes 1024 | tf_op jit(solution)/shard_map/gradient_sums/pallas_call | solution.py:220
  78.0 1.1 %collective-permute-start.16 = (f32[2,8,128]{2,1,0:T(8,128)S(1)}, f32[2,8,128]{2,1,0:T(8,128)S(1)}, u32[]{:S(2)}, u32[]{:S(2)}) collective-permute-start(f32[2,8,128]{2,1,0:T(8,128)S(1)} %get-tuple-element.43), channel_id=1, source_target_pairs={{0,16},{16,0},{1,17},{17,1},{2,18},{18,2},{3,19},{19,3},{4,20},{20... | collective-permute-start | bytes 24584 | tf_op jit(solution)/shard_map/ppermute | solution.py:317
  79.0 0.3 collective-permute-start.17
  79.3 2.2 %collective-permute-start.18 = (f32[2,8,128]{2,1,0:T(8,128)S(1)}, f32[2,8,128]{2,1,0:T(8,128)S(1)}, u32[]{:S(2)}, u32[]{:S(2)}) collective-permute-start(f32[2,8,128]{2,1,0:T(8,128)S(1)} %get-tuple-element.44), channel_id=1, source_target_pairs={{0,17},{1,16},{16,1},{17,0},{2,19},{3,18},{18,3},{19,2},{4,21},{5,... | collective-permute-start | bytes 24584 | tf_op jit(solution)/shard_map/ppermute | solution.py:318
  81.5 0.2 collective-permute-done.16
  81.7 1.0 %collective-permute-done.17 = f32[2,8,128]{2,1,0:T(8,128)S(1)} collective-permute-done((f32[2,8,128]{2,1,0:T(8,128)S(1)}, f32[2,8,128]{2,1,0:T(8,128)S(1)}, u32[]{:S(2)}, u32[]{:S(2)}) %collective-permute-start.17) | collective-permute-done | bytes 8224 | tf_op jit(solution)/shard_map/ppermute | solution.py:317
  82.7 1.2 %collective-permute-done.18 = f32[2,8,128]{2,1,0:T(8,128)S(1)} collective-permute-done((f32[2,8,128]{2,1,0:T(8,128)S(1)}, f32[2,8,128]{2,1,0:T(8,128)S(1)}, u32[]{:S(2)}, u32[]{:S(2)}) %collective-permute-start.18) | collective-permute-done | bytes 8224 | tf_op jit(solution)/shard_map/ppermute | solution.py:318
  83.9 0.0 collective-permute-start.19
  83.9 1.2 %collective-permute-done.19 = f32[2,8,128]{2,1,0:T(8,128)S(1)} collective-permute-done((f32[2,8,128]{2,1,0:T(8,128)S(1)}, f32[2,8,128]{2,1,0:T(8,128)S(1)}, u32[]{:S(2)}, u32[]{:S(2)}) %collective-permute-start.19) | collective-permute-done | bytes 8224 | tf_op jit(solution)/shard_map/ppermute | solution.py:241
  85.0 0.0 copy-done.2
  85.0 0.6 add_multiply_fusion
  (12 shorter events, 0.2 us)
Async XLA Ops:
  2.8 10.1 %copy-start = (s32[4,32768]{1,0:T(4,128)S(1)}, s32[4,32768]{1,0:T(4,128)}, u32[]{:S(2)}) copy-start(s32[4,32768]{1,0:T(4,128)} %refs_1_.1) | copy-start | bytes 1572868
  2.8 10.1 %copy-start.1 = (f32[32768]{0:T(1024)S(1)}, f32[32768]{0:T(1024)}, u32[]{:S(2)}) copy-start(f32[32768]{0:T(1024)} %param.6) | copy-start | bytes 393220
  3.7 26.1 %collective-permute-start.3 = (bf16[4,512,128]{2,1,0:T(8,128)(2,1)S(1)}, bf16[4,512,128]{2,1,0:T(8,128)(2,1)S(1)}, u32[]{:S(2)}, u32[]{:S(2)}) collective-permute-start(bf16[4,512,128]{2,1,0:T(8,128)(2,1)S(1)} %get-tuple-element.26.refs_0_), channel_id=1, source_target_pairs={{2,0},{4,2},{6,4},{1,3},{3,5},{5,7},{10,8},{12,10},{14,12},{9,11},... | collective-permute-start | bytes 1572872 | tf_op jit(solution)/shard_map/ppermute | solution.py:272
  4.9 26.8 %collective-permute-start.2 = (bf16[4,512,128]{2,1,0:T(8,128)(2,1)}, bf16[4,512,128]{2,1,0:T(8,128)(2,1)S(1)}, u32[]{:S(2)}, u32[]{:S(2)}) collective-permute-start(bf16[4,512,128]{2,1,0:T(8,128)(2,1)} %get-tuple-element.40), channel_id=1, source_target_pairs={{0,1},{1,0},{2,3},{3,2},{4,5},{5,4},{6,7},{7,6},{8,9},{9,8},{10,11... | collective-permute-start | bytes 1572872 | tf_op jit(solution)/shard_map/ppermute | solution.py:271
  11.3 22.4 %collective-permute-start = (bf16[4,512,128]{2,1,0:T(8,128)(2,1)}, bf16[4,512,128]{2,1,0:T(8,128)(2,1)S(1)}, u32[]{:S(2)}, u32[]{:S(2)}) collective-permute-start(bf16[4,512,128]{2,1,0:T(8,128)(2,1)} %get-tuple-element.42), channel_id=1, source_target_pairs={{0,16},{16,0},{1,17},{17,1},{2,18},{18,2},{3,19},{19,3},{4,20},{20... | collective-permute-start | bytes 1572872 | tf_op jit(solution)/shard_map/ppermute | solution.py:269
  12.8 22.8 %collective-permute-start.1 = (bf16[4,512,128]{2,1,0:T(8,128)(2,1)}, bf16[4,512,128]{2,1,0:T(8,128)(2,1)S(1)}, u32[]{:S(2)}, u32[]{:S(2)}) collective-permute-start(bf16[4,512,128]{2,1,0:T(8,128)(2,1)} %get-tuple-element.41), channel_id=1, source_target_pairs={{0,17},{1,16},{16,1},{17,0},{2,19},{3,18},{18,3},{19,2},{4,21},{5,... | collective-permute-start | bytes 1572872 | tf_op jit(solution)/shard_map/ppermute | solution.py:270
  28.1 10.7 %collective-permute-start.4 = (bf16[320,256]{1,0:T(8,128)(2,1)S(1)}, bf16[320,256]{1,0:T(8,128)(2,1)S(1)}, u32[]{:S(2)}, u32[]{:S(2)}) collective-permute-start(bf16[320,256]{1,0:T(8,128)(2,1)S(1)} %coupling_piece.1), channel_id=1, source_target_pairs={{0,2},{2,4},{4,6},{6,0},{1,3},{3,5},{5,7},{7,1},{8,10},{10,12},{12... | collective-permute-start | bytes 491528 | tf_op jit(solution)/shard_map/ppermute | solution.py:241
  29.7 12.5 %collective-permute-start.5 = (bf16[320,256]{1,0:T(8,128)(2,1)S(1)}, bf16[320,256]{1,0:T(8,128)(2,1)S(1)}, u32[]{:S(2)}, u32[]{:S(2)}) collective-permute-start(bf16[320,256]{1,0:T(8,128)(2,1)S(1)} %coupling_piece.1), channel_id=1, source_target_pairs={{0,4},{2,6},{4,0},{6,2},{1,5},{3,7},{5,1},{7,3},{8,12},{10,14},{12... | collective-permute-start | bytes 491528 | tf_op jit(solution)/shard_map/ppermute | solution.py:241
  31.7 10.5 %collective-permute-start.6 = (bf16[320,256]{1,0:T(8,128)(2,1)S(1)}, bf16[320,256]{1,0:T(8,128)(2,1)S(1)}, u32[]{:S(2)}, u32[]{:S(2)}) collective-permute-start(bf16[320,256]{1,0:T(8,128)(2,1)S(1)} %coupling_piece.1), channel_id=1, source_target_pairs={{0,6},{2,0},{4,2},{6,4},{1,7},{3,1},{5,3},{7,5},{8,14},{10,8},{12,... | collective-permute-start | bytes 491528 | tf_op jit(solution)/shard_map/ppermute | solution.py:241
  35.6 6.6 %collective-permute-start.7 = (bf16[1,320,256]{2,1,0:T(8,128)(2,1)S(1)}, bf16[1,320,256]{2,1,0:T(8,128)(2,1)S(1)}, u32[]{:S(2)}, u32[]{:S(2)}) collective-permute-start(bf16[1,320,256]{2,1,0:T(8,128)(2,1)S(1)} %bitcast.20), channel_id=1, source_target_pairs={{0,16},{16,0},{1,17},{17,1},{2,18},{18,2},{3,19},{19,3},{4,20},{20... | collective-permute-start | bytes 491528 | tf_op jit(solution)/shard_map/ppermute | solution.py:277
  37.1 5.3 %collective-permute-start.8 = (bf16[1,320,256]{2,1,0:T(8,128)(2,1)S(1)}, bf16[1,320,256]{2,1,0:T(8,128)(2,1)S(1)}, u32[]{:S(2)}, u32[]{:S(2)}) collective-permute-start(bf16[1,320,256]{2,1,0:T(8,128)(2,1)S(1)} %bitcast.21), channel_id=1, source_target_pairs={{0,1},{1,0},{2,3},{3,2},{4,5},{5,4},{6,7},{7,6},{8,9},{9,8},{10,11... | collective-permute-start | bytes 491528 | tf_op jit(solution)/shard_map/ppermute | solution.py:277
  42.6 23.3 %collective-permute-start.9 = (bf16[20,512,128]{2,1,0:T(8,128)(2,1)S(1)}, bf16[20,512,128]{2,1,0:T(8,128)(2,1)S(1)}, u32[]{:S(2)}, u32[]{:S(2)}) collective-permute-start(bf16[20,512,128]{2,1,0:T(8,128)(2,1)S(1)} %join_pieces.1.refs_1_), channel_id=1, source_target_pairs={{0,8},{8,0},{1,9},{9,1},{2,10},{10,2},{3,11},{11,3},{4,12},{12,4},... | collective-permute-start | bytes 7864328 | tf_op jit(solution)/shard_map/ppermute | solution.py:241
  42.6 20.6 %collective-permute-start.10 = (bf16[4,512,128]{2,1,0:T(8,128)(2,1)S(1)}, bf16[4,512,128]{2,1,0:T(8,128)(2,1)S(1)}, u32[]{:S(2)}, u32[]{:S(2)}) collective-permute-start(bf16[4,512,128]{2,1,0:T(8,128)(2,1)S(1)} %collective-permute-done.refs_1_), channel_id=1, source_target_pairs={{2,0},{4,2},{6,4},{1,3},{3,5},{5,7},{10,8},{12,10},{14,12},{9,11},... | collective-permute-start | bytes 1572872 | tf_op jit(solution)/shard_map/ppermute | solution.py:285
  44.2 13.7 %collective-permute-start.11 = (bf16[3,320,256]{2,1,0:T(8,128)(2,1)S(1)}, bf16[3,320,256]{2,1,0:T(8,128)(2,1)S(1)}, u32[]{:S(2)}, u32[]{:S(2)}) collective-permute-start(bf16[3,320,256]{2,1,0:T(8,128)(2,1)S(1)} %pad_maximum_fusion.refs_4_), channel_id=1, source_target_pairs={{0,16},{16,0},{1,17},{17,1},{2,18},{18,2},{3,19},{19,3},{4,20},{20... | collective-permute-start | bytes 1474568 | tf_op jit(solution)/shard_map/ppermute | solution.py:279
  45.5 17.7 %collective-permute-start.12 = (bf16[3,320,256]{2,1,0:T(8,128)(2,1)S(1)}, bf16[3,320,256]{2,1,0:T(8,128)(2,1)S(1)}, u32[]{:S(2)}, u32[]{:S(2)}) collective-permute-start(bf16[3,320,256]{2,1,0:T(8,128)(2,1)S(1)} %pad_maximum_fusion.refs_4_), channel_id=1, source_target_pairs={{0,1},{1,0},{2,3},{3,2},{4,5},{5,4},{6,7},{7,6},{8,9},{9,8},{10,11... | collective-permute-start | bytes 1474568 | tf_op jit(solution)/shard_map/ppermute | solution.py:280
  63.3 2.6 %collective-permute-start.13 = (bf16[4,512,128]{2,1,0:T(8,128)(2,1)S(1)}, bf16[4,512,128]{2,1,0:T(8,128)(2,1)S(1)}, u32[]{:S(2)}, u32[]{:S(2)}) collective-permute-start(bf16[4,512,128]{2,1,0:T(8,128)(2,1)S(1)} %collective-permute-done.10.refs_3_), channel_id=1, source_target_pairs={{0,8},{8,0},{1,9},{9,1},{2,10},{10,2},{3,11},{11,3},{4,12},{12,4},... | collective-permute-start | bytes 1572872 | tf_op jit(solution)/shard_map/ppermute | solution.py:241
  63.4 11.2 %collective-permute-start.14 = (bf16[4,320,128]{2,1,0:T(8,128)(2,1)S(1)}, bf16[4,320,128]{2,1,0:T(8,128)(2,1)S(1)}, u32[]{:S(2)}, u32[]{:S(2)}) collective-permute-start(bf16[4,320,128]{2,1,0:T(8,128)(2,1)S(1)} %pad_maximum_fusion.1), channel_id=1, source_target_pairs={{0,1},{1,0},{2,3},{3,2},{4,5},{5,4},{6,7},{7,6},{8,9},{9,8},{10,11... | collective-permute-start | bytes 983048 | tf_op jit(solution)/shard_map/ppermute | solution.py:300
  65.2 9.9 %collective-permute-start.15 = (bf16[4,320,128]{2,1,0:T(8,128)(2,1)S(1)}, bf16[4,320,128]{2,1,0:T(8,128)(2,1)S(1)}, u32[]{:S(2)}, u32[]{:S(2)}) collective-permute-start(bf16[4,320,128]{2,1,0:T(8,128)(2,1)S(1)} %pad_maximum_fusion.2), channel_id=1, source_target_pairs={{0,16},{16,0},{1,17},{17,1},{2,18},{18,2},{3,19},{19,3},{4,20},{20... | collective-permute-start | bytes 983048 | tf_op jit(solution)/shard_map/ppermute | solution.py:300
  74.6 10.4 %copy-start.2 = (f32[2,8,128]{2,1,0:T(8,128)S(1)}, f32[2,8,128]{2,1,0:T(8,128)}, u32[]{:S(2)}) copy-start(f32[2,8,128]{2,1,0:T(8,128)} %param.7) | copy-start | bytes 24580
  78.0 3.7 %collective-permute-start.16 = (f32[2,8,128]{2,1,0:T(8,128)S(1)}, f32[2,8,128]{2,1,0:T(8,128)S(1)}, u32[]{:S(2)}, u32[]{:S(2)}) collective-permute-start(f32[2,8,128]{2,1,0:T(8,128)S(1)} %get-tuple-element.43), channel_id=1, source_target_pairs={{0,16},{16,0},{1,17},{17,1},{2,18},{18,2},{3,19},{19,3},{4,20},{20... | collective-permute-start | bytes 24584 | tf_op jit(solution)/shard_map/ppermute | solution.py:317
  79.0 3.7 %collective-permute-start.17 = (f32[2,8,128]{2,1,0:T(8,128)S(1)}, f32[2,8,128]{2,1,0:T(8,128)S(1)}, u32[]{:S(2)}, u32[]{:S(2)}) collective-permute-start(f32[2,8,128]{2,1,0:T(8,128)S(1)} %get-tuple-element.44), channel_id=1, source_target_pairs={{0,1},{1,0},{2,3},{3,2},{4,5},{5,4},{6,7},{7,6},{8,9},{9,8},{10,11... | collective-permute-start | bytes 24584 | tf_op jit(solution)/shard_map/ppermute | solution.py:317
  79.3 4.5 %collective-permute-start.18 = (f32[2,8,128]{2,1,0:T(8,128)S(1)}, f32[2,8,128]{2,1,0:T(8,128)S(1)}, u32[]{:S(2)}, u32[]{:S(2)}) collective-permute-start(f32[2,8,128]{2,1,0:T(8,128)S(1)} %get-tuple-element.44), channel_id=1, source_target_pairs={{0,17},{1,16},{16,1},{17,0},{2,19},{3,18},{18,3},{19,2},{4,21},{5,... | collective-permute-start | bytes 24584 | tf_op jit(solution)/shard_map/ppermute | solution.py:318
  83.9 1.2 %collective-permute-start.19 = (f32[2,8,128]{2,1,0:T(8,128)S(1)}, f32[2,8,128]{2,1,0:T(8,128)S(1)}, u32[]{:S(2)}, u32[]{:S(2)}) collective-permute-start(f32[2,8,128]{2,1,0:T(8,128)S(1)} %add_add_fusion), channel_id=1, source_target_pairs={{0,8},{8,0},{1,9},{9,1},{2,10},{10,2},{3,11},{11,3},{4,12},{12,4},... | collective-permute-start | bytes 24584 | tf_op jit(solution)/shard_map/ppermute | solution.py:241
